TPU v7x, 32 devices: a whole 2x2x4 slice. The times are simulated.
32 devices in a mesh: groups: 2 (over y), clus: 4 (over z), sub: 2 (over x), rep: 2 (over core).
Axes of the slice: x: 2, y: 2, z: 4, core: 2. Of those that a mesh axis runs over, the one named last changes fastest.
Arguments:
- embeds: bfloat16 [16384, 768], P(('groups', 'clus', 'sub', 'rep')), parts along dimension 0
- cluster_of: int32 [16384], P(('groups', 'clus', 'sub', 'rep')), parts along dimension 0, may hold values from 0 to 7, as said below
- order_in: int32 [16384], P(('groups', 'clus', 'sub', 'rep')), parts along dimension 0, may hold values from 0 to 1023, as said below
- partner: int32 [16], P(('groups', 'clus', 'sub')), parts along dimension 0, may hold values from 0 to 7, as said below
- border_idx: int32 [16, 256], P(('groups', 'clus', 'sub')), parts along dimension 0, may hold values from 0 to 1023, as said below
Outputs:
- log_weight: float32 [16384], P(('groups', 'clus', 'sub', 'rep')), parts along dimension 0
There are 2 independent parts, one for each index of `groups`. A program takes and returns all parts, laid end to end along the dimension named above; each array names one. Nothing has to cross between parts.
Inputs may be any that keep to these rules, and one draw needn't show every extreme that they name: `cluster_of`: row blocks of 512 rows, in order, belong to the devices in the order of clus, sub, rep (rep fastest). Every cluster number is named by exactly 1024 rows. The owner of cluster c is c. Of the rows of one block, at most 128 name clusters of one owner, and in every draw some block has exactly 128 rows for some owner. `order_in`: the 1024 rows of one cluster have distinct positions; rows with a position below 512 lie in blocks of rep index 0, the others in blocks of rep index 1. partner[c] // 1 equals (c + 4) modulo 4 * 2. `border_idx`: the 256 positions of one cluster are distinct.
All inputs are finite; a program needn't handle non-finite values.
Results may differ from a plain program's by a relative error of at most 0.0003.
Values may be sent and summed in bfloat16 or wider, within the bound.
No kernel may reach another device: no remote copies, remote signals or barrier semaphores. Data moves between devices by JAX's collectives and lax.ppermute only.
A program may use at most 64 MiB of HBM per device.

v0:
```python
import jax
import jax.numpy as jnp
from jax import lax
from jax.sharding import PartitionSpec as P

CAP = 1024
BORDER = 256


smoothing_scale = 0.1


def passed_along(shard, axis, by):
    count = lax.axis_size(axis)
    return lax.ppermute(shard, axis, [(i, (i + by) % count) for i in range(count)])


def pick_rows(whole, positions):
    return jax.vmap(lambda block, where: jnp.take(block, where, axis=0))(whole, positions)


def per_device(embeds, cluster_of, order_in, partner, border_idx):
    rows_here = embeds.shape[0]
    width = embeds.shape[1]
    clus_count = lax.axis_size("clus")
    sub_count = lax.axis_size("sub")
    owners = clus_count * sub_count
    send = 2 * rows_here // owners
    clusters_here = partner.shape[0]
    half = CAP // 2
    side = lax.axis_index("rep")
    values = embeds.astype(jnp.float32)
    unit = (values * lax.rsqrt(jnp.mean(values * values, axis=1, keepdims=True) + 1e-06)).astype(
        jnp.bfloat16
    )
    owner = cluster_of // clusters_here
    target_rows = cluster_of % clusters_here * half + order_in % half
    indicator_matrix = (owner[:, None] == jnp.arange(owners, dtype=jnp.int32)[None, :]).astype(
        jnp.int32
    )
    rank = jnp.sum(jnp.cumsum(indicator_matrix, axis=0) * indicator_matrix, axis=1) - 1
    place = owner * send + rank
    outgoing = jnp.zeros((owners * send, width), jnp.bfloat16).at[place].set(unit)
    labels = jnp.full((owners * send,), clusters_here * half, jnp.int32).at[place].set(target_rows)
    incoming, tags = (
        lax.all_to_all(
            outgoing.reshape(owners, send, width),
            ("clus", "sub"),
            split_axis=0,
            concat_axis=0,
            tiled=True,
        ),
        lax.all_to_all(
            labels.reshape(owners, send), ("clus", "sub"), split_axis=0, concat_axis=0, tiled=True
        ),
    )
    tags = tags.reshape(-1)
    incoming = incoming.reshape(-1, width)
    mine = (
        jnp.zeros((clusters_here * half, width), jnp.bfloat16).at[tags].set(incoming, mode="drop")
    )
    mine = mine.reshape(clusters_here, half, width)
    whole = lax.all_gather(mine, "rep", axis=1, tiled=True)
    chosen = pick_rows(whole, border_idx)
    arrived = passed_along(chosen, "clus", clus_count // 2)
    tile = jnp.take(arrived, partner % clusters_here, axis=0)
    adjacent_partition = (
        jnp.einsum("khd,kcd->khc", mine, whole, preferred_element_type=jnp.float32) / width
    )
    importance_function = jnp.exp((adjacent_partition - 1.0) / smoothing_scale)
    matrix_entries_across = jnp.arange(CAP, dtype=jnp.int32)[None, :]
    selfcol = side * half + jnp.arange(half, dtype=jnp.int32)[:, None]
    importance_function = jnp.where(
        (matrix_entries_across == selfcol)[None, :, :], jnp.float32(0.0), importance_function
    )
    remote_partition = (
        jnp.einsum("khd,kbd->khb", mine, tile, preferred_element_type=jnp.float32) / width
    )
    summed_importance = jnp.sum(importance_function, axis=2) + jnp.sum(
        jnp.exp((remote_partition - 1.0) / smoothing_scale), axis=2
    )
    scores = (-jnp.log(summed_importance / (CAP - 1 + BORDER))).reshape(-1)
    padded = jnp.concatenate([scores, jnp.zeros((1,), jnp.float32)])
    answers = padded[tags].reshape(owners, send)
    returned = lax.all_to_all(answers, ("clus", "sub"), split_axis=0, concat_axis=0, tiled=True)
    return returned.reshape(-1)[place]


def solution(mesh):
    return jax.shard_map(
        per_device,
        mesh=mesh,
        in_specs=(
            P(("groups", "clus", "sub", "rep"), None),
            P(("groups", "clus", "sub", "rep")),
            P(("groups", "clus", "sub", "rep")),
            P(("groups", "clus", "sub")),
            P(("groups", "clus", "sub"), None),
        ),
        out_specs=P(("groups", "clus", "sub", "rep")),
        check_vma=False,
    )
```

profile of v0, /device:TPU:0, one launch (start us, length us, event | category | flops | bytes accessed | tf_op | source)
XLA Modules:
  0.0 139.4 jit_solution(5524516069133562151)
XLA Ops:
  6.5 0.7 fusion.14
  7.2 1.1 reduce-window.6
  8.4 0.2 slice_reduce_fusion
  8.6 0.8 fusion.13
  9.4 0.7 compare_select_fusion.3
  10.1 3.0 %scatter_custom_fusion = s32[1024]{0:T(1024)} fusion(s32[512]{0:T(512)S(1)} %get-tuple-element.7, s32[512]{0:T(512)S(1)} %get-tuple-element.8, s32[]{:T(128)} %constant.113.clone.1), kind=kCustom, calls=%fused_computation.45 | custom fusion | bytes 4100 | tf_op jit(solution)/shard_map/scatter | solution.py:44
  13.1 7.3 %all-to-all-start = ((s32[8,1,128]{2,1,0:T(1,128)}), s32[8,1,128]{2,1,0:T(1,128)S(1)}, u32[]{:S(2)}, u32[]{:S(2)}) async-start(s32[8,1,128]{2,1,0:T(1,128)} %bitcast.3), calls=%async_computation | async-start | bytes 8192 | tf_op jit(solution)/shard_map/all_to_all | solution.py:53
  20.3 1.4 fusion
  21.7 4.5 %scatter_custom_fusion.1 = bf16[1024,768]{1,0:T(8,128)(2,1)} fusion(s32[512]{0:T(512)S(1)} %get-tuple-element.7, bf16[512,768]{1,0:T(8,128)(2,1)} %param.5, f32[512]{0:T(512)S(1)} %add_rsqrt_fusion, bf16[]{:T(256)} %constant.115.clone.1), kind=kCustom, calls=%fused_computation.17 | custom fusion | flops 1179648 | bytes 2361346 | tf_op jit(solution)/shard_map/scatter | solution.py:43
  26.2 0.6 all-to-all-done
  26.8 5.4 %all-to-all-start.1 = ((bf16[8,128,768]{2,1,0:T(8,128)(2,1)}), bf16[8,128,768]{2,1,0:T(8,128)(2,1)S(1)}, u32[]{:S(2)}, u32[]{:S(2)}) async-start(bf16[8,128,768]{2,1,0:T(8,128)(2,1)} %bitcast.6), calls=%async_computation.1 | async-start | bytes 3145728 | tf_op jit(solution)/shard_map/all_to_all | solution.py:46
  32.2 0.0 copy-start.2
  32.2 0.0 all-gather.3.cloned.1.call-start
  32.3 36.4 %all-to-all-done.1 = bf16[8,128,768]{2,1,0:T(8,128)(2,1)S(1)} async-done(((bf16[8,128,768]{2,1,0:T(8,128)(2,1)}), bf16[8,128,768]{2,1,0:T(8,128)(2,1)S(1)}, u32[]{:S(2)}, u32[]{:S(2)}) %all-to-all-start.1) | async-done | bytes 1572896 | tf_op jit(solution)/shard_map/all_to_all | solution.py:46
  68.7 6.0 %scatter_custom_fusion.2 = bf16[512,768]{1,0:T(8,128)(2,1)} fusion(s32[1024]{0:T(1024)S(1)} %bitcast.37, bf16[1024,768]{1,0:T(8,128)(2,1)S(1)} %bitcast.34, bf16[]{:T(256)} %constant.115.clone.1), kind=kCustom, calls=%fused_computation.22 | custom fusion | bytes 786434 | tf_op jit(solution)/shard_map/scatter | solution.py:60
  74.7 0.0 all-gather.3.cloned.1.call-update
  74.7 0.0 copy-done.2
  74.8 9.0 %all-gather.3.cloned.1.call-done = bf16[1024,768]{1,0:T(8,128)(2,1)} async-done(((bf16[512,768]{1,0:T(8,128)(2,1)}), bf16[1024,768]{1,0:T(8,128)(2,1)}) %all-gather.3.cloned.1.call-update) | async-done | bytes 1572880 | tf_op jit(solution)/shard_map/all_gather | solution.py:63
  83.7 0.0 copy-start
  83.7 0.0 copy-start.1
  83.7 3.1 %gather_fusion.2 = bf16[256,768]{1,0:T(8,128)(2,1)S(1)} fusion(bf16[1,1024,768]{2,1,0:T(8,128)(2,1)} %bitcast.33, s32[256]{0:T(256)S(1)} %bitcast.32), kind=kCustom, calls=%fused_computation.2 | custom fusion | bytes 788480 | tf_op jit(solution)/shard_map/vmap(jit(_take))/gather | solution.py:19
  86.8 0.1 bitcast_select_fusion
  86.9 2.7 %collective-permute-start = (bf16[1,256,768]{2,1,0:T(8,128)(2,1)S(1)}, bf16[1,256,768]{2,1,0:T(8,128)(2,1)S(1)}, u32[]{:S(2)}, u32[]{:S(2)}) collective-permute-start(bf16[1,256,768]{2,1,0:T(8,128)(2,1)S(1)} %bitcast_select_fusion), channel_id=1, source_target_pairs={{0,8},{4,12},{8,0},{12,4},{1,9},{5,13},{9,1},{13,5},{2,10},{6,14},... | collective-permute-start | bytes 1179656 | tf_op jit(solution)/shard_map/ppermute | solution.py:15
  89.6 0.0 copy-done
  89.7 0.0 copy-done.1
  89.7 1.3 select_reduce_fusion
  91.0 16.7 %collective-permute-done = bf16[1,256,768]{2,1,0:T(8,128)(2,1)S(1)} collective-permute-done((bf16[1,256,768]{2,1,0:T(8,128)(2,1)S(1)}, bf16[1,256,768]{2,1,0:T(8,128)(2,1)S(1)}, u32[]{:S(2)}, u32[]{:S(2)}) %collective-permute-start) | collective-permute-done | bytes 393248 | tf_op jit(solution)/shard_map/ppermute | solution.py:15
  107.7 0.5 fusion.5
  108.1 8.8 %gather_fusion = f32[1024]{0:T(1024)} fusion(f32[513]{0:T(1024)S(1)} %pad_maximum_fusion, s32[1024]{0:T(1024)S(1)} %broadcast_clamp_fusion), kind=kCustom, calls=%fused_computation | custom fusion | bytes 12288 | tf_op jit(solution)/shard_map/gather | solution.py:84
  117.0 5.7 %all-to-all-start.2 = ((f32[8,1,128]{2,1,0:T(1,128)}), f32[8,1,128]{2,1,0:T(1,128)S(1)}, u32[]{:S(2)}, u32[]{:S(2)}) async-start(f32[8,1,128]{2,1,0:T(1,128)} %bitcast.15), calls=%async_computation.2 | async-start | bytes 8192 | tf_op jit(solution)/shard_map/all_to_all | solution.py:85
  122.7 6.5 %all-to-all-done.2 = f32[8,1,128]{2,1,0:T(1,128)S(1)} async-done(((f32[8,1,128]{2,1,0:T(1,128)}), f32[8,1,128]{2,1,0:T(1,128)S(1)}, u32[]{:S(2)}, u32[]{:S(2)}) %all-to-all-start.2) | async-done | bytes 4128 | tf_op jit(solution)/shard_map/all_to_all | solution.py:85
  129.2 3.4 %gather_fusion.1 = f32[512]{0:T(512)} fusion(f32[1024]{0:T(1024)S(1)} %bitcast.31, s32[1024]{0:T(1024)S(1)} %pad_clamp_fusion), kind=kCustom, calls=%fused_computation.1 | custom fusion | bytes 6144 | tf_op jit(solution)/shard_map/gather | solution.py:86
  (13 shorter events, 0.1 us)
Async XLA Ops:
  13.1 13.7 %all-to-all-start = ((s32[8,1,128]{2,1,0:T(1,128)}), s32[8,1,128]{2,1,0:T(1,128)S(1)}, u32[]{:S(2)}, u32[]{:S(2)}) async-start(s32[8,1,128]{2,1,0:T(1,128)} %bitcast.3), calls=%async_computation | async-start | bytes 8192 | tf_op jit(solution)/shard_map/all_to_all | solution.py:53
  26.8 41.9 %all-to-all-start.1 = ((bf16[8,128,768]{2,1,0:T(8,128)(2,1)}), bf16[8,128,768]{2,1,0:T(8,128)(2,1)S(1)}, u32[]{:S(2)}, u32[]{:S(2)}) async-start(bf16[8,128,768]{2,1,0:T(8,128)(2,1)} %bitcast.6), calls=%async_computation.1 | async-start | bytes 3145728 | tf_op jit(solution)/shard_map/all_to_all | solution.py:46
  32.2 42.5 %copy-start.2 = (s32[1,256]{1,0:T(1,128)S(1)}, s32[1,256]{1,0:T(1,128)}, u32[]{:S(2)}) copy-start(s32[1,256]{1,0:T(1,128)} %param.8) | copy-start | bytes 3076
  32.2 51.5 %all-gather.3.cloned.1.call-start = ((), (), s32[]{:S(2)}) async-start(), calls=%async_computation.3 | async-start | bytes 2359296 | tf_op jit(solution)/shard_map/all_gather | solution.py:63
  83.7 5.9 %copy-start = (bf16[1024,768]{1,0:T(8,128)(2,1)S(1)}, bf16[1024,768]{1,0:T(8,128)(2,1)}, u32[]{:S(2)}) copy-start(bf16[1024,768]{1,0:T(8,128)(2,1)} %all-gather.3.cloned.1.call-done) | copy-start | bytes 4718596
  83.7 5.9 %copy-start.1 = (bf16[512,768]{1,0:T(8,128)(2,1)S(1)}, bf16[512,768]{1,0:T(8,128)(2,1)}, u32[]{:S(2)}) copy-start(bf16[512,768]{1,0:T(8,128)(2,1)} %scatter_custom_fusion.2) | copy-start | bytes 2359300
  86.9 20.7 %collective-permute-start = (bf16[1,256,768]{2,1,0:T(8,128)(2,1)S(1)}, bf16[1,256,768]{2,1,0:T(8,128)(2,1)S(1)}, u32[]{:S(2)}, u32[]{:S(2)}) collective-permute-start(bf16[1,256,768]{2,1,0:T(8,128)(2,1)S(1)} %bitcast_select_fusion), channel_id=1, source_target_pairs={{0,8},{4,12},{8,0},{12,4},{1,9},{5,13},{9,1},{13,5},{2,10},{6,14},... | collective-permute-start | bytes 1179656 | tf_op jit(solution)/shard_map/ppermute | solution.py:15
  117.0 12.2 %all-to-all-start.2 = ((f32[8,1,128]{2,1,0:T(1,128)}), f32[8,1,128]{2,1,0:T(1,128)S(1)}, u32[]{:S(2)}, u32[]{:S(2)}) async-start(f32[8,1,128]{2,1,0:T(1,128)} %bitcast.15), calls=%async_computation.2 | async-start | bytes 8192 | tf_op jit(solution)/shard_map/all_to_all | solution.py:85
Sparse Core Ops, SparseCore 0:
  74.8 8.8 all-gather.2
where the time goes:
time: 140 us; the launch traced here: 139 us
  waiting for transfers between devices  69 us (49%)
  local copies, waits for them, and re-layouts  24.6 us (18%)
  starting transfers between devices  21.2 us (15%)
  between operations  13.5 us (10%)
  other arithmetic  9.38 us (7%)
  matrix products  1.79 us (1%)
    all_to_all x1, waiting for transfers between devices, per_device(): lax.all_to_all(outgoing.reshape(owners, send, width), ('clus', 'sub'), sp...  36.4 us
    ppermute x1, waiting for transfers between devices, passed_along(): lax.ppermute(shard, axis, [(i, (i + by) % count) for i in range(count)])  16.7 us
    all_gather x1, waiting for transfers between devices, per_device(): whole = lax.all_gather(mine, 'rep', axis=1, tiled=True)  8.95 us
    gather x1, local copies, waits for them, and re-layouts, per_device(): answers = padded[tags].reshape(owners, send)  8.84 us
    all_to_all x1, starting transfers between devices, per_device(): lax.all_to_all(labels.reshape(owners, send), ('clus', 'sub'), split_axis=...  7.25 us
    all_to_all x1, waiting for transfers between devices, per_device(): lax.all_to_all(answers, ('clus', 'sub'), split_axis=0, concat_axis=0, til...  6.46 us
    scatter x1, local copies, waits for them, and re-layouts, per_device(): jnp.zeros((clusters_here * half, width), jnp.bfloat16).at[tags]  6.01 us
    all_to_all x1, starting transfers between devices, per_device(): lax.all_to_all(answers, ('clus', 'sub'), split_axis=0, concat_axis=0, til...  5.72 us
  transfers between devices with their start and end apart: 5, of which 5 were waited for; matrix products, arithmetic and copies ran while one was open for 5% of the time, Pallas kernels for 0%

commit v1 on v0

v1 whole, which is shorter than its diff:
```python
import functools

import jax
import jax.numpy as jnp
from jax import lax
from jax.experimental import pallas as pl
from jax.experimental.pallas import tpu as pltpu
from jax.sharding import PartitionSpec as P

CAP = 1024
HALF = CAP // 2
BORDER = 256
EPS = 1e-06
SCALE = 0.1
LANES = 128
EMPTY = 4096
OWNERS = ("clus", "sub")

ROWS_BY_ROWS = (((1,), (1,)), ((), ()))
COLS_BY_COLS = (((0,), (0,)), ((), ()))


def dot(a, b, dims=(((1,), (0,)), ((), ())), precision=None):
    return lax.dot_general(
        a, b, dims, precision=precision, preferred_element_type=jnp.float32
    )


def call(body, out_shape, flops, *args):
    moved = sum(a.size * a.dtype.itemsize for a in args)
    moved += sum(o.size * o.dtype.itemsize for o in jax.tree.leaves(out_shape))
    spec = pl.BlockSpec(memory_space=pltpu.VMEM)
    many = isinstance(out_shape, (list, tuple))
    return pl.pallas_call(
        body,
        out_shape=out_shape,
        in_specs=[spec] * len(args),
        out_specs=[spec] * len(out_shape) if many else spec,
        compiler_params=pltpu.CompilerParams(vmem_limit_bytes=40 * 2**20),
        cost_estimate=pl.CostEstimate(flops=flops, bytes_accessed=moved, transcendentals=0),
    )(*args)


def iota(shape, axis):
    return lax.broadcasted_iota(jnp.int32, shape, axis)


def one_hot(condition):
    return jnp.where(condition, 1.0, 0.0).astype(jnp.bfloat16)


def pack_body(owners, send, embeds_ref, owner_ref, *outs):
    rows, width = embeds_ref.shape
    values = embeds_ref[...].astype(jnp.float32)
    mean = jnp.sum(values * values, axis=1, keepdims=True) / width
    unit = (values * lax.rsqrt(mean + EPS)).astype(jnp.bfloat16)
    owner = owner_ref[...]
    which = iota((max(owners, 16), rows), 0) == owner
    before = one_hot(iota((rows, rows), 0) < iota((rows, rows), 1))
    counts = dot(one_hot(which), before)
    rank = jnp.sum(jnp.where(which, counts, 0.0), axis=0, keepdims=True)
    place = owner * send + rank.astype(jnp.int32)
    per = owners * send // len(outs)
    for n, out in enumerate(outs):
        chosen = one_hot(iota((per, rows), 0) + n * per == place)
        out[...] = dot(chosen, unit).astype(jnp.bfloat16)


def border_body(count, *refs):
    chunks, (tags_ref, want_ref, keep_ref, give_ref) = refs[:count], refs[count:]
    incoming = jnp.concatenate([c[...] for c in chunks], axis=0)
    chosen = one_hot(want_ref[...] == tags_ref[...])
    picked = dot(chosen, incoming).astype(jnp.bfloat16)
    keep_ref[...] = picked[: BORDER // 2]
    give_ref[...] = picked[BORDER // 2 :]


def place_body(count, *refs):
    chunks, (tags_ref, mine_ref) = refs[:count], refs[count:]
    incoming = jnp.concatenate([c[...] for c in chunks], axis=0)
    chosen = one_hot(iota((HALF, incoming.shape[0]), 0) == tags_ref[...])
    mine_ref[...] = dot(chosen, incoming).astype(jnp.bfloat16)


def weigh(products, width):
    return jnp.exp((products / width - 1.0) / SCALE)


def near_body(mine_ref, other_ref, near_ref):
    mine, other = mine_ref[...], other_ref[...]
    width = mine.shape[1]
    own = weigh(dot(mine, mine, ROWS_BY_ROWS), width)
    own = jnp.where(iota(own.shape, 0) == iota(own.shape, 1), 0.0, own)
    across = weigh(dot(other, mine, ROWS_BY_ROWS), width)
    near_ref[...] = jnp.sum(own, axis=0, keepdims=True) + jnp.sum(across, axis=0, keepdims=True)


def far_body(mine_ref, first_ref, second_ref, near_ref, scores_ref):
    mine = mine_ref[...]
    width = mine.shape[1]
    total = near_ref[...]
    for tile in (first_ref, second_ref):
        far = weigh(dot(tile[...], mine, ROWS_BY_ROWS), width)
        total = total + jnp.sum(far, axis=0, keepdims=True)
    scores = -jnp.log(total / (CAP - 1 + BORDER))
    for r in range(HALF // LANES):
        scores_ref[r : r + 1, :] = scores[:, r * LANES : (r + 1) * LANES]


def answer_body(scores_ref, where_ref, out_ref):
    scores, where = scores_ref[...], where_ref[...]
    lines, rows = scores.shape[0], where.shape[1]
    line = jnp.where(iota((lines, rows), 0) == where // LANES, 1.0, 0.0)
    found = dot(scores, line, COLS_BY_COLS, precision=lax.Precision.HIGHEST)
    lane = iota((LANES, rows), 0) == where % LANES
    out_ref[...] = jnp.sum(jnp.where(lane, found, 0.0), axis=0, keepdims=True)


def per_device(embeds, cluster_of, order_in, partner, border_idx):
    rows, width = embeds.shape
    clus_count = lax.axis_size("clus")
    owners = clus_count * lax.axis_size("sub")
    send = 2 * rows // owners
    me = lax.axis_index(OWNERS)
    side = lax.axis_index("rep")
    swap = [(0, 1), (1, 0)]
    paired = owners <= 8

    def toward(x, flip):
        return lax.ppermute(x, OWNERS, [(i, i ^ flip) for i in range(owners)])

    def gather(x):
        if not paired:
            return lax.all_gather(x, OWNERS, axis=0, tiled=True)
        flip = 1
        while flip < owners:
            x = jnp.concatenate([x, toward(x, flip)], axis=0)
            flip *= 2
        return x

    base = me if paired else jnp.zeros_like(me)
    owner = cluster_of ^ base
    chunk_count = owners if paired else 1
    chunk = jax.ShapeDtypeStruct((owners * send // chunk_count, width), jnp.bfloat16)
    chunks = call(
        functools.partial(pack_body, owners, send),
        [chunk] * chunk_count,
        2 * owners * send * rows * width,
        embeds,
        owner.reshape(1, rows),
    )
    if paired:
        order = [4, 6, 1, 2, 3, 5, 7] if owners == 8 else range(1, owners)
        got = {k: toward(chunks[k], k) for k in order}
        got[0] = chunks[0]
        chunks = [got[k] for k in range(owners)]
    else:
        blocks = chunks[0].reshape(owners, send, width)
        blocks = lax.all_to_all(blocks, OWNERS, split_axis=0, concat_axis=0, tiled=True)
        chunks = [blocks.reshape(owners * send, width)]

    every = gather((cluster_of * CAP + order_in).reshape(rows // LANES, LANES))
    every = every.reshape(owners, rows)
    mask = (every // CAP) == me
    upto = (
        jnp.arange(rows, dtype=jnp.int32)[:, None] < jnp.arange(rows, dtype=jnp.int32)[None, :]
    ).astype(jnp.bfloat16)
    rank = dot(mask.astype(jnp.bfloat16), upto).astype(jnp.int32)
    rank = jnp.where(mask, rank, -1)
    hit = rank[:, None, :] == jnp.arange(send, dtype=jnp.int32)[None, :, None]
    tags = jnp.sum(jnp.where(hit, (every % HALF - EMPTY)[:, None, :], 0), axis=2) + EMPTY
    tags = tags.reshape(1, owners * send)

    want = border_idx.reshape(BORDER, 1) - side * HALF
    want = jnp.where(side == 0, want, jnp.roll(want, BORDER // 2, axis=0))
    part = jax.ShapeDtypeStruct((BORDER // 2, width), jnp.bfloat16)
    keep, give = call(
        functools.partial(border_body, len(chunks)),
        [part, part],
        2 * BORDER * owners * send * width,
        *chunks,
        tags,
        want,
    )
    chosen = keep + lax.ppermute(give, "rep", swap)
    by = clus_count // 2
    first = lax.ppermute(chosen, "clus", [(i, (i + by) % clus_count) for i in range(clus_count)])
    mine = call(
        functools.partial(place_body, len(chunks)),
        jax.ShapeDtypeStruct((HALF, width), jnp.bfloat16),
        2 * HALF * owners * send * width,
        *chunks,
        tags,
    )
    other = lax.ppermute(mine, "rep", swap)
    near = call(
        near_body,
        jax.ShapeDtypeStruct((1, HALF), jnp.float32),
        2 * HALF * CAP * width,
        mine,
        other,
    )
    second = lax.ppermute(first, "rep", swap)
    scores = call(
        far_body,
        jax.ShapeDtypeStruct((HALF // LANES, LANES), jnp.float32),
        2 * HALF * BORDER * width,
        mine,
        first,
        second,
        near,
    )
    where = owner * HALF + order_in % HALF
    answers = call(
        answer_body,
        jax.ShapeDtypeStruct((1, rows), jnp.float32),
        2 * owners * HALF * rows,
        gather(scores),
        where.reshape(1, rows),
    )
    return answers.reshape(rows)


def solution(mesh):
    return jax.shard_map(
        per_device,
        mesh=mesh,
        in_specs=(
            P(("groups", "clus", "sub", "rep"), None),
            P(("groups", "clus", "sub", "rep")),
            P(("groups", "clus", "sub", "rep")),
            P(("groups", "clus", "sub")),
            P(("groups", "clus", "sub"), None),
        ),
        out_specs=P(("groups", "clus", "sub", "rep")),
        check_vma=False,
    )
```

time: 140 us -> 83.7 us (0.60)
  waiting for transfers between devices: 69 us -> 42.2 us
  local copies, waits for them, and re-layouts: 24.6 us -> 1.42 us
  between operations: 13.5 us -> 0.15 us
  starting transfers between devices: 21.2 us -> 32.8 us
  other arithmetic: 9.38 us -> 1.13 us
  Pallas kernels: 0 us -> 5.7 us
  matrix products: 1.79 us -> 0.18 us
    all_to_all x3 -> x0, waiting for transfers between devices: 43.4 us -> none  [the longest x1 36.4 us: per_device(): lax.all_to_all(outgoing.reshape(owners, send, width), ('clus', 'sub'), sp...]
    ppermute x1 -> x17, starting transfers between devices: 2.72 us -> 32.8 us  [the longest x13 22.8 us: toward(): return lax.ppermute(x, OWNERS, [(i, i ^ flip) for i in range(owners)])]
    ppermute x1 -> x17, waiting for transfers between devices: 16.7 us -> 42.2 us  [the longest x13 31.2 us: toward(): return lax.ppermute(x, OWNERS, [(i, i ^ flip) for i in range(owners)])]
    all_to_all x3 -> x0, starting transfers between devices: 18.4 us -> none  [the longest x1 7.25 us: per_device(): lax.all_to_all(labels.reshape(owners, send), ('clus', 'sub'), split_axis=...]
    gather x4 -> x0, local copies, waits for them, and re-layouts: 15.3 us -> none  [the longest x1 8.84 us: per_device(): answers = padded[tags].reshape(owners, send)]
    scatter x2 -> x0, local copies, waits for them, and re-layouts: 9.01 us -> none  [the longest x1 6.01 us: per_device(): jnp.zeros((clusters_here * half, width), jnp.bfloat16).at[tags]]
    all_gather x1 -> x0, waiting for transfers between devices: 8.95 us -> none  [per_device(): whole = lax.all_gather(mine, 'rep', axis=1, tiled=True)]
    pallas_call x0 -> x6, Pallas kernels: none -> 5.7 us  [call(): pl.pallas_call(body, out_shape=out_shape, in_specs=[spec] * len(args), ou...]
  transfers between devices with their start and end apart: 5 -> 17, of which waited for: 5 -> 9; matrix products, arithmetic and copies ran while one was open for 5% -> 1% of each run, Pallas kernels for 0% -> 4%
where the time goes in v1:
time: 83.7 us; the launch traced here: 83.5 us
  waiting for transfers between devices  42.2 us (50%)
  starting transfers between devices  32.8 us (39%)
  Pallas kernels  5.7 us (7%)
  local copies, waits for them, and re-layouts  1.42 us (2%)
  other arithmetic  1.13 us (1%)
    ppermute x13, waiting for transfers between devices, toward(): return lax.ppermute(x, OWNERS, [(i, i ^ flip) for i in range(owners)])  31.2 us
    ppermute x13, starting transfers between devices, toward(): return lax.ppermute(x, OWNERS, [(i, i ^ flip) for i in range(owners)])  22.8 us
    ppermute x1, waiting for transfers between devices, per_device(): lax.ppermute(chosen, 'clus', [(i, (i + by) % clus_count) for i in range(c...  9.64 us
    ppermute x1, starting transfers between devices, per_device(): lax.ppermute(chosen, 'clus', [(i, (i + by) % clus_count) for i in range(c...  9.36 us
    pallas_call x6, Pallas kernels, call(): pl.pallas_call(body, out_shape=out_shape, in_specs=[spec] * len(args), ou...  5.7 us
  transfers between devices with their start and end apart: 17, of which 9 were waited for; matrix products, arithmetic and copies ran while one was open for 1% of the time, Pallas kernels for 4%

profile of v1, /device:TPU:0, one launch (start us, length us, event | category | flops | bytes accessed | tf_op | source)
XLA Modules:
  0.0 83.5 jit_solution(3866007333395023560)
XLA Ops:
  0.0 0.7 fusion.15
  0.7 2.9 %collective-permute-start.7 = (s32[4,128]{1,0:T(4,128)S(1)}, s32[4,128]{1,0:T(4,128)S(1)}, u32[]{:S(2)}, u32[]{:S(2)}) collective-permute-start(s32[4,128]{1,0:T(4,128)S(1)} %get-tuple-element.27), channel_id=1, source_target_pairs={{0,2},{2,0},{4,6},{6,4},{8,10},{10,8},{12,14},{14,12},{1,3},{3,1},... | collective-permute-start | bytes 6152 | tf_op jit(solution)/shard_map/ppermute | solution.py:130
  3.6 0.0 copy-start
  3.6 1.1 %copy-done = bf16[512,768]{1,0:T(8,128)(2,1)S(1)} copy-done((bf16[512,768]{1,0:T(8,128)(2,1)S(1)}, bf16[512,768]{1,0:T(8,128)(2,1)}, u32[]{:S(2)}) %copy-start) | copy-done | bytes 786456
  4.8 0.0 copy-start.1
  4.8 1.2 %shard_map.46 = (bf16[128,768]{1,0:T(8,128)(2,1)S(1)}, bf16[128,768]{1,0:T(8,128)(2,1)S(1)}, bf16[128,768]{1,0:T(8,128)(2,1)S(1)}, bf16[128,768]{1,0:T(8,128)(2,...) custom-call(bf16[512,768]{1,0:T(8,128)(2,1)S(1)} %copy-done, ...), custom_call_target="tpu_custom_call" | custom-call | flops 805306368 | bytes 2361344 | tf_op jit(solution)/shard_map/pallas_call | solution.py:34
  6.0 0.1 collective-permute-start
  6.1 2.1 %collective-permute-start.1 = (bf16[128,768]{1,0:T(8,128)(2,1)S(1)}, bf16[128,768]{1,0:T(8,128)(2,1)S(1)}, u32[]{:S(2)}, u32[]{:S(2)}) collective-permute-start(bf16[128,768]{1,0:T(8,128)(2,1)S(1)} %get-tuple-element.17), channel_id=1, source_target_pairs={{0,4},{2,6},{4,0},{6,2},{8,12},{10,14},{12,8},{14,10},{1,5},{3,7},... | collective-permute-start | bytes 589832 | tf_op jit(solution)/shard_map/ppermute | solution.py:130
  8.2 1.4 %collective-permute-start.2 = (bf16[128,768]{1,0:T(8,128)(2,1)S(1)}, bf16[128,768]{1,0:T(8,128)(2,1)S(1)}, u32[]{:S(2)}, u32[]{:S(2)}) collective-permute-start(bf16[128,768]{1,0:T(8,128)(2,1)S(1)} %get-tuple-element.18), channel_id=1, source_target_pairs={{0,6},{2,4},{4,2},{6,0},{8,14},{10,12},{12,10},{14,8},{1,7},{3,5},... | collective-permute-start | bytes 589832 | tf_op jit(solution)/shard_map/ppermute | solution.py:130
  9.6 2.6 %collective-permute-start.3 = (bf16[128,768]{1,0:T(8,128)(2,1)S(1)}, bf16[128,768]{1,0:T(8,128)(2,1)S(1)}, u32[]{:S(2)}, u32[]{:S(2)}) collective-permute-start(bf16[128,768]{1,0:T(8,128)(2,1)S(1)} %get-tuple-element.19), channel_id=1, source_target_pairs={{0,8},{2,10},{4,12},{6,14},{8,0},{10,2},{12,4},{14,6},{1,9},{3,11}... | collective-permute-start | bytes 589832 | tf_op jit(solution)/shard_map/ppermute | solution.py:130
  12.2 0.0 copy-done.1
  12.2 0.0 collective-permute-done.7
  12.2 1.6 %collective-permute-start.8 = (s32[8,128]{1,0:T(8,128)S(1)}, s32[8,128]{1,0:T(8,128)S(1)}, u32[]{:S(2)}, u32[]{:S(2)}) collective-permute-start(s32[8,128]{1,0:T(8,128)S(1)} %pad_add_fusion.2), channel_id=1, source_target_pairs={{0,4},{2,6},{4,0},{6,2},{8,12},{10,14},{12,8},{14,10},{1,5},{3,7},... | collective-permute-start | bytes 12296 | tf_op jit(solution)/shard_map/ppermute | solution.py:130
  13.8 7.2 %collective-permute-done.8 = s32[8,128]{1,0:T(8,128)S(1)} collective-permute-done((s32[8,128]{1,0:T(8,128)S(1)}, s32[8,128]{1,0:T(8,128)S(1)}, u32[]{:S(2)}, u32[]{:S(2)}) %collective-permute-start.8) | collective-permute-done | bytes 4128 | tf_op jit(solution)/shard_map/ppermute | solution.py:130
  21.1 2.8 %collective-permute-start.9 = (s32[16,128]{1,0:T(8,128)S(1)}, s32[16,128]{1,0:T(8,128)S(1)}, u32[]{:S(2)}, u32[]{:S(2)}) collective-permute-start(s32[16,128]{1,0:T(8,128)S(1)} %pad_add_fusion.1), channel_id=1, source_target_pairs={{0,8},{2,10},{4,12},{6,14},{8,0},{10,2},{12,4},{14,6},{1,9},{3,11}... | collective-permute-start | bytes 24584 | tf_op jit(solution)/shard_map/ppermute | solution.py:130
  23.8 1.8 %collective-permute-done.9 = s32[16,128]{1,0:T(8,128)S(1)} collective-permute-done((s32[16,128]{1,0:T(8,128)S(1)}, s32[16,128]{1,0:T(8,128)S(1)}, u32[]{:S(2)}, u32[]{:S(2)}) %collective-permute-start.9) | collective-permute-done | bytes 8224 | tf_op jit(solution)/shard_map/ppermute | solution.py:130
  25.6 3.7 %collective-permute-start.4 = (bf16[128,768]{1,0:T(8,128)(2,1)S(1)}, bf16[128,768]{1,0:T(8,128)(2,1)S(1)}, u32[]{:S(2)}, u32[]{:S(2)}) collective-permute-start(bf16[128,768]{1,0:T(8,128)(2,1)S(1)} %get-tuple-element.20), channel_id=1, source_target_pairs={{0,10},{2,8},{4,14},{6,12},{8,2},{10,0},{12,6},{14,4},{1,11},{3,9}... | collective-permute-start | bytes 589832 | tf_op jit(solution)/shard_map/ppermute | solution.py:130
  29.3 0.2 fusion
  29.5 0.3 select_reduce_fusion
  29.8 0.0 collective-permute-done.refs_1_
  29.8 1.5 %collective-permute-start.5 = (bf16[128,768]{1,0:T(8,128)(2,1)S(1)}, bf16[128,768]{1,0:T(8,128)(2,1)S(1)}, u32[]{:S(2)}, u32[]{:S(2)}) collective-permute-start(bf16[128,768]{1,0:T(8,128)(2,1)S(1)} %get-tuple-element.21), channel_id=1, source_target_pairs={{0,12},{2,14},{4,8},{6,10},{8,4},{10,6},{12,0},{14,2},{1,13},{3,15... | collective-permute-start | bytes 589832 | tf_op jit(solution)/shard_map/ppermute | solution.py:130
  31.3 0.0 collective-permute-done.1.refs_2_
  31.3 2.4 %collective-permute-start.6 = (bf16[128,768]{1,0:T(8,128)(2,1)S(1)}, bf16[128,768]{1,0:T(8,128)(2,1)S(1)}, u32[]{:S(2)}, u32[]{:S(2)}) collective-permute-start(bf16[128,768]{1,0:T(8,128)(2,1)S(1)} %get-tuple-element.22), channel_id=1, source_target_pairs={{0,14},{2,12},{4,10},{6,8},{8,6},{10,4},{12,2},{14,0},{1,15},{3,13... | collective-permute-start | bytes 589832 | tf_op jit(solution)/shard_map/ppermute | solution.py:130
  33.7 0.0 collective-permute-done.2.refs_3_
  33.7 0.0 collective-permute-done.3.refs_4_
  33.7 12.1 %collective-permute-done.4.refs_5_ = bf16[128,768]{1,0:T(8,128)(2,1)S(1)} collective-permute-done((bf16[128,768]{1,0:T(8,128)(2,1)S(1)}, bf16[128,768]{1,0:T(8,128)(2,1)S(1)}, u32[]{:S(2)}, u32[]{:S(2)}) %collective-permute-start.4) | collective-permute-done | bytes 196640 | tf_op jit(solution)/shard_map/ppermute | solution.py:130
  45.8 0.0 collective-permute-done.5.refs_6_
  45.8 0.0 collective-permute-done.6.refs_7_
  45.8 1.0 %shard_map.47.mine_ref = bf16[512,768]{1,0:T(8,128)(2,1)S(1)} custom-call(bf16[128,768]{1,0:T(8,128)(2,1)S(1)} %get-tuple-element.15.refs_0_, bf16[128,768]{1,0:T(8,128)(2,1)S(1)} %collective-permute-done.refs_1_, bf16[128,768]{1,0:T(8,128)(2,1)S(1)} %collective-permute-done.1.refs_2_, bf16[128,768]{1,0:T(8,128)(2,1)S(1)} %collective-permute-done.2.refs_3_, ...), custom_call_target="tpu_custom_call" | custom-call | flops 805306368 | bytes 2363392 | tf_op jit(solution)/shard_map/pallas_call | solution.py:34
  46.8 0.1 collective-permute-start.13
  46.9 0.1 copy.13
  47.0 0.1 copy.12
  47.2 0.6 shard_map.48
  47.8 0.6 collective-permute-start.10
  48.4 1.1 %collective-permute-done.10 = bf16[128,768]{1,0:T(8,128)(2,1)S(1)} collective-permute-done((bf16[128,768]{1,0:T(8,128)(2,1)S(1)}, bf16[128,768]{1,0:T(8,128)(2,1)S(1)}, u32[]{:S(2)}, u32[]{:S(2)}) %collective-permute-start.10) | collective-permute-done | bytes 196640 | tf_op jit(solution)/shard_map/ppermute | solution.py:185
  49.5 0.1 add.56
  49.5 9.4 %collective-permute-start.11 = (bf16[128,768]{1,0:T(8,128)(2,1)S(1)}, bf16[128,768]{1,0:T(8,128)(2,1)S(1)}, u32[]{:S(2)}, u32[]{:S(2)}) collective-permute-start(bf16[128,768]{1,0:T(8,128)(2,1)S(1)} %add.56), channel_id=1, source_target_pairs={{0,8},{4,12},{8,0},{12,4},{1,9},{5,13},{9,1},{13,5},{2,10},{6,14},... | collective-permute-start | bytes 589832 | tf_op jit(solution)/shard_map/ppermute | solution.py:187
  58.9 9.6 %collective-permute-done.11.first_ref = bf16[128,768]{1,0:T(8,128)(2,1)S(1)} collective-permute-done((bf16[128,768]{1,0:T(8,128)(2,1)S(1)}, bf16[128,768]{1,0:T(8,128)(2,1)S(1)}, u32[]{:S(2)}, u32[]{:S(2)}) %collective-permute-start.11) | collective-permute-done | bytes 196640 | tf_op jit(solution)/shard_map/ppermute | solution.py:187
  68.5 0.0 collective-permute-start.12
  68.5 0.0 collective-permute-done.13.other_ref
  68.5 1.1 %shard_map.49.near_ref = f32[1,512]{1,0:T(1,128)S(1)} custom-call(bf16[512,768]{1,0:T(8,128)(2,1)S(1)} %shard_map.47.mine_ref, bf16[512,768]{1,0:T(8,128)(2,1)S(1)} %collective-permute-done.13.other_ref), custom_call_target="tpu_custom_call" | custom-call | flops 805306368 | bytes 1574912 | tf_op jit(solution)/shard_map/pallas_call | solution.py:34
  69.7 0.3 collective-permute-done.12.second_ref
  70.0 0.7 shard_map.50
  70.6 1.7 %collective-permute-start.14 = (f32[4,128]{1,0:T(4,128)S(1)}, f32[4,128]{1,0:T(4,128)S(1)}, u32[]{:S(2)}, u32[]{:S(2)}) collective-permute-start(f32[4,128]{1,0:T(4,128)S(1)} %shard_map.50), channel_id=1, source_target_pairs={{0,2},{2,0},{4,6},{6,4},{8,10},{10,8},{12,14},{14,12},{1,3},{3,1},... | collective-permute-start | bytes 6152 | tf_op jit(solution)/shard_map/ppermute | solution.py:130
  72.4 1.9 %collective-permute-done.14 = f32[4,128]{1,0:T(4,128)S(1)} collective-permute-done((f32[4,128]{1,0:T(4,128)S(1)}, f32[4,128]{1,0:T(4,128)S(1)}, u32[]{:S(2)}, u32[]{:S(2)}) %collective-permute-start.14) | collective-permute-done | bytes 2080 | tf_op jit(solution)/shard_map/ppermute | solution.py:130
  74.3 0.0 collective-permute-start.15
  74.3 3.6 %collective-permute-done.15 = f32[8,128]{1,0:T(8,128)S(1)} collective-permute-done((f32[8,128]{1,0:T(8,128)S(1)}, f32[8,128]{1,0:T(8,128)S(1)}, u32[]{:S(2)}, u32[]{:S(2)}) %collective-permute-start.15) | collective-permute-done | bytes 4128 | tf_op jit(solution)/shard_map/ppermute | solution.py:130
  77.9 0.1 collective-permute-start.16
  78.0 4.5 %collective-permute-done.16 = f32[16,128]{1,0:T(8,128)S(1)} collective-permute-done((f32[16,128]{1,0:T(8,128)S(1)}, f32[16,128]{1,0:T(8,128)S(1)}, u32[]{:S(2)}, u32[]{:S(2)}) %collective-permute-start.16) | collective-permute-done | bytes 8224 | tf_op jit(solution)/shard_map/ppermute | solution.py:130
  82.5 1.0 %shard_map.51 = f32[1,512]{1,0:T(1,128)} custom-call(f32[32,128]{1,0:T(8,128)S(1)} %pad_maximum_fusion.scores_ref, s32[1,512]{1,0:T(1,128)S(1)} %bitcast.14), custom_call_target="tpu_custom_call" | custom-call | flops 4194304 | bytes 20480 | tf_op jit(solution)/shard_map/pallas_call | solution.py:34
  (14 shorter events, 0.1 us)
Async XLA Ops:
  0.7 11.5 %collective-permute-start.7 = (s32[4,128]{1,0:T(4,128)S(1)}, s32[4,128]{1,0:T(4,128)S(1)}, u32[]{:S(2)}, u32[]{:S(2)}) collective-permute-start(s32[4,128]{1,0:T(4,128)S(1)} %get-tuple-element.27), channel_id=1, source_target_pairs={{0,2},{2,0},{4,6},{6,4},{8,10},{10,8},{12,14},{14,12},{1,3},{3,1},... | collective-permute-start | bytes 6152 | tf_op jit(solution)/shard_map/ppermute | solution.py:130
  3.6 1.1 %copy-start = (bf16[512,768]{1,0:T(8,128)(2,1)S(1)}, bf16[512,768]{1,0:T(8,128)(2,1)}, u32[]{:S(2)}) copy-start(bf16[512,768]{1,0:T(8,128)(2,1)} %embeds_ref.1) | copy-start | bytes 2359300
  4.8 7.4 %copy-start.1 = (s32[1,256]{1,0:T(1,128)S(1)}, s32[1,256]{1,0:T(1,128)}, u32[]{:S(2)}) copy-start(s32[1,256]{1,0:T(1,128)} %param.8) | copy-start | bytes 3076
  6.0 23.8 %collective-permute-start = (bf16[128,768]{1,0:T(8,128)(2,1)S(1)}, bf16[128,768]{1,0:T(8,128)(2,1)S(1)}, u32[]{:S(2)}, u32[]{:S(2)}) collective-permute-start(bf16[128,768]{1,0:T(8,128)(2,1)S(1)} %get-tuple-element.16), channel_id=1, source_target_pairs={{0,2},{2,0},{4,6},{6,4},{8,10},{10,8},{12,14},{14,12},{1,3},{3,1},... | collective-permute-start | bytes 589832 | tf_op jit(solution)/shard_map/ppermute | solution.py:130
  6.1 25.2 %collective-permute-start.1 = (bf16[128,768]{1,0:T(8,128)(2,1)S(1)}, bf16[128,768]{1,0:T(8,128)(2,1)S(1)}, u32[]{:S(2)}, u32[]{:S(2)}) collective-permute-start(bf16[128,768]{1,0:T(8,128)(2,1)S(1)} %get-tuple-element.17), channel_id=1, source_target_pairs={{0,4},{2,6},{4,0},{6,2},{8,12},{10,14},{12,8},{14,10},{1,5},{3,7},... | collective-permute-start | bytes 589832 | tf_op jit(solution)/shard_map/ppermute | solution.py:130
  8.2 25.5 %collective-permute-start.2 = (bf16[128,768]{1,0:T(8,128)(2,1)S(1)}, bf16[128,768]{1,0:T(8,128)(2,1)S(1)}, u32[]{:S(2)}, u32[]{:S(2)}) collective-permute-start(bf16[128,768]{1,0:T(8,128)(2,1)S(1)} %get-tuple-element.18), channel_id=1, source_target_pairs={{0,6},{2,4},{4,2},{6,0},{8,14},{10,12},{12,10},{14,8},{1,7},{3,5},... | collective-permute-start | bytes 589832 | tf_op jit(solution)/shard_map/ppermute | solution.py:130
  9.6 24.1 %collective-permute-start.3 = (bf16[128,768]{1,0:T(8,128)(2,1)S(1)}, bf16[128,768]{1,0:T(8,128)(2,1)S(1)}, u32[]{:S(2)}, u32[]{:S(2)}) collective-permute-start(bf16[128,768]{1,0:T(8,128)(2,1)S(1)} %get-tuple-element.19), channel_id=1, source_target_pairs={{0,8},{2,10},{4,12},{6,14},{8,0},{10,2},{12,4},{14,6},{1,9},{3,11}... | collective-permute-start | bytes 589832 | tf_op jit(solution)/shard_map/ppermute | solution.py:130
  12.2 8.9 %collective-permute-start.8 = (s32[8,128]{1,0:T(8,128)S(1)}, s32[8,128]{1,0:T(8,128)S(1)}, u32[]{:S(2)}, u32[]{:S(2)}) collective-permute-start(s32[8,128]{1,0:T(8,128)S(1)} %pad_add_fusion.2), channel_id=1, source_target_pairs={{0,4},{2,6},{4,0},{6,2},{8,12},{10,14},{12,8},{14,10},{1,5},{3,7},... | collective-permute-start | bytes 12296 | tf_op jit(solution)/shard_map/ppermute | solution.py:130
  21.1 4.5 %collective-permute-start.9 = (s32[16,128]{1,0:T(8,128)S(1)}, s32[16,128]{1,0:T(8,128)S(1)}, u32[]{:S(2)}, u32[]{:S(2)}) collective-permute-start(s32[16,128]{1,0:T(8,128)S(1)} %pad_add_fusion.1), channel_id=1, source_target_pairs={{0,8},{2,10},{4,12},{6,14},{8,0},{10,2},{12,4},{14,6},{1,9},{3,11}... | collective-permute-start | bytes 24584 | tf_op jit(solution)/shard_map/ppermute | solution.py:130
  25.6 20.2 %collective-permute-start.4 = (bf16[128,768]{1,0:T(8,128)(2,1)S(1)}, bf16[128,768]{1,0:T(8,128)(2,1)S(1)}, u32[]{:S(2)}, u32[]{:S(2)}) collective-permute-start(bf16[128,768]{1,0:T(8,128)(2,1)S(1)} %get-tuple-element.20), channel_id=1, source_target_pairs={{0,10},{2,8},{4,14},{6,12},{8,2},{10,0},{12,6},{14,4},{1,11},{3,9}... | collective-permute-start | bytes 589832 | tf_op jit(solution)/shard_map/ppermute | solution.py:130
  29.8 16.0 %collective-permute-start.5 = (bf16[128,768]{1,0:T(8,128)(2,1)S(1)}, bf16[128,768]{1,0:T(8,128)(2,1)S(1)}, u32[]{:S(2)}, u32[]{:S(2)}) collective-permute-start(bf16[128,768]{1,0:T(8,128)(2,1)S(1)} %get-tuple-element.21), channel_id=1, source_target_pairs={{0,12},{2,14},{4,8},{6,10},{8,4},{10,6},{12,0},{14,2},{1,13},{3,15... | collective-permute-start | bytes 589832 | tf_op jit(solution)/shard_map/ppermute | solution.py:130
  31.3 14.5 %collective-permute-start.6 = (bf16[128,768]{1,0:T(8,128)(2,1)S(1)}, bf16[128,768]{1,0:T(8,128)(2,1)S(1)}, u32[]{:S(2)}, u32[]{:S(2)}) collective-permute-start(bf16[128,768]{1,0:T(8,128)(2,1)S(1)} %get-tuple-element.22), channel_id=1, source_target_pairs={{0,14},{2,12},{4,10},{6,8},{8,6},{10,4},{12,2},{14,0},{1,15},{3,13... | collective-permute-start | bytes 589832 | tf_op jit(solution)/shard_map/ppermute | solution.py:130
  46.8 21.7 %collective-permute-start.13 = (bf16[512,768]{1,0:T(8,128)(2,1)S(1)}, bf16[512,768]{1,0:T(8,128)(2,1)S(1)}, u32[]{:S(2)}, u32[]{:S(2)}) collective-permute-start(bf16[512,768]{1,0:T(8,128)(2,1)S(1)} %shard_map.47.mine_ref), channel_id=1, source_target_pairs={{0,1},{1,0},{2,3},{3,2},{4,5},{5,4},{6,7},{7,6},{8,9},{9,8},{10,11... | collective-permute-start | bytes 2359304 | tf_op jit(solution)/shard_map/ppermute | solution.py:195
  47.8 1.6 %collective-permute-start.10 = (bf16[128,768]{1,0:T(8,128)(2,1)S(1)}, bf16[128,768]{1,0:T(8,128)(2,1)S(1)}, u32[]{:S(2)}, u32[]{:S(2)}) collective-permute-start(bf16[128,768]{1,0:T(8,128)(2,1)S(1)} %get-tuple-element.24), channel_id=1, source_target_pairs={{0,1},{1,0},{2,3},{3,2},{4,5},{5,4},{6,7},{7,6},{8,9},{9,8},{10,11... | collective-permute-start | bytes 589832 | tf_op jit(solution)/shard_map/ppermute | solution.py:185
  49.5 19.0 %collective-permute-start.11 = (bf16[128,768]{1,0:T(8,128)(2,1)S(1)}, bf16[128,768]{1,0:T(8,128)(2,1)S(1)}, u32[]{:S(2)}, u32[]{:S(2)}) collective-permute-start(bf16[128,768]{1,0:T(8,128)(2,1)S(1)} %add.56), channel_id=1, source_target_pairs={{0,8},{4,12},{8,0},{12,4},{1,9},{5,13},{9,1},{13,5},{2,10},{6,14},... | collective-permute-start | bytes 589832 | tf_op jit(solution)/shard_map/ppermute | solution.py:187
  68.5 1.4 %collective-permute-start.12 = (bf16[128,768]{1,0:T(8,128)(2,1)S(1)}, bf16[128,768]{1,0:T(8,128)(2,1)S(1)}, u32[]{:S(2)}, u32[]{:S(2)}) collective-permute-start(bf16[128,768]{1,0:T(8,128)(2,1)S(1)} %collective-permute-done.11.first_ref), channel_id=1, source_target_pairs={{0,1},{1,0},{2,3},{3,2},{4,5},{5,4},{6,7},{7,6},{8,9},{9,8},{10,11... | collective-permute-start | bytes 589832 | tf_op jit(solution)/shard_map/ppermute | solution.py:203
  70.6 3.7 %collective-permute-start.14 = (f32[4,128]{1,0:T(4,128)S(1)}, f32[4,128]{1,0:T(4,128)S(1)}, u32[]{:S(2)}, u32[]{:S(2)}) collective-permute-start(f32[4,128]{1,0:T(4,128)S(1)} %shard_map.50), channel_id=1, source_target_pairs={{0,2},{2,0},{4,6},{6,4},{8,10},{10,8},{12,14},{14,12},{1,3},{3,1},... | collective-permute-start | bytes 6152 | tf_op jit(solution)/shard_map/ppermute | solution.py:130
  74.3 3.6 %collective-permute-start.15 = (f32[8,128]{1,0:T(8,128)S(1)}, f32[8,128]{1,0:T(8,128)S(1)}, u32[]{:S(2)}, u32[]{:S(2)}) collective-permute-start(f32[8,128]{1,0:T(8,128)S(1)} %pad_maximum_fusion.2), channel_id=1, source_target_pairs={{0,4},{2,6},{4,0},{6,2},{8,12},{10,14},{12,8},{14,10},{1,5},{3,7},... | collective-permute-start | bytes 12296 | tf_op jit(solution)/shard_map/ppermute | solution.py:130
  77.9 4.6 %collective-permute-start.16 = (f32[16,128]{1,0:T(8,128)S(1)}, f32[16,128]{1,0:T(8,128)S(1)}, u32[]{:S(2)}, u32[]{:S(2)}) collective-permute-start(f32[16,128]{1,0:T(8,128)S(1)} %pad_maximum_fusion.1), channel_id=1, source_target_pairs={{0,8},{2,10},{4,12},{6,14},{8,0},{10,2},{12,4},{14,6},{1,9},{3,11}... | collective-permute-start | bytes 24584 | tf_op jit(solution)/shard_map/ppermute | solution.py:130

commit v2 on v1

v2 whole, which is shorter than its diff:
```python
import functools

import jax
import jax.numpy as jnp
from jax import lax
from jax.experimental import pallas as pl
from jax.experimental.pallas import tpu as pltpu
from jax.sharding import PartitionSpec as P

CAP = 1024
HALF = CAP // 2
BORDER = 256
EPS = 1e-06
SCALE = 0.1
LANES = 128
TAG_ROWS = 8
TAG_BASE = 32
EMPTY = 4096
PIECES = 4
OWNERS = ("clus", "sub")

ROWS_BY_ROWS = (((1,), (1,)), ((), ()))


def dot(a, b, dims=(((1,), (0,)), ((), ()))):
    return lax.dot_general(a, b, dims, preferred_element_type=jnp.float32)


def call(body, out_shape, flops, *args, after=()):
    leaves, tree = jax.tree.flatten(args)
    moved = sum(a.size * a.dtype.itemsize for a in leaves)
    moved += sum(o.size * o.dtype.itemsize for o in jax.tree.leaves(out_shape))
    spec = pl.BlockSpec(memory_space=pltpu.VMEM)
    many = isinstance(out_shape, (list, tuple))
    count = len(leaves)

    def kernel(*refs):
        body(*jax.tree.unflatten(tree, refs[:count]), *refs[count + len(after) :])

    return pl.pallas_call(
        kernel,
        out_shape=out_shape,
        in_specs=[spec] * count + [pl.BlockSpec(memory_space=pl.ANY)] * len(after),
        out_specs=[spec] * len(out_shape) if many else spec,
        compiler_params=pltpu.CompilerParams(vmem_limit_bytes=40 * 2**20),
        cost_estimate=pl.CostEstimate(flops=flops, bytes_accessed=moved, transcendentals=0),
    )(*leaves, *after)


def iota(shape, axis):
    return lax.broadcasted_iota(jnp.int32, shape, axis)


def one_hot(condition):
    return jnp.where(condition, 1.0, 0.0).astype(jnp.bfloat16)


TAGS = {
    0: ((0,), ()),
    1: ((1, 3, 5, 7), ()),
    2: ((2, 6), ((1, 1), (1, 3))),
    4: ((4,), ((1, 2), (2, 1), (2, 3))),
}
TAG_LINE = ((0, 0), (1, 0), (2, 0), (2, 2), (4, 0), (4, 1), (4, 2), (4, 3))
STEPS = (((7, 6, 1, 3, 0), ()), ((2, 5), (1,)), ((4,), (1, 2)))


def pack(send, blocks, unit, place, position, arrived, outs):
    rows, width = unit.shape
    parts = jnp.where(iota((16, rows), 0) == 0, position // TAG_BASE, position % TAG_BASE)
    parts = parts.astype(jnp.float32).astype(jnp.bfloat16)

    def chosen(block):
        return one_hot(iota((send, rows), 0) + block * send == place)

    def tag_line(block):
        found = dot(parts, chosen(block), ROWS_BY_ROWS)
        return jnp.concatenate([found[0:1], found[1:2]], axis=1)

    for block, out in zip(blocks, outs):
        out[:send, :] = dot(chosen(block), unit).astype(jnp.bfloat16)
        if block in TAGS:
            own, handed = TAGS[block]
            lines = [tag_line(b) for b in own]
            lines += [arrived[c][send:, : 2 * send][n : n + 1] for c, n in handed]
            lines = [line.astype(jnp.float32) for line in lines]
            lines.append(jnp.zeros((TAG_ROWS - len(lines), 2 * send), jnp.float32))
            lines = jnp.concatenate(lines, axis=0)
            rest = jnp.zeros((TAG_ROWS, width - 2 * send), jnp.float32)
            out[send:, :] = jnp.concatenate([lines, rest], axis=1).astype(jnp.bfloat16)


def rank_body(owners, send, cluster_ref, base_ref, place_ref):
    rows = cluster_ref.shape[1]
    owner = cluster_ref[...] ^ base_ref[...]
    which = iota((max(owners, 16), rows), 0) == owner
    before = one_hot(iota((rows, rows), 0) < iota((rows, rows), 1))
    counts = dot(one_hot(which), before)
    rank = jnp.sum(jnp.where(which, counts, 0.0), axis=0, keepdims=True)
    place_ref[...] = owner * send + rank.astype(jnp.int32)


def first_body(send, blocks, embeds_ref, place_ref, order_ref, unit_ref, *outs):
    values = embeds_ref[...].astype(jnp.float32)
    mean = jnp.sum(values * values, axis=1, keepdims=True) / values.shape[1]
    unit = (values * lax.rsqrt(mean + EPS)).astype(jnp.bfloat16)
    unit_ref[...] = unit
    place = place_ref[...]
    if blocks:
        pack(send, blocks, unit, place, order_ref[...] % HALF + 1, {}, outs)
    else:
        (out,) = outs
        chosen = one_hot(iota((out.shape[0], place.shape[1]), 0) == place)
        out[...] = dot(chosen, unit).astype(jnp.bfloat16)


def pack_body(send, blocks, unit_ref, place_ref, order_ref, arrived, *outs):
    position = order_ref[...] % HALF + 1
    pack(send, blocks, unit_ref[...], place_ref[...], position, arrived, outs)


def tags_of(chunks, tags, send):
    if tags:
        return tags[0][...]
    found = []
    for chunk, line in TAG_LINE:
        lines = chunks[chunk][send:, : 2 * send].astype(jnp.float32)[line : line + 1]
        found.append(lines[:, :send] * TAG_BASE + lines[:, send:])
    found = jnp.concatenate(found, axis=1).astype(jnp.int32)
    return jnp.where(found == 0, EMPTY, found - 1)


def rows_of(chunks, send):
    if 1 not in chunks:
        return chunks[0][...]
    return jnp.concatenate([chunks[k][:send, :] for k in range(8)], axis=0)


def border_body(send, chunks, want_ref, tags, keep_ref, give_ref):
    chosen = one_hot(want_ref[...] == tags_of(chunks, tags, send))
    picked = dot(chosen, rows_of(chunks, send)).astype(jnp.bfloat16)
    keep_ref[...] = picked[: BORDER // 2]
    give_ref[...] = picked[BORDER // 2 :]


def place_body(send, chunks, tags, *mine_refs):
    tags = tags_of(chunks, tags, send)
    rows = rows_of(chunks, send)
    first = 0
    for mine_ref in mine_refs:
        count = mine_ref.shape[0]
        chosen = one_hot(iota((count, tags.shape[1]), 0) + first == tags)
        mine_ref[...] = dot(chosen, rows).astype(jnp.bfloat16)
        first += count


def weigh(products, width):
    return jnp.exp((products / width - 1.0) / SCALE)


def near_body(mine_refs, other_refs, near_ref):
    mine = jnp.concatenate([ref[...] for ref in mine_refs], axis=0)
    other = jnp.concatenate([ref[...] for ref in other_refs], axis=0)
    width = mine.shape[1]
    own = weigh(dot(mine, mine, ROWS_BY_ROWS), width)
    own = jnp.where(iota(own.shape, 0) == iota(own.shape, 1), 0.0, own)
    across = weigh(dot(other, mine, ROWS_BY_ROWS), width)
    near_ref[...] = jnp.sum(own, axis=0, keepdims=True) + jnp.sum(across, axis=0, keepdims=True)


def far_body(mine_refs, other_refs, tile_ref, near_ref, here_ref, there_ref):
    tile = tile_ref[...]
    for rows_refs, out_ref in ((mine_refs, here_ref), (other_refs, there_ref)):
        rows = jnp.concatenate([ref[...] for ref in rows_refs], axis=0)
        far = weigh(dot(tile, rows, ROWS_BY_ROWS), tile.shape[1])
        total = jnp.sum(far, axis=0, keepdims=True)
        if out_ref is here_ref:
            total = total + near_ref[...]
        for r in range(HALF // LANES):
            out_ref[r : r + 1, :] = total[:, r * LANES : (r + 1) * LANES]


def answer_body(scores_ref, cluster_ref, order_ref, base_ref, out_ref):
    lines_each = HALF // LANES
    place = order_ref[...] % HALF
    line = (cluster_ref[...] ^ base_ref[...]) * lines_each + place // LANES
    lane = place % LANES

    def add(n, found):
        scores = jnp.broadcast_to(scores_ref[pl.ds(n, 1), :], lane.shape)
        there = jnp.take_along_axis(scores, lane, axis=1)
        return jnp.where(line == n, there, found)

    lines = scores_ref.shape[0]
    found = jnp.zeros(lane.shape, jnp.float32)
    out_ref[...] = lax.fori_loop(0, lines, add, found, unroll=lines <= 64)


def per_device(embeds, cluster_of, order_in, partner, border_idx):
    rows, width = embeds.shape
    clus_count = lax.axis_size("clus")
    owners = clus_count * lax.axis_size("sub")
    send = 2 * rows // owners
    me = lax.axis_index(OWNERS)
    side = lax.axis_index("rep")
    swap = [(0, 1), (1, 0)]
    paired = owners == 8

    def toward(x, flip):
        return lax.ppermute(x, OWNERS, [(i, i ^ flip) for i in range(owners)])

    def gather(x):
        if not paired:
            return lax.all_gather(x, OWNERS, axis=0, tiled=True)
        for flip in (1, 2, 4):
            x = jnp.concatenate([x, toward(x, flip)], axis=0)
        return x

    base = me if paired else jnp.zeros_like(me)
    base = base.reshape(1, 1)
    cluster_row = cluster_of.reshape(1, rows)
    order_row = order_in.reshape(1, rows)

    def shapes(blocks):
        sizes = [(send + TAG_ROWS * (b in TAGS), width) for b in blocks] or [(owners * send, width)]
        return [jax.ShapeDtypeStruct(size, jnp.bfloat16) for size in sizes]

    place = call(
        functools.partial(rank_body, owners, send),
        jax.ShapeDtypeStruct((1, rows), jnp.int32),
        2 * owners * rows * rows,
        cluster_row,
        base,
    )

    def first(blocks):
        return call(
            functools.partial(first_body, send, blocks),
            [jax.ShapeDtypeStruct((rows, width), jnp.bfloat16), *shapes(blocks)],
            2 * rows * rows * width,
            embeds,
            place,
            order_row,
        )

    if paired:
        chunks = {}
        for blocks, needed in STEPS:
            if not chunks:
                unit, *packed = first(blocks)
            else:
                handed = {k: chunks[k] for k in needed}
                packed = call(
                    functools.partial(pack_body, send, blocks),
                    shapes(blocks),
                    2 * len(blocks) * send * rows * width,
                    unit,
                    place,
                    order_row,
                    handed,
                )
            for block, chunk in zip(blocks, packed):
                chunks[block] = toward(chunk, block) if block else chunk
        tags = []
    else:
        _, blocks = first(())
        blocks = blocks.reshape(owners, send, width)
        blocks = lax.all_to_all(blocks, OWNERS, split_axis=0, concat_axis=0, tiled=True)
        chunks = {0: blocks.reshape(owners * send, width)}
        every = gather(cluster_of * CAP + order_in).reshape(owners, rows)
        mask = (every // CAP) == me
        index = jnp.arange(rows, dtype=jnp.int32)
        before = (index[:, None] < index[None, :]).astype(jnp.bfloat16)
        rank = dot(mask.astype(jnp.bfloat16), before).astype(jnp.int32)
        rank = jnp.where(mask, rank, -1)
        hit = rank[:, None, :] == index[None, :send, None]
        found = jnp.sum(jnp.where(hit, (every % HALF - EMPTY)[:, None, :], 0), axis=2) + EMPTY
        tags = [found.reshape(1, owners * send)]

    want = border_idx.reshape(BORDER, 1) - side * HALF
    want = jnp.where(side == 0, want, jnp.roll(want, BORDER // 2, axis=0))
    by = clus_count // 2
    across = [(i, (i + by) % clus_count) for i in range(clus_count)]
    part = jax.ShapeDtypeStruct((BORDER // 2, width), jnp.bfloat16)
    keep, give = call(
        functools.partial(border_body, send),
        [part, part],
        2 * BORDER * owners * send * width,
        chunks,
        want,
        tags,
    )
    tile = lax.ppermute(keep + lax.ppermute(give, "rep", swap), "clus", across)
    part = jax.ShapeDtypeStruct((HALF // PIECES, width), jnp.bfloat16)
    mine = call(
        functools.partial(place_body, send),
        [part] * PIECES,
        2 * HALF * owners * send * width,
        chunks,
        tags,
        after=[give],
    )
    other = [lax.ppermute(part, "rep", swap) for part in mine]
    near = call(
        near_body,
        jax.ShapeDtypeStruct((1, HALF), jnp.float32),
        2 * HALF * CAP * width,
        mine,
        other,
    )
    lines = jax.ShapeDtypeStruct((HALF // LANES, LANES), jnp.float32)
    here, there = call(
        far_body,
        [lines, lines],
        2 * HALF * BORDER * width,
        mine,
        other,
        tile,
        near,
    )
    total = here + lax.ppermute(there, "rep", swap)
    scores = -jnp.log(total / (CAP - 1 + BORDER))
    answers = call(
        answer_body,
        jax.ShapeDtypeStruct((rows // LANES, LANES), jnp.float32),
        owners * HALF,
        gather(scores),
        cluster_of.reshape(rows // LANES, LANES),
        order_in.reshape(rows // LANES, LANES),
        base,
    )
    return answers.reshape(rows)


def solution(mesh):
    return jax.shard_map(
        per_device,
        mesh=mesh,
        in_specs=(
            P(("groups", "clus", "sub", "rep"), None),
            P(("groups", "clus", "sub", "rep")),
            P(("groups", "clus", "sub", "rep")),
            P(("groups", "clus", "sub")),
            P(("groups", "clus", "sub"), None),
        ),
        out_specs=P(("groups", "clus", "sub", "rep")),
        check_vma=False,
    )
```

time: 83.7 us -> 74.8 us (0.89)
  starting transfers between devices: 32.8 us -> 23.3 us
  local copies, waits for them, and re-layouts: 1.42 us -> 3.21 us
  other arithmetic: 1.13 us -> 0.11 us
    ppermute x4 -> x7, starting transfers between devices: 9.98 us -> 1.41 us  [the longest x4 1.15 us: per_device(): other = [lax.ppermute(part, 'rep', swap) for part in mine]]
    ppermute x13 -> x10, waiting for transfers between devices: 31.2 us -> 29.3 us  [toward(): return lax.ppermute(x, OWNERS, [(i, i ^ flip) for i in range(owners)])]
    unnamed x4 -> x8, local copies, waits for them, and re-layouts: 1.14 us -> 2.93 us
    ppermute x4 -> x7, waiting for transfers between devices: 11 us -> 12.3 us  [the longest x2 9.92 us: per_device(): tile = lax.ppermute(keep + lax.ppermute(give, 'rep', swap), 'clus', across)]
    ppermute x13 -> x10, starting transfers between devices: 22.8 us -> 21.9 us  [toward(): return lax.ppermute(x, OWNERS, [(i, i ^ flip) for i in range(owners)])]
    pallas_call x6 -> x9, Pallas kernels: 5.7 us -> 6.22 us  [call(): pl.pallas_call(kernel, out_shape=out_shape, in_specs=[spec] * count + [pl...]
  transfers between devices with their start and end apart: 17 -> 17, of which waited for: 9 -> 13; matrix products, arithmetic and copies ran while one was open for 1% -> 0% of each run, Pallas kernels for 4% -> 4%
where the time goes in v2:
time: 74.8 us; the launch traced here: 74.6 us
  waiting for transfers between devices  41.6 us (56%)
  starting transfers between devices  23.3 us (31%)
  Pallas kernels  6.22 us (8%)
  local copies, waits for them, and re-layouts  3.21 us (4%)
    ppermute x10, waiting for transfers between devices, toward(): return lax.ppermute(x, OWNERS, [(i, i ^ flip) for i in range(owners)])  29.3 us
    ppermute x10, starting transfers between devices, toward(): return lax.ppermute(x, OWNERS, [(i, i ^ flip) for i in range(owners)])  21.9 us
    ppermute x2, waiting for transfers between devices, per_device(): tile = lax.ppermute(keep + lax.ppermute(give, 'rep', swap), 'clus', across)  9.92 us
    pallas_call x9, Pallas kernels, call(): pl.pallas_call(kernel, out_shape=out_shape, in_specs=[spec] * count + [pl...  6.22 us
    unnamed x8, local copies, waits for them, and re-layouts  2.93 us
  transfers between devices with their start and end apart: 17, of which 13 were waited for; matrix products, arithmetic and copies ran while one was open for 0% of the time, Pallas kernels for 4%

profile of v2, /device:TPU:0, one launch (start us, length us, event | category | flops | bytes accessed | tf_op | source)
XLA Modules:
  0.0 74.6 jit_solution(18023645159007044724)
XLA Ops:
  0.0 0.0 copy-start.1
  0.0 0.7 copy-done.1
  0.7 0.0 copy-start
  0.7 0.2 shard_map.46.refs_1_
  0.9 0.4 copy-done
  1.4 0.0 copy-start.2
  1.4 1.1 %copy-done.2 = bf16[512,768]{1,0:T(8,128)(2,1)S(1)} copy-done((bf16[512,768]{1,0:T(8,128)(2,1)S(1)}, bf16[512,768]{1,0:T(8,128)(2,1)}, u32[]{:S(2)}) %copy-start.2) | copy-done | bytes 786456
  2.5 1.1 %shard_map.47 = (bf16[512,768]{1,0:T(8,128)(2,1)S(1)}, bf16[128,768]{1,0:T(8,128)(2,1)S(1)}, bf16[128,768]{1,0:T(8,128)(2,1)S(1)}, bf16[136,768]{1,0:T(8,128)(2,...) custom-call(bf16[512,768]{1,0:T(8,128)(2,1)S(1)} %copy-done.2, s32[1,512]{1,0:T(1,128)S(1)} %shard_map.46.refs_1_, ...), custom_call_target="tpu_custom_call" | custom-call | flops 402653184 | bytes 2584576 | tf_op jit(solution)/shard_map/pallas_call | solution.py:40
  3.6 4.0 %collective-permute-start.2 = (bf16[128,768]{1,0:T(8,128)(2,1)S(1)}, bf16[128,768]{1,0:T(8,128)(2,1)S(1)}, u32[]{:S(2)}, u32[]{:S(2)}) collective-permute-start(bf16[128,768]{1,0:T(8,128)(2,1)S(1)} %get-tuple-element.25), channel_id=1, source_target_pairs={{0,6},{2,4},{4,2},{6,0},{8,14},{10,12},{12,10},{14,8},{1,7},{3,5},... | collective-permute-start | bytes 589832 | tf_op jit(solution)/shard_map/ppermute | solution.py:210
  7.6 2.5 %collective-permute-start.5 = (bf16[128,768]{1,0:T(8,128)(2,1)S(1)}, bf16[128,768]{1,0:T(8,128)(2,1)S(1)}, u32[]{:S(2)}, u32[]{:S(2)}) collective-permute-start(bf16[128,768]{1,0:T(8,128)(2,1)S(1)} %get-tuple-element.27), channel_id=1, source_target_pairs={{0,12},{2,14},{4,8},{6,10},{8,4},{10,6},{12,0},{14,2},{1,13},{3,15... | collective-permute-start | bytes 589832 | tf_op jit(solution)/shard_map/ppermute | solution.py:210
  10.1 1.3 %collective-permute-start.6 = (bf16[128,768]{1,0:T(8,128)(2,1)S(1)}, bf16[128,768]{1,0:T(8,128)(2,1)S(1)}, u32[]{:S(2)}, u32[]{:S(2)}) collective-permute-start(bf16[128,768]{1,0:T(8,128)(2,1)S(1)} %get-tuple-element.28), channel_id=1, source_target_pairs={{0,14},{2,12},{4,10},{6,8},{8,6},{10,4},{12,2},{14,0},{1,15},{3,13... | collective-permute-start | bytes 589832 | tf_op jit(solution)/shard_map/ppermute | solution.py:210
  11.4 1.5 %collective-permute-start = (bf16[136,768]{1,0:T(8,128)(2,1)S(1)}, bf16[136,768]{1,0:T(8,128)(2,1)S(1)}, u32[]{:S(2)}, u32[]{:S(2)}) collective-permute-start(bf16[136,768]{1,0:T(8,128)(2,1)S(1)} %get-tuple-element.22), channel_id=1, source_target_pairs={{0,2},{2,0},{4,6},{6,4},{8,10},{10,8},{12,14},{14,12},{1,3},{3,1},... | collective-permute-start | bytes 626696 | tf_op jit(solution)/shard_map/ppermute | solution.py:210
  12.9 0.0 copy-start.3
  12.9 0.7 copy-done.3
  13.6 0.1 copy.11
  13.7 3.7 %collective-permute-done.refs_3_.refs_1_ = bf16[136,768]{1,0:T(8,128)(2,1)S(1)} collective-permute-done((bf16[136,768]{1,0:T(8,128)(2,1)S(1)}, bf16[136,768]{1,0:T(8,128)(2,1)S(1)}, u32[]{:S(2)}, u32[]{:S(2)}) %collective-permute-start) | collective-permute-done | bytes 208928 | tf_op jit(solution)/shard_map/ppermute | solution.py:210
  17.4 0.4 shard_map.48
  17.9 1.9 %collective-permute-start.1 = (bf16[136,768]{1,0:T(8,128)(2,1)S(1)}, bf16[136,768]{1,0:T(8,128)(2,1)S(1)}, u32[]{:S(2)}, u32[]{:S(2)}) collective-permute-start(bf16[136,768]{1,0:T(8,128)(2,1)S(1)} %get-tuple-element.24), channel_id=1, source_target_pairs={{0,4},{2,6},{4,0},{6,2},{8,12},{10,14},{12,8},{14,10},{1,5},{3,7},... | collective-permute-start | bytes 626696 | tf_op jit(solution)/shard_map/ppermute | solution.py:210
  19.8 0.1 copy.10
  19.9 7.4 %collective-permute-start.4 = (bf16[128,768]{1,0:T(8,128)(2,1)S(1)}, bf16[128,768]{1,0:T(8,128)(2,1)S(1)}, u32[]{:S(2)}, u32[]{:S(2)}) collective-permute-start(bf16[128,768]{1,0:T(8,128)(2,1)S(1)} %get-tuple-element.26), channel_id=1, source_target_pairs={{0,10},{2,8},{4,14},{6,12},{8,2},{10,0},{12,6},{14,4},{1,11},{3,9}... | collective-permute-start | bytes 589832 | tf_op jit(solution)/shard_map/ppermute | solution.py:210
  27.3 0.4 collective-permute-done.1.refs_4_.refs_2_
  27.7 0.3 shard_map.49
  28.0 2.7 %collective-permute-start.3 = (bf16[136,768]{1,0:T(8,128)(2,1)S(1)}, bf16[136,768]{1,0:T(8,128)(2,1)S(1)}, u32[]{:S(2)}, u32[]{:S(2)}) collective-permute-start(bf16[136,768]{1,0:T(8,128)(2,1)S(1)} %shard_map.49), channel_id=1, source_target_pairs={{0,8},{2,10},{4,12},{6,14},{8,0},{10,2},{12,4},{14,6},{1,9},{3,11}... | collective-permute-start | bytes 626696 | tf_op jit(solution)/shard_map/ppermute | solution.py:210
  30.7 0.0 collective-permute-done.2.refs_3_
  30.7 0.0 collective-permute-done.5.refs_6_
  30.7 0.0 collective-permute-done.6.refs_7_
  30.8 10.7 %collective-permute-done.4.refs_5_ = bf16[128,768]{1,0:T(8,128)(2,1)S(1)} collective-permute-done((bf16[128,768]{1,0:T(8,128)(2,1)S(1)}, bf16[128,768]{1,0:T(8,128)(2,1)S(1)}, u32[]{:S(2)}, u32[]{:S(2)}) %collective-permute-start.4) | collective-permute-done | bytes 196640 | tf_op jit(solution)/shard_map/ppermute | solution.py:210
  41.5 3.4 %collective-permute-done.3.refs_4_ = bf16[136,768]{1,0:T(8,128)(2,1)S(1)} collective-permute-done((bf16[136,768]{1,0:T(8,128)(2,1)S(1)}, bf16[136,768]{1,0:T(8,128)(2,1)S(1)}, u32[]{:S(2)}, u32[]{:S(2)}) %collective-permute-start.3) | collective-permute-done | bytes 208928 | tf_op jit(solution)/shard_map/ppermute | solution.py:210
  44.8 0.6 shard_map.50
  45.5 0.1 collective-permute-start.11
  45.5 1.0 %shard_map.51 = (bf16[128,768]{1,0:T(8,128)(2,1)S(1)}, bf16[128,768]{1,0:T(8,128)(2,1)S(1)}, bf16[128,768]{1,0:T(8,128)(2,1)S(1)}, bf16[128,768]{1,0:T(8,128)(2,1)S(1)}) custom-call(bf16[136,768]{1,0:T(8,128)(2,1)S(1)} %get-tuple-element.21.refs_0_, bf16[136,768]{1,0:T(8,128)(2,1)S(1)} %collective-permute-done.refs_3_.refs_1_, ...), custom_call_target="tpu_custom_call" | custom-call | flops 805306368 | bytes 2408448 | tf_op jit(solution)/shard_map/pallas_call | solution.py:40
  46.6 0.6 collective-permute-start.7
  47.1 0.1 collective-permute-start.8
  47.2 0.4 collective-permute-start.9
  47.6 0.1 collective-permute-start.10
  47.7 0.0 collective-permute-done.11
  47.7 0.1 add.10
  47.8 0.1 collective-permute-start.12
  47.8 0.3 collective-permute-done.7.refs_4_
  48.2 0.4 collective-permute-done.8.refs_5_
  48.6 0.3 collective-permute-done.9.refs_6_
  48.8 0.3 collective-permute-done.10.refs_7_
  49.1 1.1 %shard_map.52.refs_9_ = f32[1,512]{1,0:T(1,128)S(1)} custom-call(bf16[128,768]{1,0:T(8,128)(2,1)S(1)} %get-tuple-element.30.refs_0_, bf16[128,768]{1,0:T(8,128)(2,1)S(1)} %get-tuple-element.31.refs_1_, bf16[128,768]{1,0:T(8,128)(2,1)S(1)} %get-tuple-element.32.refs_2_, bf16[128,768]{1,0:T(8,128)(2,1)S(1)} %get-tuple-element.33.refs_3_, ...), custom_call_target="tpu_custom_call" | custom-call | flops 805306368 | bytes 1574912 | tf_op jit(solution)/shard_map/pallas_call | solution.py:40
  50.3 9.9 %collective-permute-done.12.refs_8_ = bf16[128,768]{1,0:T(8,128)(2,1)S(1)} collective-permute-done((bf16[128,768]{1,0:T(8,128)(2,1)S(1)}, bf16[128,768]{1,0:T(8,128)(2,1)S(1)}, u32[]{:S(2)}, u32[]{:S(2)}) %collective-permute-start.12) | collective-permute-done | bytes 196640 | tf_op jit(solution)/shard_map/ppermute | solution.py:293
  60.2 0.7 shard_map.53
  60.9 0.1 collective-permute-start.13
  61.0 1.1 %collective-permute-done.13 = f32[4,128]{1,0:T(4,128)S(1)} collective-permute-done((f32[4,128]{1,0:T(4,128)S(1)}, f32[4,128]{1,0:T(4,128)S(1)}, u32[]{:S(2)}, u32[]{:S(2)}) %collective-permute-start.13) | collective-permute-done | bytes 2080 | tf_op jit(solution)/shard_map/ppermute | solution.py:321
  62.1 0.5 collective-permute-start.14
  62.6 3.1 %collective-permute-done.14 = f32[4,128]{1,0:T(4,128)S(1)} collective-permute-done((f32[4,128]{1,0:T(4,128)S(1)}, f32[4,128]{1,0:T(4,128)S(1)}, u32[]{:S(2)}, u32[]{:S(2)}) %collective-permute-start.14) | collective-permute-done | bytes 2080 | tf_op jit(solution)/shard_map/ppermute | solution.py:210
  65.7 0.0 collective-permute-start.15
  65.7 3.6 %collective-permute-done.15 = f32[8,128]{1,0:T(8,128)S(1)} collective-permute-done((f32[8,128]{1,0:T(8,128)S(1)}, f32[8,128]{1,0:T(8,128)S(1)}, u32[]{:S(2)}, u32[]{:S(2)}) %collective-permute-start.15) | collective-permute-done | bytes 4128 | tf_op jit(solution)/shard_map/ppermute | solution.py:210
  69.3 0.1 collective-permute-start.16
  69.4 4.5 %collective-permute-done.16 = f32[16,128]{1,0:T(8,128)S(1)} collective-permute-done((f32[16,128]{1,0:T(8,128)S(1)}, f32[16,128]{1,0:T(8,128)S(1)}, u32[]{:S(2)}, u32[]{:S(2)}) %collective-permute-start.16) | collective-permute-done | bytes 8224 | tf_op jit(solution)/shard_map/ppermute | solution.py:210
  73.9 0.7 shard_map.54
  (9 shorter events, 0.1 us)
Async XLA Ops:
  0.0 0.7 copy-start.1
  0.7 0.7 copy-start
  1.4 1.1 %copy-start.2 = (bf16[512,768]{1,0:T(8,128)(2,1)S(1)}, bf16[512,768]{1,0:T(8,128)(2,1)}, u32[]{:S(2)}) copy-start(bf16[512,768]{1,0:T(8,128)(2,1)} %refs_0_.1) | copy-start | bytes 2359300
  3.6 27.2 %collective-permute-start.2 = (bf16[128,768]{1,0:T(8,128)(2,1)S(1)}, bf16[128,768]{1,0:T(8,128)(2,1)S(1)}, u32[]{:S(2)}, u32[]{:S(2)}) collective-permute-start(bf16[128,768]{1,0:T(8,128)(2,1)S(1)} %get-tuple-element.25), channel_id=1, source_target_pairs={{0,6},{2,4},{4,2},{6,0},{8,14},{10,12},{12,10},{14,8},{1,7},{3,5},... | collective-permute-start | bytes 589832 | tf_op jit(solution)/shard_map/ppermute | solution.py:210
  7.6 23.2 %collective-permute-start.5 = (bf16[128,768]{1,0:T(8,128)(2,1)S(1)}, bf16[128,768]{1,0:T(8,128)(2,1)S(1)}, u32[]{:S(2)}, u32[]{:S(2)}) collective-permute-start(bf16[128,768]{1,0:T(8,128)(2,1)S(1)} %get-tuple-element.27), channel_id=1, source_target_pairs={{0,12},{2,14},{4,8},{6,10},{8,4},{10,6},{12,0},{14,2},{1,13},{3,15... | collective-permute-start | bytes 589832 | tf_op jit(solution)/shard_map/ppermute | solution.py:210
  10.1 20.7 %collective-permute-start.6 = (bf16[128,768]{1,0:T(8,128)(2,1)S(1)}, bf16[128,768]{1,0:T(8,128)(2,1)S(1)}, u32[]{:S(2)}, u32[]{:S(2)}) collective-permute-start(bf16[128,768]{1,0:T(8,128)(2,1)S(1)} %get-tuple-element.28), channel_id=1, source_target_pairs={{0,14},{2,12},{4,10},{6,8},{8,6},{10,4},{12,2},{14,0},{1,15},{3,13... | collective-permute-start | bytes 589832 | tf_op jit(solution)/shard_map/ppermute | solution.py:210
  11.4 6.1 %collective-permute-start = (bf16[136,768]{1,0:T(8,128)(2,1)S(1)}, bf16[136,768]{1,0:T(8,128)(2,1)S(1)}, u32[]{:S(2)}, u32[]{:S(2)}) collective-permute-start(bf16[136,768]{1,0:T(8,128)(2,1)S(1)} %get-tuple-element.22), channel_id=1, source_target_pairs={{0,2},{2,0},{4,6},{6,4},{8,10},{10,8},{12,14},{14,12},{1,3},{3,1},... | collective-permute-start | bytes 626696 | tf_op jit(solution)/shard_map/ppermute | solution.py:210
  12.9 0.7 copy-start.3
  17.9 9.8 %collective-permute-start.1 = (bf16[136,768]{1,0:T(8,128)(2,1)S(1)}, bf16[136,768]{1,0:T(8,128)(2,1)S(1)}, u32[]{:S(2)}, u32[]{:S(2)}) collective-permute-start(bf16[136,768]{1,0:T(8,128)(2,1)S(1)} %get-tuple-element.24), channel_id=1, source_target_pairs={{0,4},{2,6},{4,0},{6,2},{8,12},{10,14},{12,8},{14,10},{1,5},{3,7},... | collective-permute-start | bytes 626696 | tf_op jit(solution)/shard_map/ppermute | solution.py:210
  19.9 21.5 %collective-permute-start.4 = (bf16[128,768]{1,0:T(8,128)(2,1)S(1)}, bf16[128,768]{1,0:T(8,128)(2,1)S(1)}, u32[]{:S(2)}, u32[]{:S(2)}) collective-permute-start(bf16[128,768]{1,0:T(8,128)(2,1)S(1)} %get-tuple-element.26), channel_id=1, source_target_pairs={{0,10},{2,8},{4,14},{6,12},{8,2},{10,0},{12,6},{14,4},{1,11},{3,9}... | collective-permute-start | bytes 589832 | tf_op jit(solution)/shard_map/ppermute | solution.py:210
  28.0 16.8 %collective-permute-start.3 = (bf16[136,768]{1,0:T(8,128)(2,1)S(1)}, bf16[136,768]{1,0:T(8,128)(2,1)S(1)}, u32[]{:S(2)}, u32[]{:S(2)}) collective-permute-start(bf16[136,768]{1,0:T(8,128)(2,1)S(1)} %shard_map.49), channel_id=1, source_target_pairs={{0,8},{2,10},{4,12},{6,14},{8,0},{10,2},{12,4},{14,6},{1,9},{3,11}... | collective-permute-start | bytes 626696 | tf_op jit(solution)/shard_map/ppermute | solution.py:210
  45.5 2.2 %collective-permute-start.11 = (bf16[128,768]{1,0:T(8,128)(2,1)S(1)}, bf16[128,768]{1,0:T(8,128)(2,1)S(1)}, u32[]{:S(2)}, u32[]{:S(2)}) collective-permute-start(bf16[128,768]{1,0:T(8,128)(2,1)S(1)} %get-tuple-element.29.refs_8_), channel_id=1, source_target_pairs={{0,1},{1,0},{2,3},{3,2},{4,5},{5,4},{6,7},{7,6},{8,9},{9,8},{10,11... | collective-permute-start | bytes 589832 | tf_op jit(solution)/shard_map/ppermute | solution.py:293
  46.6 1.6 %collective-permute-start.7 = (bf16[128,768]{1,0:T(8,128)(2,1)S(1)}, bf16[128,768]{1,0:T(8,128)(2,1)S(1)}, u32[]{:S(2)}, u32[]{:S(2)}) collective-permute-start(bf16[128,768]{1,0:T(8,128)(2,1)S(1)} %get-tuple-element.30.refs_0_), channel_id=1, source_target_pairs={{0,1},{1,0},{2,3},{3,2},{4,5},{5,4},{6,7},{7,6},{8,9},{9,8},{10,11... | collective-permute-start | bytes 589832 | tf_op jit(solution)/shard_map/ppermute | solution.py:303
  47.1 1.4 %collective-permute-start.8 = (bf16[128,768]{1,0:T(8,128)(2,1)S(1)}, bf16[128,768]{1,0:T(8,128)(2,1)S(1)}, u32[]{:S(2)}, u32[]{:S(2)}) collective-permute-start(bf16[128,768]{1,0:T(8,128)(2,1)S(1)} %get-tuple-element.31.refs_1_), channel_id=1, source_target_pairs={{0,1},{1,0},{2,3},{3,2},{4,5},{5,4},{6,7},{7,6},{8,9},{9,8},{10,11... | collective-permute-start | bytes 589832 | tf_op jit(solution)/shard_map/ppermute | solution.py:303
  47.2 1.6 %collective-permute-start.9 = (bf16[128,768]{1,0:T(8,128)(2,1)S(1)}, bf16[128,768]{1,0:T(8,128)(2,1)S(1)}, u32[]{:S(2)}, u32[]{:S(2)}) collective-permute-start(bf16[128,768]{1,0:T(8,128)(2,1)S(1)} %get-tuple-element.32.refs_2_), channel_id=1, source_target_pairs={{0,1},{1,0},{2,3},{3,2},{4,5},{5,4},{6,7},{7,6},{8,9},{9,8},{10,11... | collective-permute-start | bytes 589832 | tf_op jit(solution)/shard_map/ppermute | solution.py:303
  47.6 1.5 %collective-permute-start.10 = (bf16[128,768]{1,0:T(8,128)(2,1)S(1)}, bf16[128,768]{1,0:T(8,128)(2,1)S(1)}, u32[]{:S(2)}, u32[]{:S(2)}) collective-permute-start(bf16[128,768]{1,0:T(8,128)(2,1)S(1)} %get-tuple-element.33.refs_3_), channel_id=1, source_target_pairs={{0,1},{1,0},{2,3},{3,2},{4,5},{5,4},{6,7},{7,6},{8,9},{9,8},{10,11... | collective-permute-start | bytes 589832 | tf_op jit(solution)/shard_map/ppermute | solution.py:303
  47.8 12.4 %collective-permute-start.12 = (bf16[128,768]{1,0:T(8,128)(2,1)S(1)}, bf16[128,768]{1,0:T(8,128)(2,1)S(1)}, u32[]{:S(2)}, u32[]{:S(2)}) collective-permute-start(bf16[128,768]{1,0:T(8,128)(2,1)S(1)} %add.10), channel_id=1, source_target_pairs={{0,8},{4,12},{8,0},{12,4},{1,9},{5,13},{9,1},{13,5},{2,10},{6,14},... | collective-permute-start | bytes 589832 | tf_op jit(solution)/shard_map/ppermute | solution.py:293
  60.9 1.2 %collective-permute-start.13 = (f32[4,128]{1,0:T(4,128)S(1)}, f32[4,128]{1,0:T(4,128)S(1)}, u32[]{:S(2)}, u32[]{:S(2)}) collective-permute-start(f32[4,128]{1,0:T(4,128)S(1)} %get-tuple-element.36), channel_id=1, source_target_pairs={{0,1},{1,0},{2,3},{3,2},{4,5},{5,4},{6,7},{7,6},{8,9},{9,8},{10,11... | collective-permute-start | bytes 6152 | tf_op jit(solution)/shard_map/ppermute | solution.py:321
  62.1 3.6 %collective-permute-start.14 = (f32[4,128]{1,0:T(4,128)S(1)}, f32[4,128]{1,0:T(4,128)S(1)}, u32[]{:S(2)}, u32[]{:S(2)}) collective-permute-start(f32[4,128]{1,0:T(4,128)S(1)} %log_negate_fusion), channel_id=1, source_target_pairs={{0,2},{2,0},{4,6},{6,4},{8,10},{10,8},{12,14},{14,12},{1,3},{3,1},... | collective-permute-start | bytes 6152 | tf_op jit(solution)/shard_map/ppermute | solution.py:210
  65.7 3.6 %collective-permute-start.15 = (f32[8,128]{1,0:T(8,128)S(1)}, f32[8,128]{1,0:T(8,128)S(1)}, u32[]{:S(2)}, u32[]{:S(2)}) collective-permute-start(f32[8,128]{1,0:T(8,128)S(1)} %pad_maximum_fusion.2), channel_id=1, source_target_pairs={{0,4},{2,6},{4,0},{6,2},{8,12},{10,14},{12,8},{14,10},{1,5},{3,7},... | collective-permute-start | bytes 12296 | tf_op jit(solution)/shard_map/ppermute | solution.py:210
  69.3 4.6 %collective-permute-start.16 = (f32[16,128]{1,0:T(8,128)S(1)}, f32[16,128]{1,0:T(8,128)S(1)}, u32[]{:S(2)}, u32[]{:S(2)}) collective-permute-start(f32[16,128]{1,0:T(8,128)S(1)} %pad_maximum_fusion.1), channel_id=1, source_target_pairs={{0,8},{2,10},{4,12},{6,14},{8,0},{10,2},{12,4},{14,6},{1,9},{3,11}... | collective-permute-start | bytes 24584 | tf_op jit(solution)/shard_map/ppermute | solution.py:210

commit v3 on v2

--- a/solution.py
+++ b/solution.py
@@ -57,18 +57,19 @@
 
 TAGS = {
     0: ((0,), ()),
-    1: ((1, 3, 5, 7), ()),
-    2: ((2, 6), ((1, 1), (1, 3))),
-    4: ((4,), ((1, 2), (2, 1), (2, 3))),
+    1: ((1, 3, 6, 4), ()),
+    2: ((2, 5), ((1, 1), (1, 3))),
+    7: ((7,), ((1, 2), (2, 1), (2, 3))),
 }
-TAG_LINE = ((0, 0), (1, 0), (2, 0), (2, 2), (4, 0), (4, 1), (4, 2), (4, 3))
-STEPS = (((7, 6, 1, 3, 0), ()), ((2, 5), (1,)), ((4,), (1, 2)))
+TAG_LINE = ((0, 0), (1, 0), (2, 0), (2, 2), (7, 3), (7, 2), (7, 1), (7, 0))
+STEPS = (((6, 4), ()), ((1, 0), ()), ((2, 5), (1,)), ((7, 3), (1, 2)))
 
 
 def pack(send, blocks, unit, place, position, arrived, outs):
     rows, width = unit.shape
-    parts = jnp.where(iota((16, rows), 0) == 0, position // TAG_BASE, position % TAG_BASE)
-    parts = parts.astype(jnp.float32).astype(jnp.bfloat16)
+    if position is not None:
+        parts = jnp.where(iota((16, rows), 0) == 0, position // TAG_BASE, position % TAG_BASE)
+        parts = parts.astype(jnp.float32).astype(jnp.bfloat16)
 
     def chosen(block):
         return one_hot(iota((send, rows), 0) + block * send == place)
@@ -90,28 +91,27 @@
             out[send:, :] = jnp.concatenate([lines, rest], axis=1).astype(jnp.bfloat16)
 
 
-def rank_body(owners, send, cluster_ref, base_ref, place_ref):
+def unit_body(embeds_ref, unit_ref):
+    values = embeds_ref[...].astype(jnp.float32)
+    mean = jnp.sum(values * values, axis=1, keepdims=True) / values.shape[1]
+    unit_ref[...] = (values * lax.rsqrt(mean + EPS)).astype(jnp.bfloat16)
+
+
+def first_body(owners, send, blocks, unit_ref, cluster_ref, base_ref, place_ref, *outs):
     rows = cluster_ref.shape[1]
     owner = cluster_ref[...] ^ base_ref[...]
     which = iota((max(owners, 16), rows), 0) == owner
     before = one_hot(iota((rows, rows), 0) < iota((rows, rows), 1))
     counts = dot(one_hot(which), before)
     rank = jnp.sum(jnp.where(which, counts, 0.0), axis=0, keepdims=True)
-    place_ref[...] = owner * send + rank.astype(jnp.int32)
-
-
-def first_body(send, blocks, embeds_ref, place_ref, order_ref, unit_ref, *outs):
-    values = embeds_ref[...].astype(jnp.float32)
-    mean = jnp.sum(values * values, axis=1, keepdims=True) / values.shape[1]
-    unit = (values * lax.rsqrt(mean + EPS)).astype(jnp.bfloat16)
-    unit_ref[...] = unit
-    place = place_ref[...]
+    place = owner * send + rank.astype(jnp.int32)
+    place_ref[...] = place
     if blocks:
-        pack(send, blocks, unit, place, order_ref[...] % HALF + 1, {}, outs)
+        pack(send, blocks, unit_ref[...], place, None, {}, outs)
     else:
         (out,) = outs
-        chosen = one_hot(iota((out.shape[0], place.shape[1]), 0) == place)
-        out[...] = dot(chosen, unit).astype(jnp.bfloat16)
+        chosen = one_hot(iota((out.shape[0], rows), 0) == place)
+        out[...] = dot(chosen, unit_ref[...]).astype(jnp.bfloat16)
 
 
 def pack_body(send, blocks, unit_ref, place_ref, order_ref, arrived, *outs):
@@ -209,12 +209,22 @@
     def toward(x, flip):
         return lax.ppermute(x, OWNERS, [(i, i ^ flip) for i in range(owners)])
 
+    def across(x, flip):
+        pairs = [(2 * i + r, 2 * (i ^ flip) + 1 - r) for i in range(owners) for r in range(2)]
+        return lax.ppermute(x, (*OWNERS, "rep"), pairs)
+
     def gather(x):
+        return lax.all_gather(x, OWNERS, axis=0, tiled=True)
+
+    def gather_halves(mine, other):
         if not paired:
-            return lax.all_gather(x, OWNERS, axis=0, tiled=True)
+            return gather(mine)
         for flip in (1, 2, 4):
-            x = jnp.concatenate([x, toward(x, flip)], axis=0)
-        return x
+            arrived = across(jnp.concatenate([other, mine]) if flip < 4 else other, flip)
+            mine = jnp.concatenate([mine, arrived[: mine.shape[0]]])
+            if flip < 4:
+                other = jnp.concatenate([other, arrived[other.shape[0] :]])
+        return mine
 
     base = me if paired else jnp.zeros_like(me)
     base = base.reshape(1, 1)
@@ -225,29 +235,23 @@
         sizes = [(send + TAG_ROWS * (b in TAGS), width) for b in blocks] or [(owners * send, width)]
         return [jax.ShapeDtypeStruct(size, jnp.bfloat16) for size in sizes]
 
-    place = call(
-        functools.partial(rank_body, owners, send),
-        jax.ShapeDtypeStruct((1, rows), jnp.int32),
-        2 * owners * rows * rows,
-        cluster_row,
-        base,
-    )
+    unit = call(unit_body, jax.ShapeDtypeStruct((rows, width), jnp.bfloat16), 0, embeds)
 
     def first(blocks):
         return call(
-            functools.partial(first_body, send, blocks),
-            [jax.ShapeDtypeStruct((rows, width), jnp.bfloat16), *shapes(blocks)],
+            functools.partial(first_body, owners, send, blocks),
+            [jax.ShapeDtypeStruct((1, rows), jnp.int32), *shapes(blocks)],
             2 * rows * rows * width,
-            embeds,
-            place,
-            order_row,
+            unit,
+            cluster_row,
+            base,
         )
 
     if paired:
         chunks = {}
         for blocks, needed in STEPS:
             if not chunks:
-                unit, *packed = first(blocks)
+                place, *packed = first(blocks)
             else:
                 handed = {k: chunks[k] for k in needed}
                 packed = call(
@@ -280,7 +284,9 @@
     want = border_idx.reshape(BORDER, 1) - side * HALF
     want = jnp.where(side == 0, want, jnp.roll(want, BORDER // 2, axis=0))
     by = clus_count // 2
-    across = [(i, (i + by) % clus_count) for i in range(clus_count)]
+    opposite = [
+        (2 * i + r, 2 * ((i + by) % clus_count) + 1 - r) for i in range(clus_count) for r in range(2)
+    ]
     part = jax.ShapeDtypeStruct((BORDER // 2, width), jnp.bfloat16)
     keep, give = call(
         functools.partial(border_body, send),
@@ -290,7 +296,7 @@
         want,
         tags,
     )
-    tile = lax.ppermute(keep + lax.ppermute(give, "rep", swap), "clus", across)
+    tile = lax.ppermute(keep + lax.ppermute(give, "rep", swap), ("clus", "rep"), opposite)
     part = jax.ShapeDtypeStruct((HALF // PIECES, width), jnp.bfloat16)
     mine = call(
         functools.partial(place_body, send),
@@ -318,13 +324,15 @@
         tile,
         near,
     )
-    total = here + lax.ppermute(there, "rep", swap)
-    scores = -jnp.log(total / (CAP - 1 + BORDER))
+    swapped = lax.ppermute(jnp.concatenate([there, here]), "rep", swap)
+    totals = jnp.concatenate([here, there]) + swapped
+    scores = -jnp.log(totals / (CAP - 1 + BORDER))
+    lines = HALF // LANES
     answers = call(
         answer_body,
         jax.ShapeDtypeStruct((rows // LANES, LANES), jnp.float32),
         owners * HALF,
-        gather(scores),
+        gather_halves(scores[:lines], scores[lines:]),
         cluster_of.reshape(rows // LANES, LANES),
         order_in.reshape(rows // LANES, LANES),
         base,

time: 74.8 us -> 71.2 us (0.952)
  waiting for transfers between devices: 41.6 us -> 39.6 us
  starting transfers between devices: 23.3 us -> 21.9 us
    ppermute x10 -> x7, waiting for transfers between devices: 29.3 us -> 20.6 us  [toward(): return lax.ppermute(x, OWNERS, [(i, i ^ flip) for i in range(owners)])]
    ppermute x3 -> x6, waiting for transfers between devices: 11 us -> 18.9 us  [the longest x3 9.51 us: across(): return lax.ppermute(x, (*OWNERS, 'rep'), pairs)]
    ppermute x10 -> x7, starting transfers between devices: 21.9 us -> 15.7 us  [toward(): return lax.ppermute(x, OWNERS, [(i, i ^ flip) for i in range(owners)])]
    ppermute x3 -> x6, starting transfers between devices: 0.26 us -> 5.08 us  [the longest x1 4.06 us: per_device(): lax.ppermute(keep + lax.ppermute(give, 'rep', swap), ('clus', 'rep'), opp...]
    ppermute x4, waiting for transfers between devices: 1.27 us -> 0.01 us  [per_device(): other = [lax.ppermute(part, 'rep', swap) for part in mine]]
    pallas_call x9 -> x10, Pallas kernels: 6.22 us -> 6.4 us  [call(): pl.pallas_call(kernel, out_shape=out_shape, in_specs=[spec] * count + [pl...]
  transfers between devices with their start and end apart: 17 -> 17, of which waited for: 13 -> 9; matrix products, arithmetic and copies ran while one was open for 0% -> 0% of each run, Pallas kernels for 4% -> 5%
where the time goes in v3:
time: 71.2 us; the launch traced here: 71 us
  waiting for transfers between devices  39.6 us (56%)
  starting transfers between devices  21.9 us (31%)
  Pallas kernels  6.4 us (9%)
  local copies, waits for them, and re-layouts  2.78 us (4%)
    ppermute x7, waiting for transfers between devices, toward(): return lax.ppermute(x, OWNERS, [(i, i ^ flip) for i in range(owners)])  20.6 us
    ppermute x7, starting transfers between devices, toward(): return lax.ppermute(x, OWNERS, [(i, i ^ flip) for i in range(owners)])  15.7 us
    ppermute x3, waiting for transfers between devices, across(): return lax.ppermute(x, (*OWNERS, 'rep'), pairs)  9.51 us
    ppermute x1, waiting for transfers between devices, per_device(): lax.ppermute(keep + lax.ppermute(give, 'rep', swap), ('clus', 'rep'), opp...  8.37 us
    pallas_call x10, Pallas kernels, call(): pl.pallas_call(kernel, out_shape=out_shape, in_specs=[spec] * count + [pl...  6.4 us
    ppermute x1, starting transfers between devices, per_device(): lax.ppermute(keep + lax.ppermute(give, 'rep', swap), ('clus', 'rep'), opp...  4.06 us
    unnamed x8, local copies, waits for them, and re-layouts  2.49 us
  transfers between devices with their start and end apart: 17, of which 9 were waited for; matrix products, arithmetic and copies ran while one was open for 0% of the time, Pallas kernels for 5%

profile of v3, /device:TPU:0, one launch (start us, length us, event | category | flops | bytes accessed | tf_op | source)
XLA Modules:
  0.0 71.0 jit_solution(3906755748069730415)
XLA Ops:
  0.0 0.0 copy-start
  0.0 1.1 %copy-done = bf16[512,768]{1,0:T(8,128)(2,1)S(1)} copy-done((bf16[512,768]{1,0:T(8,128)(2,1)S(1)}, bf16[512,768]{1,0:T(8,128)(2,1)}, u32[]{:S(2)}) %copy-start) | copy-done | bytes 786456
  1.1 0.2 shard_map.46.refs_0_
  1.4 0.0 copy-start.2
  1.4 0.7 copy-done.2
  2.1 0.6 shard_map.47
  2.7 4.1 %collective-permute-start.3 = (bf16[128,768]{1,0:T(8,128)(2,1)S(1)}, bf16[128,768]{1,0:T(8,128)(2,1)S(1)}, u32[]{:S(2)}, u32[]{:S(2)}) collective-permute-start(bf16[128,768]{1,0:T(8,128)(2,1)S(1)} %get-tuple-element.27), channel_id=1, source_target_pairs={{0,8},{2,10},{4,12},{6,14},{8,0},{10,2},{12,4},{14,6},{1,9},{3,11}... | collective-permute-start | bytes 589832 | tf_op jit(solution)/shard_map/ppermute | solution.py:210
  6.8 0.0 copy-start.1
  6.8 1.3 %collective-permute-start.5 = (bf16[128,768]{1,0:T(8,128)(2,1)S(1)}, bf16[128,768]{1,0:T(8,128)(2,1)S(1)}, u32[]{:S(2)}, u32[]{:S(2)}) collective-permute-start(bf16[128,768]{1,0:T(8,128)(2,1)S(1)} %get-tuple-element.29), channel_id=1, source_target_pairs={{0,12},{2,14},{4,8},{6,10},{8,4},{10,6},{12,0},{14,2},{1,13},{3,15... | collective-permute-start | bytes 589832 | tf_op jit(solution)/shard_map/ppermute | solution.py:210
  8.1 0.0 copy-done.1
  8.1 0.5 shard_map.48
  8.7 1.6 %collective-permute-start = (bf16[136,768]{1,0:T(8,128)(2,1)S(1)}, bf16[136,768]{1,0:T(8,128)(2,1)S(1)}, u32[]{:S(2)}, u32[]{:S(2)}) collective-permute-start(bf16[136,768]{1,0:T(8,128)(2,1)S(1)} %get-tuple-element.24), channel_id=1, source_target_pairs={{0,2},{2,0},{4,6},{6,4},{8,10},{10,8},{12,14},{14,12},{1,3},{3,1},... | collective-permute-start | bytes 626696 | tf_op jit(solution)/shard_map/ppermute | solution.py:210
  10.2 0.0 copy-start.3
  10.2 0.7 copy-done.3
  10.9 0.1 copy.11
  11.1 4.0 %collective-permute-done.refs_3_.refs_1_ = bf16[136,768]{1,0:T(8,128)(2,1)S(1)} collective-permute-done((bf16[136,768]{1,0:T(8,128)(2,1)S(1)}, bf16[136,768]{1,0:T(8,128)(2,1)S(1)}, u32[]{:S(2)}, u32[]{:S(2)}) %collective-permute-start) | collective-permute-done | bytes 208928 | tf_op jit(solution)/shard_map/ppermute | solution.py:210
  15.1 0.4 shard_map.49
  15.6 1.2 %collective-permute-start.1 = (bf16[136,768]{1,0:T(8,128)(2,1)S(1)}, bf16[136,768]{1,0:T(8,128)(2,1)S(1)}, u32[]{:S(2)}, u32[]{:S(2)}) collective-permute-start(bf16[136,768]{1,0:T(8,128)(2,1)S(1)} %get-tuple-element.25), channel_id=1, source_target_pairs={{0,4},{2,6},{4,0},{6,2},{8,12},{10,14},{12,8},{14,10},{1,5},{3,7},... | collective-permute-start | bytes 626696 | tf_op jit(solution)/shard_map/ppermute | solution.py:210
  16.8 0.1 copy.10
  16.9 2.8 %collective-permute-start.4 = (bf16[128,768]{1,0:T(8,128)(2,1)S(1)}, bf16[128,768]{1,0:T(8,128)(2,1)S(1)}, u32[]{:S(2)}, u32[]{:S(2)}) collective-permute-start(bf16[128,768]{1,0:T(8,128)(2,1)S(1)} %get-tuple-element.28), channel_id=1, source_target_pairs={{0,10},{2,8},{4,14},{6,12},{8,2},{10,0},{12,6},{14,4},{1,11},{3,9}... | collective-permute-start | bytes 589832 | tf_op jit(solution)/shard_map/ppermute | solution.py:210
  19.8 4.8 %collective-permute-done.1.refs_4_.refs_2_ = bf16[136,768]{1,0:T(8,128)(2,1)S(1)} collective-permute-done((bf16[136,768]{1,0:T(8,128)(2,1)S(1)}, bf16[136,768]{1,0:T(8,128)(2,1)S(1)}, u32[]{:S(2)}, u32[]{:S(2)}) %collective-permute-start.1) | collective-permute-done | bytes 208928 | tf_op jit(solution)/shard_map/ppermute | solution.py:210
  24.6 0.4 shard_map.50
  25.0 1.0 %collective-permute-start.2 = (bf16[128,768]{1,0:T(8,128)(2,1)S(1)}, bf16[128,768]{1,0:T(8,128)(2,1)S(1)}, u32[]{:S(2)}, u32[]{:S(2)}) collective-permute-start(bf16[128,768]{1,0:T(8,128)(2,1)S(1)} %get-tuple-element.26), channel_id=1, source_target_pairs={{0,6},{2,4},{4,2},{6,0},{8,14},{10,12},{12,10},{14,8},{1,7},{3,5},... | collective-permute-start | bytes 589832 | tf_op jit(solution)/shard_map/ppermute | solution.py:210
  26.0 3.6 %collective-permute-start.6 = (bf16[136,768]{1,0:T(8,128)(2,1)S(1)}, bf16[136,768]{1,0:T(8,128)(2,1)S(1)}, u32[]{:S(2)}, u32[]{:S(2)}) collective-permute-start(bf16[136,768]{1,0:T(8,128)(2,1)S(1)} %get-tuple-element.30), channel_id=1, source_target_pairs={{0,14},{2,12},{4,10},{6,8},{8,6},{10,4},{12,2},{14,0},{1,15},{3,13... | collective-permute-start | bytes 626696 | tf_op jit(solution)/shard_map/ppermute | solution.py:210
  29.6 0.0 collective-permute-done.3.refs_4_
  29.6 0.0 collective-permute-done.5.refs_6_
  29.7 9.8 %collective-permute-done.4.refs_5_ = bf16[128,768]{1,0:T(8,128)(2,1)S(1)} collective-permute-done((bf16[128,768]{1,0:T(8,128)(2,1)S(1)}, bf16[128,768]{1,0:T(8,128)(2,1)S(1)}, u32[]{:S(2)}, u32[]{:S(2)}) %collective-permute-start.4) | collective-permute-done | bytes 196640 | tf_op jit(solution)/shard_map/ppermute | solution.py:210
  39.4 2.0 %collective-permute-done.2.refs_3_ = bf16[128,768]{1,0:T(8,128)(2,1)S(1)} collective-permute-done((bf16[128,768]{1,0:T(8,128)(2,1)S(1)}, bf16[128,768]{1,0:T(8,128)(2,1)S(1)}, u32[]{:S(2)}, u32[]{:S(2)}) %collective-permute-start.2) | collective-permute-done | bytes 196640 | tf_op jit(solution)/shard_map/ppermute | solution.py:210
  41.4 0.0 collective-permute-done.6.refs_7_
  41.4 0.6 shard_map.51
  42.1 0.1 collective-permute-start.11
  42.1 1.0 %shard_map.52 = (bf16[128,768]{1,0:T(8,128)(2,1)S(1)}, bf16[128,768]{1,0:T(8,128)(2,1)S(1)}, bf16[128,768]{1,0:T(8,128)(2,1)S(1)}, bf16[128,768]{1,0:T(8,128)(2,1)S(1)}) custom-call(bf16[136,768]{1,0:T(8,128)(2,1)S(1)} %get-tuple-element.23.refs_0_, bf16[136,768]{1,0:T(8,128)(2,1)S(1)} %collective-permute-done.refs_3_.refs_1_, ...), custom_call_target="tpu_custom_call" | custom-call | flops 805306368 | bytes 2408448 | tf_op jit(solution)/shard_map/pallas_call | solution.py:40
  43.2 0.6 collective-permute-start.7
  43.7 0.1 collective-permute-start.8
  43.8 0.4 collective-permute-start.9
  44.2 0.1 collective-permute-start.10
  44.3 0.0 collective-permute-done.11
  44.4 4.1 %collective-permute-start.12 = (bf16[128,768]{1,0:T(8,128)(2,1)S(1)}, bf16[128,768]{1,0:T(8,128)(2,1)S(1)}, u32[]{:S(2)}, u32[]{:S(2)}) collective-permute-start(bf16[128,768]{1,0:T(8,128)(2,1)S(1)} %add.10), channel_id=1, source_target_pairs={{0,9},{1,8},{4,13},{5,12},{8,1},{9,0},{12,5},{13,4},{2,11},{3,10},... | collective-permute-start | bytes 589832 | tf_op jit(solution)/shard_map/ppermute | solution.py:299
  48.4 0.0 collective-permute-done.7.refs_4_
  48.4 0.0 collective-permute-done.8.refs_5_
  48.4 0.0 collective-permute-done.9.refs_6_
  48.4 0.0 collective-permute-done.10.refs_7_
  48.4 1.1 %shard_map.53.refs_9_ = f32[1,512]{1,0:T(1,128)S(1)} custom-call(bf16[128,768]{1,0:T(8,128)(2,1)S(1)} %get-tuple-element.32.refs_0_, bf16[128,768]{1,0:T(8,128)(2,1)S(1)} %get-tuple-element.33.refs_1_, bf16[128,768]{1,0:T(8,128)(2,1)S(1)} %get-tuple-element.34.refs_2_, bf16[128,768]{1,0:T(8,128)(2,1)S(1)} %get-tuple-element.35.refs_3_, ...), custom_call_target="tpu_custom_call" | custom-call | flops 805306368 | bytes 1574912 | tf_op jit(solution)/shard_map/pallas_call | solution.py:40
  49.6 8.4 %collective-permute-done.12.refs_8_ = bf16[128,768]{1,0:T(8,128)(2,1)S(1)} collective-permute-done((bf16[128,768]{1,0:T(8,128)(2,1)S(1)}, bf16[128,768]{1,0:T(8,128)(2,1)S(1)}, u32[]{:S(2)}, u32[]{:S(2)}) %collective-permute-start.12) | collective-permute-done | bytes 196640 | tf_op jit(solution)/shard_map/ppermute | solution.py:299
  58.0 0.7 shard_map.54
  58.7 0.2 collective-permute-start.13
  58.8 1.1 %collective-permute-done.13 = f32[8,128]{1,0:T(8,128)S(1)} collective-permute-done((f32[8,128]{1,0:T(8,128)S(1)}, f32[8,128]{1,0:T(8,128)S(1)}, u32[]{:S(2)}, u32[]{:S(2)}) %collective-permute-start.13) | collective-permute-done | bytes 4128 | tf_op jit(solution)/shard_map/ppermute | solution.py:327
  59.9 0.2 collective-permute-start.14
  60.2 2.9 %collective-permute-done.14 = f32[8,128]{1,0:T(8,128)S(1)} collective-permute-done((f32[8,128]{1,0:T(8,128)S(1)}, f32[8,128]{1,0:T(8,128)S(1)}, u32[]{:S(2)}, u32[]{:S(2)}) %collective-permute-start.14) | collective-permute-done | bytes 4128 | tf_op jit(solution)/shard_map/ppermute | solution.py:214
  63.0 0.1 collective-permute-start.15
  63.1 3.1 %collective-permute-done.15 = f32[16,128]{1,0:T(8,128)S(1)} collective-permute-done((f32[16,128]{1,0:T(8,128)S(1)}, f32[16,128]{1,0:T(8,128)S(1)}, u32[]{:S(2)}, u32[]{:S(2)}) %collective-permute-start.15) | collective-permute-done | bytes 8224 | tf_op jit(solution)/shard_map/ppermute | solution.py:214
  66.2 0.5 collective-permute-start.16
  66.7 3.6 %collective-permute-done.16 = f32[16,128]{1,0:T(8,128)S(1)} collective-permute-done((f32[16,128]{1,0:T(8,128)S(1)}, f32[16,128]{1,0:T(8,128)S(1)}, u32[]{:S(2)}, u32[]{:S(2)}) %collective-permute-start.16) | collective-permute-done | bytes 8224 | tf_op jit(solution)/shard_map/ppermute | solution.py:214
  70.3 0.7 shard_map.55
  (15 shorter events, 0.2 us)
Async XLA Ops:
  0.0 1.1 %copy-start = (bf16[512,768]{1,0:T(8,128)(2,1)S(1)}, bf16[512,768]{1,0:T(8,128)(2,1)}, u32[]{:S(2)}) copy-start(bf16[512,768]{1,0:T(8,128)(2,1)} %refs_0_.1) | copy-start | bytes 2359300
  1.4 0.7 copy-start.2
  2.7 27.0 %collective-permute-start.3 = (bf16[128,768]{1,0:T(8,128)(2,1)S(1)}, bf16[128,768]{1,0:T(8,128)(2,1)S(1)}, u32[]{:S(2)}, u32[]{:S(2)}) collective-permute-start(bf16[128,768]{1,0:T(8,128)(2,1)S(1)} %get-tuple-element.27), channel_id=1, source_target_pairs={{0,8},{2,10},{4,12},{6,14},{8,0},{10,2},{12,4},{14,6},{1,9},{3,11}... | collective-permute-start | bytes 589832 | tf_op jit(solution)/shard_map/ppermute | solution.py:210
  6.8 1.4 %copy-start.1 = (s32[512]{0:T(512)S(1)}, s32[512]{0:T(512)}, u32[]{:S(2)}) copy-start(s32[512]{0:T(512)} %param.7) | copy-start | bytes 6148
  6.8 22.9 %collective-permute-start.5 = (bf16[128,768]{1,0:T(8,128)(2,1)S(1)}, bf16[128,768]{1,0:T(8,128)(2,1)S(1)}, u32[]{:S(2)}, u32[]{:S(2)}) collective-permute-start(bf16[128,768]{1,0:T(8,128)(2,1)S(1)} %get-tuple-element.29), channel_id=1, source_target_pairs={{0,12},{2,14},{4,8},{6,10},{8,4},{10,6},{12,0},{14,2},{1,13},{3,15... | collective-permute-start | bytes 589832 | tf_op jit(solution)/shard_map/ppermute | solution.py:210
  8.7 6.4 %collective-permute-start = (bf16[136,768]{1,0:T(8,128)(2,1)S(1)}, bf16[136,768]{1,0:T(8,128)(2,1)S(1)}, u32[]{:S(2)}, u32[]{:S(2)}) collective-permute-start(bf16[136,768]{1,0:T(8,128)(2,1)S(1)} %get-tuple-element.24), channel_id=1, source_target_pairs={{0,2},{2,0},{4,6},{6,4},{8,10},{10,8},{12,14},{14,12},{1,3},{3,1},... | collective-permute-start | bytes 626696 | tf_op jit(solution)/shard_map/ppermute | solution.py:210
  10.2 0.7 copy-start.3
  15.6 9.0 %collective-permute-start.1 = (bf16[136,768]{1,0:T(8,128)(2,1)S(1)}, bf16[136,768]{1,0:T(8,128)(2,1)S(1)}, u32[]{:S(2)}, u32[]{:S(2)}) collective-permute-start(bf16[136,768]{1,0:T(8,128)(2,1)S(1)} %get-tuple-element.25), channel_id=1, source_target_pairs={{0,4},{2,6},{4,0},{6,2},{8,12},{10,14},{12,8},{14,10},{1,5},{3,7},... | collective-permute-start | bytes 626696 | tf_op jit(solution)/shard_map/ppermute | solution.py:210
  16.9 22.5 %collective-permute-start.4 = (bf16[128,768]{1,0:T(8,128)(2,1)S(1)}, bf16[128,768]{1,0:T(8,128)(2,1)S(1)}, u32[]{:S(2)}, u32[]{:S(2)}) collective-permute-start(bf16[128,768]{1,0:T(8,128)(2,1)S(1)} %get-tuple-element.28), channel_id=1, source_target_pairs={{0,10},{2,8},{4,14},{6,12},{8,2},{10,0},{12,6},{14,4},{1,11},{3,9}... | collective-permute-start | bytes 589832 | tf_op jit(solution)/shard_map/ppermute | solution.py:210
  25.0 16.4 %collective-permute-start.2 = (bf16[128,768]{1,0:T(8,128)(2,1)S(1)}, bf16[128,768]{1,0:T(8,128)(2,1)S(1)}, u32[]{:S(2)}, u32[]{:S(2)}) collective-permute-start(bf16[128,768]{1,0:T(8,128)(2,1)S(1)} %get-tuple-element.26), channel_id=1, source_target_pairs={{0,6},{2,4},{4,2},{6,0},{8,14},{10,12},{12,10},{14,8},{1,7},{3,5},... | collective-permute-start | bytes 589832 | tf_op jit(solution)/shard_map/ppermute | solution.py:210
  26.0 15.4 %collective-permute-start.6 = (bf16[136,768]{1,0:T(8,128)(2,1)S(1)}, bf16[136,768]{1,0:T(8,128)(2,1)S(1)}, u32[]{:S(2)}, u32[]{:S(2)}) collective-permute-start(bf16[136,768]{1,0:T(8,128)(2,1)S(1)} %get-tuple-element.30), channel_id=1, source_target_pairs={{0,14},{2,12},{4,10},{6,8},{8,6},{10,4},{12,2},{14,0},{1,15},{3,13... | collective-permute-start | bytes 626696 | tf_op jit(solution)/shard_map/ppermute | solution.py:210
  42.1 2.2 %collective-permute-start.11 = (bf16[128,768]{1,0:T(8,128)(2,1)S(1)}, bf16[128,768]{1,0:T(8,128)(2,1)S(1)}, u32[]{:S(2)}, u32[]{:S(2)}) collective-permute-start(bf16[128,768]{1,0:T(8,128)(2,1)S(1)} %get-tuple-element.31.refs_8_), channel_id=1, source_target_pairs={{0,1},{1,0},{2,3},{3,2},{4,5},{5,4},{6,7},{7,6},{8,9},{9,8},{10,11... | collective-permute-start | bytes 589832 | tf_op jit(solution)/shard_map/ppermute | solution.py:299
  43.2 5.3 %collective-permute-start.7 = (bf16[128,768]{1,0:T(8,128)(2,1)S(1)}, bf16[128,768]{1,0:T(8,128)(2,1)S(1)}, u32[]{:S(2)}, u32[]{:S(2)}) collective-permute-start(bf16[128,768]{1,0:T(8,128)(2,1)S(1)} %get-tuple-element.32.refs_0_), channel_id=1, source_target_pairs={{0,1},{1,0},{2,3},{3,2},{4,5},{5,4},{6,7},{7,6},{8,9},{9,8},{10,11... | collective-permute-start | bytes 589832 | tf_op jit(solution)/shard_map/ppermute | solution.py:309
  43.7 4.7 %collective-permute-start.8 = (bf16[128,768]{1,0:T(8,128)(2,1)S(1)}, bf16[128,768]{1,0:T(8,128)(2,1)S(1)}, u32[]{:S(2)}, u32[]{:S(2)}) collective-permute-start(bf16[128,768]{1,0:T(8,128)(2,1)S(1)} %get-tuple-element.33.refs_1_), channel_id=1, source_target_pairs={{0,1},{1,0},{2,3},{3,2},{4,5},{5,4},{6,7},{7,6},{8,9},{9,8},{10,11... | collective-permute-start | bytes 589832 | tf_op jit(solution)/shard_map/ppermute | solution.py:309
  43.8 4.6 %collective-permute-start.9 = (bf16[128,768]{1,0:T(8,128)(2,1)S(1)}, bf16[128,768]{1,0:T(8,128)(2,1)S(1)}, u32[]{:S(2)}, u32[]{:S(2)}) collective-permute-start(bf16[128,768]{1,0:T(8,128)(2,1)S(1)} %get-tuple-element.34.refs_2_), channel_id=1, source_target_pairs={{0,1},{1,0},{2,3},{3,2},{4,5},{5,4},{6,7},{7,6},{8,9},{9,8},{10,11... | collective-permute-start | bytes 589832 | tf_op jit(solution)/shard_map/ppermute | solution.py:309
  44.2 4.2 %collective-permute-start.10 = (bf16[128,768]{1,0:T(8,128)(2,1)S(1)}, bf16[128,768]{1,0:T(8,128)(2,1)S(1)}, u32[]{:S(2)}, u32[]{:S(2)}) collective-permute-start(bf16[128,768]{1,0:T(8,128)(2,1)S(1)} %get-tuple-element.35.refs_3_), channel_id=1, source_target_pairs={{0,1},{1,0},{2,3},{3,2},{4,5},{5,4},{6,7},{7,6},{8,9},{9,8},{10,11... | collective-permute-start | bytes 589832 | tf_op jit(solution)/shard_map/ppermute | solution.py:309
  44.4 13.6 %collective-permute-start.12 = (bf16[128,768]{1,0:T(8,128)(2,1)S(1)}, bf16[128,768]{1,0:T(8,128)(2,1)S(1)}, u32[]{:S(2)}, u32[]{:S(2)}) collective-permute-start(bf16[128,768]{1,0:T(8,128)(2,1)S(1)} %add.10), channel_id=1, source_target_pairs={{0,9},{1,8},{4,13},{5,12},{8,1},{9,0},{12,5},{13,4},{2,11},{3,10},... | collective-permute-start | bytes 589832 | tf_op jit(solution)/shard_map/ppermute | solution.py:299
  58.7 1.2 %collective-permute-start.13 = (f32[8,128]{1,0:T(8,128)S(1)}, f32[8,128]{1,0:T(8,128)S(1)}, u32[]{:S(2)}, u32[]{:S(2)}) collective-permute-start(f32[8,128]{1,0:T(8,128)S(1)} %pad_maximum_fusion.3), channel_id=1, source_target_pairs={{0,1},{1,0},{2,3},{3,2},{4,5},{5,4},{6,7},{7,6},{8,9},{9,8},{10,11... | collective-permute-start | bytes 12296 | tf_op jit(solution)/shard_map/ppermute | solution.py:327
  59.9 3.1 %collective-permute-start.14 = (f32[8,128]{1,0:T(8,128)S(1)}, f32[8,128]{1,0:T(8,128)S(1)}, u32[]{:S(2)}, u32[]{:S(2)}) collective-permute-start(f32[8,128]{1,0:T(8,128)S(1)} %pad_maximum_fusion.4), channel_id=1, source_target_pairs={{0,3},{1,2},{2,1},{3,0},{4,7},{5,6},{6,5},{7,4},{8,11},{9,10},{10,... | collective-permute-start | bytes 12296 | tf_op jit(solution)/shard_map/ppermute | solution.py:214
  63.0 3.1 %collective-permute-start.15 = (f32[16,128]{1,0:T(8,128)S(1)}, f32[16,128]{1,0:T(8,128)S(1)}, u32[]{:S(2)}, u32[]{:S(2)}) collective-permute-start(f32[16,128]{1,0:T(8,128)S(1)} %pad_maximum_fusion.1), channel_id=1, source_target_pairs={{0,5},{1,4},{2,7},{3,6},{4,1},{5,0},{6,3},{7,2},{8,13},{9,12},{10,... | collective-permute-start | bytes 24584 | tf_op jit(solution)/shard_map/ppermute | solution.py:214
  66.2 4.1 %collective-permute-start.16 = (f32[16,128]{1,0:T(8,128)S(1)}, f32[16,128]{1,0:T(8,128)S(1)}, u32[]{:S(2)}, u32[]{:S(2)}) collective-permute-start(f32[16,128]{1,0:T(8,128)S(1)} %fusion), channel_id=1, source_target_pairs={{0,9},{1,8},{2,11},{3,10},{4,13},{5,12},{6,15},{7,14},{8,1},{9,0},... | collective-permute-start | bytes 24584 | tf_op jit(solution)/shard_map/ppermute | solution.py:214

commit v4 on v3

--- a/solution.py
+++ b/solution.py
@@ -16,7 +16,7 @@
 TAG_ROWS = 8
 TAG_BASE = 32
 EMPTY = 4096
-PIECES = 4
+PIECES = (64, 112, 112, 112, 112)
 OWNERS = ("clus", "sub")
 
 ROWS_BY_ROWS = (((1,), (1,)), ((), ()))
@@ -43,7 +43,9 @@
         in_specs=[spec] * count + [pl.BlockSpec(memory_space=pl.ANY)] * len(after),
         out_specs=[spec] * len(out_shape) if many else spec,
         compiler_params=pltpu.CompilerParams(vmem_limit_bytes=40 * 2**20),
-        cost_estimate=pl.CostEstimate(flops=flops, bytes_accessed=moved, transcendentals=0),
+        cost_estimate=pl.CostEstimate(
+            flops=flops, bytes_accessed=moved if flops else 0, transcendentals=0
+        ),
     )(*leaves, *after)
 
 
@@ -136,22 +138,25 @@
     return jnp.concatenate([chunks[k][:send, :] for k in range(8)], axis=0)
 
 
-def border_body(send, chunks, want_ref, tags, keep_ref, give_ref):
-    chosen = one_hot(want_ref[...] == tags_of(chunks, tags, send))
+def border_body(send, chunks, want_ref, tags, keep_ref, give_ref, head_ref):
+    tags = tags_of(chunks, tags, send)
+    first = iota((head_ref.shape[0], tags.shape[1]), 0)
+    chosen = jnp.concatenate([one_hot(want_ref[...] == tags), one_hot(first == tags)], axis=0)
     picked = dot(chosen, rows_of(chunks, send)).astype(jnp.bfloat16)
     keep_ref[...] = picked[: BORDER // 2]
-    give_ref[...] = picked[BORDER // 2 :]
+    give_ref[...] = picked[BORDER // 2 : BORDER]
+    head_ref[...] = picked[BORDER:]
 
 
 def place_body(send, chunks, tags, *mine_refs):
     tags = tags_of(chunks, tags, send)
-    rows = rows_of(chunks, send)
+    first = HALF - sum(ref.shape[0] for ref in mine_refs)
+    chosen = one_hot(iota((HALF - first, tags.shape[1]), 0) + first == tags)
+    placed = dot(chosen, rows_of(chunks, send)).astype(jnp.bfloat16)
     first = 0
-    for mine_ref in mine_refs:
-        count = mine_ref.shape[0]
-        chosen = one_hot(iota((count, tags.shape[1]), 0) + first == tags)
-        mine_ref[...] = dot(chosen, rows).astype(jnp.bfloat16)
-        first += count
+    for ref in mine_refs:
+        ref[...] = placed[first : first + ref.shape[0]]
+        first += ref.shape[0]
 
 
 def weigh(products, width):
@@ -288,29 +293,31 @@
         (2 * i + r, 2 * ((i + by) % clus_count) + 1 - r) for i in range(clus_count) for r in range(2)
     ]
     part = jax.ShapeDtypeStruct((BORDER // 2, width), jnp.bfloat16)
-    keep, give = call(
+    pieces = [jax.ShapeDtypeStruct((count, width), jnp.bfloat16) for count in PIECES]
+    keep, give, head = call(
         functools.partial(border_body, send),
-        [part, part],
+        [part, part, pieces[0]],
         2 * BORDER * owners * send * width,
         chunks,
         want,
         tags,
     )
-    tile = lax.ppermute(keep + lax.ppermute(give, "rep", swap), ("clus", "rep"), opposite)
-    part = jax.ShapeDtypeStruct((HALF // PIECES, width), jnp.bfloat16)
-    mine = call(
+    chosen = keep + lax.ppermute(give, "rep", swap)
+    tile = lax.ppermute(chosen, ("clus", "rep"), opposite)
+    rest = call(
         functools.partial(place_body, send),
-        [part] * PIECES,
+        pieces[1:],
         2 * HALF * owners * send * width,
         chunks,
         tags,
         after=[give],
     )
+    mine = [head, *rest]
     other = [lax.ppermute(part, "rep", swap) for part in mine]
     near = call(
         near_body,
         jax.ShapeDtypeStruct((1, HALF), jnp.float32),
-        2 * HALF * CAP * width,
+        0,
         mine,
         other,
     )

time: 71.2 us -> 70 us (0.983)
  waiting for transfers between devices: 39.6 us -> 37.4 us
  starting transfers between devices: 21.9 us -> 22.9 us
    ppermute x2, waiting for transfers between devices: 8.37 us -> 5.86 us  [the longest x1 4.93 us: per_device(): tile = lax.ppermute(chosen, ('clus', 'rep'), opposite)]
    ppermute x4 -> x5, waiting for transfers between devices: 0.01 us -> 1.27 us  [per_device(): other = [lax.ppermute(part, 'rep', swap) for part in mine]]
    ppermute x3, waiting for transfers between devices: 9.51 us -> 8.64 us  [across(): return lax.ppermute(x, (*OWNERS, 'rep'), pairs)]
    ppermute x3, starting transfers between devices: 0.77 us -> 1.63 us  [across(): return lax.ppermute(x, (*OWNERS, 'rep'), pairs)]
    ppermute x4 -> x5, starting transfers between devices: 1.15 us -> 1.58 us  [per_device(): other = [lax.ppermute(part, 'rep', swap) for part in mine]]
  transfers between devices with their start and end apart: 17 -> 18, of which waited for: 9 -> 14; matrix products, arithmetic and copies ran while one was open for 0% -> 1% of each run, Pallas kernels for 5% -> 5%
where the time goes in v4:
time: 70 us; the launch traced here: 69.8 us
  waiting for transfers between devices  37.4 us (53%)
  starting transfers between devices  22.9 us (33%)
  Pallas kernels  6.37 us (9%)
  local copies, waits for them, and re-layouts  2.78 us (4%)
    ppermute x7, waiting for transfers between devices, toward(): return lax.ppermute(x, OWNERS, [(i, i ^ flip) for i in range(owners)])  20.6 us
    ppermute x7, starting transfers between devices, toward(): return lax.ppermute(x, OWNERS, [(i, i ^ flip) for i in range(owners)])  15.7 us
    ppermute x3, waiting for transfers between devices, across(): return lax.ppermute(x, (*OWNERS, 'rep'), pairs)  8.64 us
    pallas_call x10, Pallas kernels, call(): pl.pallas_call(kernel, out_shape=out_shape, in_specs=[spec] * count + [pl...  6.37 us
    ppermute x1, waiting for transfers between devices, per_device(): tile = lax.ppermute(chosen, ('clus', 'rep'), opposite)  4.93 us
    ppermute x1, starting transfers between devices, per_device(): tile = lax.ppermute(chosen, ('clus', 'rep'), opposite)  3.75 us
    unnamed x8, local copies, waits for them, and re-layouts  2.49 us
    ppermute x3, starting transfers between devices, across(): return lax.ppermute(x, (*OWNERS, 'rep'), pairs)  1.63 us
  transfers between devices with their start and end apart: 18, of which 14 were waited for; matrix products, arithmetic and copies ran while one was open for 1% of the time, Pallas kernels for 5%

profile of v4, /device:TPU:0, one launch (start us, length us, event | category | flops | bytes accessed | tf_op | source)
XLA Modules:
  0.0 69.8 jit_solution(7468474866987203569)
XLA Ops:
  0.0 0.0 copy-start
  0.0 1.1 %copy-done = bf16[512,768]{1,0:T(8,128)(2,1)S(1)} copy-done((bf16[512,768]{1,0:T(8,128)(2,1)S(1)}, bf16[512,768]{1,0:T(8,128)(2,1)}, u32[]{:S(2)}) %copy-start) | copy-done | bytes 786456
  1.1 0.2 shard_map.46.refs_0_
  1.4 0.0 copy-start.2
  1.4 0.7 copy-done.2
  2.1 0.6 shard_map.47
  2.7 4.1 %collective-permute-start.3 = (bf16[128,768]{1,0:T(8,128)(2,1)S(1)}, bf16[128,768]{1,0:T(8,128)(2,1)S(1)}, u32[]{:S(2)}, u32[]{:S(2)}) collective-permute-start(bf16[128,768]{1,0:T(8,128)(2,1)S(1)} %get-tuple-element.28), channel_id=1, source_target_pairs={{0,8},{2,10},{4,12},{6,14},{8,0},{10,2},{12,4},{14,6},{1,9},{3,11}... | collective-permute-start | bytes 589832 | tf_op jit(solution)/shard_map/ppermute | solution.py:215
  6.8 0.0 copy-start.1
  6.8 1.3 %collective-permute-start.5 = (bf16[128,768]{1,0:T(8,128)(2,1)S(1)}, bf16[128,768]{1,0:T(8,128)(2,1)S(1)}, u32[]{:S(2)}, u32[]{:S(2)}) collective-permute-start(bf16[128,768]{1,0:T(8,128)(2,1)S(1)} %get-tuple-element.30), channel_id=1, source_target_pairs={{0,12},{2,14},{4,8},{6,10},{8,4},{10,6},{12,0},{14,2},{1,13},{3,15... | collective-permute-start | bytes 589832 | tf_op jit(solution)/shard_map/ppermute | solution.py:215
  8.1 0.0 copy-done.1
  8.1 0.5 shard_map.48
  8.7 1.6 %collective-permute-start = (bf16[136,768]{1,0:T(8,128)(2,1)S(1)}, bf16[136,768]{1,0:T(8,128)(2,1)S(1)}, u32[]{:S(2)}, u32[]{:S(2)}) collective-permute-start(bf16[136,768]{1,0:T(8,128)(2,1)S(1)} %get-tuple-element.25), channel_id=1, source_target_pairs={{0,2},{2,0},{4,6},{6,4},{8,10},{10,8},{12,14},{14,12},{1,3},{3,1},... | collective-permute-start | bytes 626696 | tf_op jit(solution)/shard_map/ppermute | solution.py:215
  10.2 0.0 copy-start.3
  10.2 0.7 copy-done.3
  10.9 0.1 copy.11
  11.1 4.0 %collective-permute-done.refs_3_.refs_1_ = bf16[136,768]{1,0:T(8,128)(2,1)S(1)} collective-permute-done((bf16[136,768]{1,0:T(8,128)(2,1)S(1)}, bf16[136,768]{1,0:T(8,128)(2,1)S(1)}, u32[]{:S(2)}, u32[]{:S(2)}) %collective-permute-start) | collective-permute-done | bytes 208928 | tf_op jit(solution)/shard_map/ppermute | solution.py:215
  15.1 0.4 shard_map.49
  15.6 1.2 %collective-permute-start.1 = (bf16[136,768]{1,0:T(8,128)(2,1)S(1)}, bf16[136,768]{1,0:T(8,128)(2,1)S(1)}, u32[]{:S(2)}, u32[]{:S(2)}) collective-permute-start(bf16[136,768]{1,0:T(8,128)(2,1)S(1)} %get-tuple-element.26), channel_id=1, source_target_pairs={{0,4},{2,6},{4,0},{6,2},{8,12},{10,14},{12,8},{14,10},{1,5},{3,7},... | collective-permute-start | bytes 626696 | tf_op jit(solution)/shard_map/ppermute | solution.py:215
  16.8 0.1 copy.10
  16.9 2.8 %collective-permute-start.4 = (bf16[128,768]{1,0:T(8,128)(2,1)S(1)}, bf16[128,768]{1,0:T(8,128)(2,1)S(1)}, u32[]{:S(2)}, u32[]{:S(2)}) collective-permute-start(bf16[128,768]{1,0:T(8,128)(2,1)S(1)} %get-tuple-element.29), channel_id=1, source_target_pairs={{0,10},{2,8},{4,14},{6,12},{8,2},{10,0},{12,6},{14,4},{1,11},{3,9}... | collective-permute-start | bytes 589832 | tf_op jit(solution)/shard_map/ppermute | solution.py:215
  19.8 4.8 %collective-permute-done.1.refs_4_.refs_2_ = bf16[136,768]{1,0:T(8,128)(2,1)S(1)} collective-permute-done((bf16[136,768]{1,0:T(8,128)(2,1)S(1)}, bf16[136,768]{1,0:T(8,128)(2,1)S(1)}, u32[]{:S(2)}, u32[]{:S(2)}) %collective-permute-start.1) | collective-permute-done | bytes 208928 | tf_op jit(solution)/shard_map/ppermute | solution.py:215
  24.6 0.4 shard_map.50
  25.0 1.0 %collective-permute-start.2 = (bf16[128,768]{1,0:T(8,128)(2,1)S(1)}, bf16[128,768]{1,0:T(8,128)(2,1)S(1)}, u32[]{:S(2)}, u32[]{:S(2)}) collective-permute-start(bf16[128,768]{1,0:T(8,128)(2,1)S(1)} %get-tuple-element.27), channel_id=1, source_target_pairs={{0,6},{2,4},{4,2},{6,0},{8,14},{10,12},{12,10},{14,8},{1,7},{3,5},... | collective-permute-start | bytes 589832 | tf_op jit(solution)/shard_map/ppermute | solution.py:215
  26.0 3.6 %collective-permute-start.6 = (bf16[136,768]{1,0:T(8,128)(2,1)S(1)}, bf16[136,768]{1,0:T(8,128)(2,1)S(1)}, u32[]{:S(2)}, u32[]{:S(2)}) collective-permute-start(bf16[136,768]{1,0:T(8,128)(2,1)S(1)} %get-tuple-element.31), channel_id=1, source_target_pairs={{0,14},{2,12},{4,10},{6,8},{8,6},{10,4},{12,2},{14,0},{1,15},{3,13... | collective-permute-start | bytes 626696 | tf_op jit(solution)/shard_map/ppermute | solution.py:215
  29.6 0.0 collective-permute-done.3.refs_4_
  29.6 0.0 collective-permute-done.5.refs_6_
  29.7 9.8 %collective-permute-done.4.refs_5_ = bf16[128,768]{1,0:T(8,128)(2,1)S(1)} collective-permute-done((bf16[128,768]{1,0:T(8,128)(2,1)S(1)}, bf16[128,768]{1,0:T(8,128)(2,1)S(1)}, u32[]{:S(2)}, u32[]{:S(2)}) %collective-permute-start.4) | collective-permute-done | bytes 196640 | tf_op jit(solution)/shard_map/ppermute | solution.py:215
  39.4 2.0 %collective-permute-done.2.refs_3_ = bf16[128,768]{1,0:T(8,128)(2,1)S(1)} collective-permute-done((bf16[128,768]{1,0:T(8,128)(2,1)S(1)}, bf16[128,768]{1,0:T(8,128)(2,1)S(1)}, u32[]{:S(2)}, u32[]{:S(2)}) %collective-permute-start.2) | collective-permute-done | bytes 196640 | tf_op jit(solution)/shard_map/ppermute | solution.py:215
  41.4 0.0 collective-permute-done.6.refs_7_
  41.4 0.7 %shard_map.51 = (bf16[128,768]{1,0:T(8,128)(2,1)S(1)}, bf16[128,768]{1,0:T(8,128)(2,1)S(1)}, bf16[64,768]{1,0:T(8,128)(2,1)S(1)}) custom-call(bf16[136,768]{1,0:T(8,128)(2,1)S(1)} %get-tuple-element.24.refs_0_, bf16[136,768]{1,0:T(8,128)(2,1)S(1)} %collective-permute-done.refs_3_.refs_1_, bf16[136,768]{1,0:T(8,128)(2,1)S(1)} %collective-permute-done.1.refs_4_.refs_2_, ...), custom_call_target="tpu_custom_call" | custom-call | flops 402653184 | bytes 2114560 | tf_op jit(solution)/shard_map/pallas_call | solution.py:40
  42.2 0.1 collective-permute-start.12
  42.2 0.5 collective-permute-start.7
  42.7 0.9 %collective-permute-done.12 = bf16[128,768]{1,0:T(8,128)(2,1)S(1)} collective-permute-done((bf16[128,768]{1,0:T(8,128)(2,1)S(1)}, bf16[128,768]{1,0:T(8,128)(2,1)S(1)}, u32[]{:S(2)}, u32[]{:S(2)}) %collective-permute-start.12) | collective-permute-done | bytes 196640 | tf_op jit(solution)/shard_map/ppermute | solution.py:305
  43.7 3.8 %collective-permute-start.13 = (bf16[128,768]{1,0:T(8,128)(2,1)S(1)}, bf16[128,768]{1,0:T(8,128)(2,1)S(1)}, u32[]{:S(2)}, u32[]{:S(2)}) collective-permute-start(bf16[128,768]{1,0:T(8,128)(2,1)S(1)} %add.10), channel_id=1, source_target_pairs={{0,9},{1,8},{4,13},{5,12},{8,1},{9,0},{12,5},{13,4},{2,11},{3,10},... | collective-permute-start | bytes 589832 | tf_op jit(solution)/shard_map/ppermute | solution.py:306
  47.5 0.9 %shard_map.52 = (bf16[112,768]{1,0:T(8,128)(2,1)S(1)}, bf16[112,768]{1,0:T(8,128)(2,1)S(1)}, bf16[112,768]{1,0:T(8,128)(2,1)S(1)}, bf16[112,768]{1,0:T(8,128)(2,1)S(1)}) custom-call(bf16[136,768]{1,0:T(8,128)(2,1)S(1)} %get-tuple-element.24.refs_0_, bf16[136,768]{1,0:T(8,128)(2,1)S(1)} %collective-permute-done.refs_3_.refs_1_, ...), custom_call_target="tpu_custom_call" | custom-call | flops 805306368 | bytes 2310144 | tf_op jit(solution)/shard_map/pallas_call | solution.py:40
  48.4 0.4 collective-permute-start.8
  48.8 0.1 collective-permute-start.9
  48.9 0.4 collective-permute-start.10
  49.3 0.0 collective-permute-done.7.refs_5_
  49.3 0.1 collective-permute-start.11
  49.5 0.4 collective-permute-done.8.refs_6_
  49.8 0.4 collective-permute-done.9.refs_7_
  50.2 0.2 collective-permute-done.10.refs_8_
  50.5 0.3 collective-permute-done.11.refs_9_
  50.7 1.1 %shard_map.53.refs_11_ = f32[1,512]{1,0:T(1,128)S(1)} custom-call(bf16[64,768]{1,0:T(8,128)(2,1)S(1)} %get-tuple-element.32.refs_0_, bf16[112,768]{1,0:T(8,128)(2,1)S(1)} %get-tuple-element.34.refs_1_, bf16[112,768]{1,0:T(8,128)(2,1)S(1)} %get-tuple-element.35.refs_2_, bf16[112,768]{1,0:T(8,128)(2,1)S(1)} %get-tuple-element.36.refs_3_, ...), custom_call_target="tpu_custom_call" | custom-call | tf_op jit(solution)/shard_map/pallas_call | solution.py:40
  51.9 4.9 %collective-permute-done.13.refs_10_ = bf16[128,768]{1,0:T(8,128)(2,1)S(1)} collective-permute-done((bf16[128,768]{1,0:T(8,128)(2,1)S(1)}, bf16[128,768]{1,0:T(8,128)(2,1)S(1)}, u32[]{:S(2)}, u32[]{:S(2)}) %collective-permute-start.13) | collective-permute-done | bytes 196640 | tf_op jit(solution)/shard_map/ppermute | solution.py:306
  56.8 0.7 shard_map.54
  57.5 0.2 collective-permute-start.14
  57.7 1.0 %collective-permute-done.14 = f32[8,128]{1,0:T(8,128)S(1)} collective-permute-done((f32[8,128]{1,0:T(8,128)S(1)}, f32[8,128]{1,0:T(8,128)S(1)}, u32[]{:S(2)}, u32[]{:S(2)}) %collective-permute-start.14) | collective-permute-done | bytes 4128 | tf_op jit(solution)/shard_map/ppermute | solution.py:334
  58.8 0.4 collective-permute-start.15
  59.1 2.7 %collective-permute-done.15 = f32[8,128]{1,0:T(8,128)S(1)} collective-permute-done((f32[8,128]{1,0:T(8,128)S(1)}, f32[8,128]{1,0:T(8,128)S(1)}, u32[]{:S(2)}, u32[]{:S(2)}) %collective-permute-start.15) | collective-permute-done | bytes 4128 | tf_op jit(solution)/shard_map/ppermute | solution.py:219
  61.9 0.1 collective-permute-start.16
  62.0 3.1 %collective-permute-done.16 = f32[16,128]{1,0:T(8,128)S(1)} collective-permute-done((f32[16,128]{1,0:T(8,128)S(1)}, f32[16,128]{1,0:T(8,128)S(1)}, u32[]{:S(2)}, u32[]{:S(2)}) %collective-permute-start.16) | collective-permute-done | bytes 8224 | tf_op jit(solution)/shard_map/ppermute | solution.py:219
  65.0 1.2 %collective-permute-start.17 = (f32[16,128]{1,0:T(8,128)S(1)}, f32[16,128]{1,0:T(8,128)S(1)}, u32[]{:S(2)}, u32[]{:S(2)}) collective-permute-start(f32[16,128]{1,0:T(8,128)S(1)} %fusion), channel_id=1, source_target_pairs={{0,9},{1,8},{2,11},{3,10},{4,13},{5,12},{6,15},{7,14},{8,1},{9,0},... | collective-permute-start | bytes 24584 | tf_op jit(solution)/shard_map/ppermute | solution.py:219
  66.2 2.8 %collective-permute-done.17 = f32[16,128]{1,0:T(8,128)S(1)} collective-permute-done((f32[16,128]{1,0:T(8,128)S(1)}, f32[16,128]{1,0:T(8,128)S(1)}, u32[]{:S(2)}, u32[]{:S(2)}) %collective-permute-start.17) | collective-permute-done | bytes 8224 | tf_op jit(solution)/shard_map/ppermute | solution.py:219
  69.1 0.7 %shard_map.55 = f32[4,128]{1,0:T(4,128)} custom-call(f32[32,128]{1,0:T(8,128)S(1)} %pad_maximum_fusion.refs_0_, s32[4,128]{1,0:T(4,128)S(1)} %bitcast.17, s32[4,128]{1,0:T(4,128)S(1)} %bitcast.15, s32[1,1]{1,0:T(1,128)} %bitcast.1.refs_2_.refs_3_), custom_call_target="tpu_custom_call" | custom-call | flops 4096 | bytes 22532 | tf_op jit(solution)/shard_map/pallas_call | solution.py:40
  (15 shorter events, 0.2 us)
Async XLA Ops:
  0.0 1.1 %copy-start = (bf16[512,768]{1,0:T(8,128)(2,1)S(1)}, bf16[512,768]{1,0:T(8,128)(2,1)}, u32[]{:S(2)}) copy-start(bf16[512,768]{1,0:T(8,128)(2,1)} %refs_0_.1) | copy-start | bytes 2359300
  1.4 0.7 copy-start.2
  2.7 27.0 %collective-permute-start.3 = (bf16[128,768]{1,0:T(8,128)(2,1)S(1)}, bf16[128,768]{1,0:T(8,128)(2,1)S(1)}, u32[]{:S(2)}, u32[]{:S(2)}) collective-permute-start(bf16[128,768]{1,0:T(8,128)(2,1)S(1)} %get-tuple-element.28), channel_id=1, source_target_pairs={{0,8},{2,10},{4,12},{6,14},{8,0},{10,2},{12,4},{14,6},{1,9},{3,11}... | collective-permute-start | bytes 589832 | tf_op jit(solution)/shard_map/ppermute | solution.py:215
  6.8 1.4 %copy-start.1 = (s32[512]{0:T(512)S(1)}, s32[512]{0:T(512)}, u32[]{:S(2)}) copy-start(s32[512]{0:T(512)} %param.7) | copy-start | bytes 6148
  6.8 22.9 %collective-permute-start.5 = (bf16[128,768]{1,0:T(8,128)(2,1)S(1)}, bf16[128,768]{1,0:T(8,128)(2,1)S(1)}, u32[]{:S(2)}, u32[]{:S(2)}) collective-permute-start(bf16[128,768]{1,0:T(8,128)(2,1)S(1)} %get-tuple-element.30), channel_id=1, source_target_pairs={{0,12},{2,14},{4,8},{6,10},{8,4},{10,6},{12,0},{14,2},{1,13},{3,15... | collective-permute-start | bytes 589832 | tf_op jit(solution)/shard_map/ppermute | solution.py:215
  8.7 6.4 %collective-permute-start = (bf16[136,768]{1,0:T(8,128)(2,1)S(1)}, bf16[136,768]{1,0:T(8,128)(2,1)S(1)}, u32[]{:S(2)}, u32[]{:S(2)}) collective-permute-start(bf16[136,768]{1,0:T(8,128)(2,1)S(1)} %get-tuple-element.25), channel_id=1, source_target_pairs={{0,2},{2,0},{4,6},{6,4},{8,10},{10,8},{12,14},{14,12},{1,3},{3,1},... | collective-permute-start | bytes 626696 | tf_op jit(solution)/shard_map/ppermute | solution.py:215
  10.2 0.7 copy-start.3
  15.6 9.0 %collective-permute-start.1 = (bf16[136,768]{1,0:T(8,128)(2,1)S(1)}, bf16[136,768]{1,0:T(8,128)(2,1)S(1)}, u32[]{:S(2)}, u32[]{:S(2)}) collective-permute-start(bf16[136,768]{1,0:T(8,128)(2,1)S(1)} %get-tuple-element.26), channel_id=1, source_target_pairs={{0,4},{2,6},{4,0},{6,2},{8,12},{10,14},{12,8},{14,10},{1,5},{3,7},... | collective-permute-start | bytes 626696 | tf_op jit(solution)/shard_map/ppermute | solution.py:215
  16.9 22.5 %collective-permute-start.4 = (bf16[128,768]{1,0:T(8,128)(2,1)S(1)}, bf16[128,768]{1,0:T(8,128)(2,1)S(1)}, u32[]{:S(2)}, u32[]{:S(2)}) collective-permute-start(bf16[128,768]{1,0:T(8,128)(2,1)S(1)} %get-tuple-element.29), channel_id=1, source_target_pairs={{0,10},{2,8},{4,14},{6,12},{8,2},{10,0},{12,6},{14,4},{1,11},{3,9}... | collective-permute-start | bytes 589832 | tf_op jit(solution)/shard_map/ppermute | solution.py:215
  25.0 16.4 %collective-permute-start.2 = (bf16[128,768]{1,0:T(8,128)(2,1)S(1)}, bf16[128,768]{1,0:T(8,128)(2,1)S(1)}, u32[]{:S(2)}, u32[]{:S(2)}) collective-permute-start(bf16[128,768]{1,0:T(8,128)(2,1)S(1)} %get-tuple-element.27), channel_id=1, source_target_pairs={{0,6},{2,4},{4,2},{6,0},{8,14},{10,12},{12,10},{14,8},{1,7},{3,5},... | collective-permute-start | bytes 589832 | tf_op jit(solution)/shard_map/ppermute | solution.py:215
  26.0 15.4 %collective-permute-start.6 = (bf16[136,768]{1,0:T(8,128)(2,1)S(1)}, bf16[136,768]{1,0:T(8,128)(2,1)S(1)}, u32[]{:S(2)}, u32[]{:S(2)}) collective-permute-start(bf16[136,768]{1,0:T(8,128)(2,1)S(1)} %get-tuple-element.31), channel_id=1, source_target_pairs={{0,14},{2,12},{4,10},{6,8},{8,6},{10,4},{12,2},{14,0},{1,15},{3,13... | collective-permute-start | bytes 626696 | tf_op jit(solution)/shard_map/ppermute | solution.py:215
  42.2 1.5 %collective-permute-start.12 = (bf16[128,768]{1,0:T(8,128)(2,1)S(1)}, bf16[128,768]{1,0:T(8,128)(2,1)S(1)}, u32[]{:S(2)}, u32[]{:S(2)}) collective-permute-start(bf16[128,768]{1,0:T(8,128)(2,1)S(1)} %get-tuple-element.33.refs_8_), channel_id=1, source_target_pairs={{0,1},{1,0},{2,3},{3,2},{4,5},{5,4},{6,7},{7,6},{8,9},{9,8},{10,11... | collective-permute-start | bytes 589832 | tf_op jit(solution)/shard_map/ppermute | solution.py:305
  42.2 7.1 %collective-permute-start.7 = (bf16[64,768]{1,0:T(8,128)(2,1)S(1)}, bf16[64,768]{1,0:T(8,128)(2,1)S(1)}, u32[]{:S(2)}, u32[]{:S(2)}) collective-permute-start(bf16[64,768]{1,0:T(8,128)(2,1)S(1)} %get-tuple-element.32.refs_0_), channel_id=1, source_target_pairs={{0,1},{1,0},{2,3},{3,2},{4,5},{5,4},{6,7},{7,6},{8,9},{9,8},{10,11... | collective-permute-start | bytes 294920 | tf_op jit(solution)/shard_map/ppermute | solution.py:316
  43.7 13.1 %collective-permute-start.13 = (bf16[128,768]{1,0:T(8,128)(2,1)S(1)}, bf16[128,768]{1,0:T(8,128)(2,1)S(1)}, u32[]{:S(2)}, u32[]{:S(2)}) collective-permute-start(bf16[128,768]{1,0:T(8,128)(2,1)S(1)} %add.10), channel_id=1, source_target_pairs={{0,9},{1,8},{4,13},{5,12},{8,1},{9,0},{12,5},{13,4},{2,11},{3,10},... | collective-permute-start | bytes 589832 | tf_op jit(solution)/shard_map/ppermute | solution.py:306
  48.4 1.5 %collective-permute-start.8 = (bf16[112,768]{1,0:T(8,128)(2,1)S(1)}, bf16[112,768]{1,0:T(8,128)(2,1)S(1)}, u32[]{:S(2)}, u32[]{:S(2)}) collective-permute-start(bf16[112,768]{1,0:T(8,128)(2,1)S(1)} %get-tuple-element.34.refs_1_), channel_id=1, source_target_pairs={{0,1},{1,0},{2,3},{3,2},{4,5},{5,4},{6,7},{7,6},{8,9},{9,8},{10,11... | collective-permute-start | bytes 516104 | tf_op jit(solution)/shard_map/ppermute | solution.py:316
  48.8 1.4 %collective-permute-start.9 = (bf16[112,768]{1,0:T(8,128)(2,1)S(1)}, bf16[112,768]{1,0:T(8,128)(2,1)S(1)}, u32[]{:S(2)}, u32[]{:S(2)}) collective-permute-start(bf16[112,768]{1,0:T(8,128)(2,1)S(1)} %get-tuple-element.35.refs_2_), channel_id=1, source_target_pairs={{0,1},{1,0},{2,3},{3,2},{4,5},{5,4},{6,7},{7,6},{8,9},{9,8},{10,11... | collective-permute-start | bytes 516104 | tf_op jit(solution)/shard_map/ppermute | solution.py:316
  48.9 1.5 %collective-permute-start.10 = (bf16[112,768]{1,0:T(8,128)(2,1)S(1)}, bf16[112,768]{1,0:T(8,128)(2,1)S(1)}, u32[]{:S(2)}, u32[]{:S(2)}) collective-permute-start(bf16[112,768]{1,0:T(8,128)(2,1)S(1)} %get-tuple-element.36.refs_3_), channel_id=1, source_target_pairs={{0,1},{1,0},{2,3},{3,2},{4,5},{5,4},{6,7},{7,6},{8,9},{9,8},{10,11... | collective-permute-start | bytes 516104 | tf_op jit(solution)/shard_map/ppermute | solution.py:316
  49.3 1.4 %collective-permute-start.11 = (bf16[112,768]{1,0:T(8,128)(2,1)S(1)}, bf16[112,768]{1,0:T(8,128)(2,1)S(1)}, u32[]{:S(2)}, u32[]{:S(2)}) collective-permute-start(bf16[112,768]{1,0:T(8,128)(2,1)S(1)} %get-tuple-element.37.refs_4_), channel_id=1, source_target_pairs={{0,1},{1,0},{2,3},{3,2},{4,5},{5,4},{6,7},{7,6},{8,9},{9,8},{10,11... | collective-permute-start | bytes 516104 | tf_op jit(solution)/shard_map/ppermute | solution.py:316
  57.5 1.2 %collective-permute-start.14 = (f32[8,128]{1,0:T(8,128)S(1)}, f32[8,128]{1,0:T(8,128)S(1)}, u32[]{:S(2)}, u32[]{:S(2)}) collective-permute-start(f32[8,128]{1,0:T(8,128)S(1)} %pad_maximum_fusion.3), channel_id=1, source_target_pairs={{0,1},{1,0},{2,3},{3,2},{4,5},{5,4},{6,7},{7,6},{8,9},{9,8},{10,11... | collective-permute-start | bytes 12296 | tf_op jit(solution)/shard_map/ppermute | solution.py:334
  58.8 3.1 %collective-permute-start.15 = (f32[8,128]{1,0:T(8,128)S(1)}, f32[8,128]{1,0:T(8,128)S(1)}, u32[]{:S(2)}, u32[]{:S(2)}) collective-permute-start(f32[8,128]{1,0:T(8,128)S(1)} %pad_maximum_fusion.4), channel_id=1, source_target_pairs={{0,3},{1,2},{2,1},{3,0},{4,7},{5,6},{6,5},{7,4},{8,11},{9,10},{10,... | collective-permute-start | bytes 12296 | tf_op jit(solution)/shard_map/ppermute | solution.py:219
  61.9 3.1 %collective-permute-start.16 = (f32[16,128]{1,0:T(8,128)S(1)}, f32[16,128]{1,0:T(8,128)S(1)}, u32[]{:S(2)}, u32[]{:S(2)}) collective-permute-start(f32[16,128]{1,0:T(8,128)S(1)} %pad_maximum_fusion.1), channel_id=1, source_target_pairs={{0,5},{1,4},{2,7},{3,6},{4,1},{5,0},{6,3},{7,2},{8,13},{9,12},{10,... | collective-permute-start | bytes 24584 | tf_op jit(solution)/shard_map/ppermute | solution.py:219
  65.0 4.0 %collective-permute-start.17 = (f32[16,128]{1,0:T(8,128)S(1)}, f32[16,128]{1,0:T(8,128)S(1)}, u32[]{:S(2)}, u32[]{:S(2)}) collective-permute-start(f32[16,128]{1,0:T(8,128)S(1)} %fusion), channel_id=1, source_target_pairs={{0,9},{1,8},{2,11},{3,10},{4,13},{5,12},{6,15},{7,14},{8,1},{9,0},... | collective-permute-start | bytes 24584 | tf_op jit(solution)/shard_map/ppermute | solution.py:219

commit v5 on v4

--- a/solution.py
+++ b/solution.py
@@ -1,4 +1,5 @@
 import functools
+import math
 
 import jax
 import jax.numpy as jnp
@@ -67,53 +68,96 @@
 STEPS = (((6, 4), ()), ((1, 0), ()), ((2, 5), (1,)), ((7, 3), (1, 2)))
 
 
+BELOW = {0: TAG_ROWS, 1: 6 * TAG_ROWS, 2: 6 * TAG_ROWS, 7: TAG_ROWS}
+
+
+def chunk_shape(block, send, width):
+    if block in TAGS:
+        return width // LANES * send + BELOW[block], LANES
+    return send, width
+
+
+def rows_in(chunk, send):
+    if chunk.shape[0] == send:
+        return chunk[...]
+    columns = [chunk[n : n + send, :] for n in range(0, chunk.shape[0] - send + 1, send)]
+    return jnp.concatenate(columns, axis=1)
+
+
+def digits_in(chunk, send):
+    first = chunk.shape[0] // send * send
+    return chunk[first : first + TAG_ROWS, :].astype(jnp.float32)
+
+
 def pack(send, blocks, unit, place, position, arrived, outs):
     rows, width = unit.shape
     if position is not None:
         parts = jnp.where(iota((16, rows), 0) == 0, position // TAG_BASE, position % TAG_BASE)
         parts = parts.astype(jnp.float32).astype(jnp.bfloat16)
+    digits = {k: digits_in(ref, send) for k, ref in arrived.items()}
 
     def chosen(block):
         return one_hot(iota((send, rows), 0) + block * send == place)
 
-    def tag_line(block):
-        found = dot(parts, chosen(block), ROWS_BY_ROWS)
-        return jnp.concatenate([found[0:1], found[1:2]], axis=1)
-
     for block, out in zip(blocks, outs):
-        out[:send, :] = dot(chosen(block), unit).astype(jnp.bfloat16)
-        if block in TAGS:
-            own, handed = TAGS[block]
-            lines = [tag_line(b) for b in own]
-            lines += [arrived[c][send:, : 2 * send][n : n + 1] for c, n in handed]
-            lines = [line.astype(jnp.float32) for line in lines]
-            lines.append(jnp.zeros((TAG_ROWS - len(lines), 2 * send), jnp.float32))
-            lines = jnp.concatenate(lines, axis=0)
-            rest = jnp.zeros((TAG_ROWS, width - 2 * send), jnp.float32)
-            out[send:, :] = jnp.concatenate([lines, rest], axis=1).astype(jnp.bfloat16)
-
-
-def unit_body(embeds_ref, unit_ref):
+        packed = dot(chosen(block), unit).astype(jnp.bfloat16)
+        if block not in TAGS:
+            out[...] = packed
+            continue
+        for n in range(width // LANES):
+            out[n * send : (n + 1) * send, :] = packed[:, n * LANES : (n + 1) * LANES]
+        own, handed = TAGS[block]
+        lines = []
+        for b in own:
+            found = dot(parts, chosen(b), ROWS_BY_ROWS)
+            lines.append((found[0:1], found[1:2]))
+        for c, n in handed:
+            lines.append((digits[c][n : n + 1], digits[c][n + TAG_ROWS // 2 :][:1]))
+        lines += [(jnp.zeros((1, send), jnp.float32),) * 2] * (TAG_ROWS // 2 - len(lines))
+        lines = [high for high, _ in lines] + [low for _, low in lines]
+        rest = jnp.zeros((BELOW[block] - TAG_ROWS, send), jnp.float32)
+        lines = jnp.concatenate([*lines, rest] if rest.size else lines, axis=0)
+        out[width // LANES * send :, :] = lines.astype(jnp.bfloat16)
+
+
+def steps_body(steps_ref):
+    steps_ref[...] = one_hot(iota(steps_ref.shape, 0) % LANES < iota(steps_ref.shape, 1))
+    steps_ref[LANES:, :] = jnp.ones((LANES, LANES), jnp.bfloat16)
+
+
+def ranks(which, steps):
+    lines, rows = which.shape
+    hits = jnp.where(which, 1.0, 0.0)
+    sums = jnp.zeros((lines, LANES), jnp.float32)
+    parts, totals = [], []
+    for n in range(0, rows, LANES):
+        parts.append(hits[:, n : n + LANES])
+        totals.append(sums)
+        sums = sums + parts[-1]
+    both = [jnp.concatenate(x, axis=0).astype(jnp.bfloat16) for x in (parts, totals)]
+    found = dot(jnp.concatenate(both, axis=1), steps)
+    return jnp.concatenate([found[n : n + lines] for n in range(0, found.shape[0], lines)], axis=1)
+
+
+def place_of_body(owners, send, steps_ref, cluster_ref, base_ref, place_ref):
+    owner = cluster_ref[...] ^ base_ref[...]
+    which = iota((max(owners, 16), cluster_ref.shape[1]), 0) == owner
+    rank = jnp.sum(jnp.where(which, ranks(which, steps_ref[...]), 0.0), axis=0, keepdims=True)
+    place_ref[...] = owner * send + rank.astype(jnp.int32)
+
+
+def first_body(send, blocks, embeds_ref, place_ref, unit_ref, *outs):
     values = embeds_ref[...].astype(jnp.float32)
     mean = jnp.sum(values * values, axis=1, keepdims=True) / values.shape[1]
-    unit_ref[...] = (values * lax.rsqrt(mean + EPS)).astype(jnp.bfloat16)
-
-
-def first_body(owners, send, blocks, unit_ref, cluster_ref, base_ref, place_ref, *outs):
-    rows = cluster_ref.shape[1]
-    owner = cluster_ref[...] ^ base_ref[...]
-    which = iota((max(owners, 16), rows), 0) == owner
-    before = one_hot(iota((rows, rows), 0) < iota((rows, rows), 1))
-    counts = dot(one_hot(which), before)
-    rank = jnp.sum(jnp.where(which, counts, 0.0), axis=0, keepdims=True)
-    place = owner * send + rank.astype(jnp.int32)
-    place_ref[...] = place
+    unit = (values * lax.rsqrt(mean + EPS)).astype(jnp.bfloat16)
+    unit_ref[...] = unit
+    place = place_ref[...]
     if blocks:
-        pack(send, blocks, unit_ref[...], place, None, {}, outs)
+        pack(send, blocks, unit, place, None, {}, outs)
     else:
         (out,) = outs
-        chosen = one_hot(iota((out.shape[0], rows), 0) == place)
-        out[...] = dot(chosen, unit_ref[...]).astype(jnp.bfloat16)
+        chosen = one_hot(iota((out.shape[0], place.shape[1]), 0) == place)
+        out[...] = dot(chosen, unit).astype(jnp.bfloat16)
 
 
 def pack_body(send, blocks, unit_ref, place_ref, order_ref, arrived, *outs):
@@ -124,10 +168,11 @@
 def tags_of(chunks, tags, send):
     if tags:
         return tags[0][...]
+    digits = {k: digits_in(chunks[k], send) for k in TAGS}
     found = []
-    for chunk, line in TAG_LINE:
-        lines = chunks[chunk][send:, : 2 * send].astype(jnp.float32)[line : line + 1]
-        found.append(lines[:, :send] * TAG_BASE + lines[:, send:])
+    for k, n in TAG_LINE:
+        low = n + TAG_ROWS // 2
+        found.append(digits[k][n : n + 1] * TAG_BASE + digits[k][low : low + 1])
     found = jnp.concatenate(found, axis=1).astype(jnp.int32)
     return jnp.where(found == 0, EMPTY, found - 1)
 
@@ -135,17 +180,22 @@
 def rows_of(chunks, send):
     if 1 not in chunks:
         return chunks[0][...]
-    return jnp.concatenate([chunks[k][:send, :] for k in range(8)], axis=0)
-
-
-def border_body(send, chunks, want_ref, tags, keep_ref, give_ref, head_ref):
+    return jnp.concatenate([rows_in(chunks[k], send) for k in range(8)], axis=0)
+
+
+def give_body(send, chunks, want_ref, tags, give_ref):
+    chosen = one_hot(want_ref[BORDER // 2 :, :] == tags_of(chunks, tags, send))
+    give_ref[...] = dot(chosen, rows_of(chunks, send)).astype(jnp.bfloat16)
+
+
+def keep_body(send, chunks, want_ref, tags, keep_ref, head_ref):
     tags = tags_of(chunks, tags, send)
     first = iota((head_ref.shape[0], tags.shape[1]), 0)
-    chosen = jnp.concatenate([one_hot(want_ref[...] == tags), one_hot(first == tags)], axis=0)
+    chosen = [one_hot(want_ref[: BORDER // 2, :] == tags), one_hot(first == tags)]
+    chosen = jnp.concatenate(chosen, axis=0)
     picked = dot(chosen, rows_of(chunks, send)).astype(jnp.bfloat16)
-    keep_ref[...] = picked[: BORDER // 2]
-    give_ref[...] = picked[BORDER // 2 : BORDER]
-    head_ref[...] = picked[BORDER:]
+    keep_ref[...] = picked[: keep_ref.shape[0]]
+    head_ref[...] = picked[keep_ref.shape[0] :]
 
 
 def place_body(send, chunks, tags, *mine_refs):
@@ -160,7 +210,8 @@
 
 
 def weigh(products, width):
-    return jnp.exp((products / width - 1.0) / SCALE)
+    by = math.log2(math.e) / SCALE
+    return jnp.exp2(products * (by / width) - by)
 
 
 def near_body(mine_refs, other_refs, near_ref):
@@ -237,26 +288,33 @@
     order_row = order_in.reshape(1, rows)
 
     def shapes(blocks):
-        sizes = [(send + TAG_ROWS * (b in TAGS), width) for b in blocks] or [(owners * send, width)]
+        sizes = [chunk_shape(b, send, width) for b in blocks] or [(owners * send, width)]
         return [jax.ShapeDtypeStruct(size, jnp.bfloat16) for size in sizes]
 
-    unit = call(unit_body, jax.ShapeDtypeStruct((rows, width), jnp.bfloat16), 0, embeds)
+    steps = call(steps_body, jax.ShapeDtypeStruct((2 * LANES, LANES), jnp.bfloat16), 2 * 10**9)
+    place = call(
+        functools.partial(place_of_body, owners, send),
+        jax.ShapeDtypeStruct((1, rows), jnp.int32),
+        10**8,
+        steps,
+        cluster_row,
+        base,
+    )
 
     def first(blocks):
         return call(
-            functools.partial(first_body, owners, send, blocks),
-            [jax.ShapeDtypeStruct((1, rows), jnp.int32), *shapes(blocks)],
+            functools.partial(first_body, send, blocks),
+            [jax.ShapeDtypeStruct((rows, width), jnp.bfloat16), *shapes(blocks)],
             2 * rows * rows * width,
-            unit,
-            cluster_row,
-            base,
+            embeds,
+            place,
         )
 
     if paired:
         chunks = {}
         for blocks, needed in STEPS:
             if not chunks:
-                place, *packed = first(blocks)
+                unit, *packed = first(blocks)
             else:
                 handed = {k: chunks[k] for k in needed}
                 packed = call(
@@ -286,21 +344,30 @@
         found = jnp.sum(jnp.where(hit, (every % HALF - EMPTY)[:, None, :], 0), axis=2) + EMPTY
         tags = [found.reshape(1, owners * send)]
 
-    want = border_idx.reshape(BORDER, 1) - side * HALF
-    want = jnp.where(side == 0, want, jnp.roll(want, BORDER // 2, axis=0))
     by = clus_count // 2
     opposite = [
         (2 * i + r, 2 * ((i + by) % clus_count) + 1 - r) for i in range(clus_count) for r in range(2)
     ]
+    want = border_idx.reshape(BORDER, 1) - side * HALF
+    want = jnp.where(side == 0, want, jnp.roll(want, BORDER // 2, axis=0))
     part = jax.ShapeDtypeStruct((BORDER // 2, width), jnp.bfloat16)
     pieces = [jax.ShapeDtypeStruct((count, width), jnp.bfloat16) for count in PIECES]
-    keep, give, head = call(
-        functools.partial(border_body, send),
-        [part, part, pieces[0]],
-        2 * BORDER * owners * send * width,
+    give = call(
+        functools.partial(give_body, send),
+        part,
+        BORDER * owners * send * width,
         chunks,
         want,
         tags,
+    )
+    keep, head = call(
+        functools.partial(keep_body, send),
+        [part, pieces[0]],
+        BORDER * owners * send * width,
+        chunks,
+        want,
+        tags,
+        after=[give],
     )
     chosen = keep + lax.ppermute(give, "rep", swap)
     tile = lax.ppermute(chosen, ("clus", "rep"), opposite)
@@ -310,7 +377,7 @@
         2 * HALF * owners * send * width,
         chunks,
         tags,
-        after=[give],
+        after=[keep],
     )
     mine = [head, *rest]
     other = [lax.ppermute(part, "rep", swap) for part in mine]

time: 70 us -> 68.3 us (0.976)
  waiting for transfers between devices: 37.4 us -> 36.4 us
  local copies, waits for them, and re-layouts: 2.78 us -> 1.86 us
    unnamed x8, local copies, waits for them, and re-layouts: 2.49 us -> 1.57 us
    pallas_call x10 -> x12, Pallas kernels: 6.37 us -> 6.43 us  [call(): pl.pallas_call(kernel, out_shape=out_shape, in_specs=[spec] * count + [pl...]
  transfers between devices with their start and end apart: 18 -> 18, of which waited for: 14 -> 14; matrix products, arithmetic and copies ran while one was open for 1% -> 1% of each run, Pallas kernels for 5% -> 6%
where the time goes in v5:
time: 68.3 us; the launch traced here: 68.1 us
  waiting for transfers between devices  36.4 us (53%)
  starting transfers between devices  23.1 us (34%)
  Pallas kernels  6.43 us (9%)
  local copies, waits for them, and re-layouts  1.86 us (3%)
    ppermute x7, waiting for transfers between devices, toward(): return lax.ppermute(x, OWNERS, [(i, i ^ flip) for i in range(owners)])  20.4 us
    ppermute x7, starting transfers between devices, toward(): return lax.ppermute(x, OWNERS, [(i, i ^ flip) for i in range(owners)])  15.7 us
    ppermute x3, waiting for transfers between devices, across(): return lax.ppermute(x, (*OWNERS, 'rep'), pairs)  8.36 us
    pallas_call x12, Pallas kernels, call(): pl.pallas_call(kernel, out_shape=out_shape, in_specs=[spec] * count + [pl...  6.43 us
    ppermute x1, waiting for transfers between devices, per_device(): tile = lax.ppermute(chosen, ('clus', 'rep'), opposite)  5.03 us
    ppermute x1, starting transfers between devices, per_device(): tile = lax.ppermute(chosen, ('clus', 'rep'), opposite)  3.53 us
    ppermute x3, starting transfers between devices, across(): return lax.ppermute(x, (*OWNERS, 'rep'), pairs)  1.95 us
    ppermute x5, starting transfers between devices, per_device(): other = [lax.ppermute(part, 'rep', swap) for part in mine]  1.64 us
  transfers between devices with their start and end apart: 18, of which 14 were waited for; matrix products, arithmetic and copies ran while one was open for 1% of the time, Pallas kernels for 6%

profile of v5, /device:TPU:0, one launch (start us, length us, event | category | flops | bytes accessed | tf_op | source)
XLA Modules:
  0.0 68.1 jit_solution(3921168272726637158)
XLA Ops:
  0.0 0.0 copy-start.2
  0.0 0.0 copy-start.1
  0.0 0.7 %copy-done.1 = s32[512]{0:T(512)S(1)} copy-done((s32[512]{0:T(512)S(1)}, s32[512]{0:T(512)}, u32[]{:S(2)}) %copy-start.1) | copy-done | bytes 2072
  0.8 0.2 shard_map.47.refs_1_
  1.0 0.1 copy-done.2
  1.1 0.6 shard_map.48
  1.7 4.1 %collective-permute-start.3 = (bf16[128,768]{1,0:T(8,128)(2,1)S(1)}, bf16[128,768]{1,0:T(8,128)(2,1)S(1)}, u32[]{:S(2)}, u32[]{:S(2)}) collective-permute-start(bf16[128,768]{1,0:T(8,128)(2,1)S(1)} %get-tuple-element.27), channel_id=1, source_target_pairs={{0,8},{2,10},{4,12},{6,14},{8,0},{10,2},{12,4},{14,6},{1,9},{3,11}... | collective-permute-start | bytes 589832 | tf_op jit(solution)/shard_map/ppermute | solution.py:266
  5.8 0.0 copy-start
  5.8 1.3 %collective-permute-start.5 = (bf16[128,768]{1,0:T(8,128)(2,1)S(1)}, bf16[128,768]{1,0:T(8,128)(2,1)S(1)}, u32[]{:S(2)}, u32[]{:S(2)}) collective-permute-start(bf16[128,768]{1,0:T(8,128)(2,1)S(1)} %get-tuple-element.29), channel_id=1, source_target_pairs={{0,12},{2,14},{4,8},{6,10},{8,4},{10,6},{12,0},{14,2},{1,13},{3,15... | collective-permute-start | bytes 589832 | tf_op jit(solution)/shard_map/ppermute | solution.py:266
  7.2 0.0 copy-done
  7.2 0.5 shard_map.49
  7.7 1.6 %collective-permute-start = (bf16[816,128]{1,0:T(8,128)(2,1)S(1)}, bf16[816,128]{1,0:T(8,128)(2,1)S(1)}, u32[]{:S(2)}, u32[]{:S(2)}) collective-permute-start(bf16[816,128]{1,0:T(8,128)(2,1)S(1)} %get-tuple-element.24), channel_id=1, source_target_pairs={{0,2},{2,0},{4,6},{6,4},{8,10},{10,8},{12,14},{14,12},{1,3},{3,1},... | collective-permute-start | bytes 626696 | tf_op jit(solution)/shard_map/ppermute | solution.py:266
  9.3 0.0 copy-start.3
  9.3 0.7 copy-done.3
  10.0 0.1 copy.11
  10.1 4.0 %collective-permute-done.refs_3_.refs_1_ = bf16[816,128]{1,0:T(8,128)(2,1)S(1)} collective-permute-done((bf16[816,128]{1,0:T(8,128)(2,1)S(1)}, bf16[816,128]{1,0:T(8,128)(2,1)S(1)}, u32[]{:S(2)}, u32[]{:S(2)}) %collective-permute-start) | collective-permute-done | bytes 208928 | tf_op jit(solution)/shard_map/ppermute | solution.py:266
  14.2 0.4 shard_map.50
  14.6 1.2 %collective-permute-start.1 = (bf16[816,128]{1,0:T(8,128)(2,1)S(1)}, bf16[816,128]{1,0:T(8,128)(2,1)S(1)}, u32[]{:S(2)}, u32[]{:S(2)}) collective-permute-start(bf16[816,128]{1,0:T(8,128)(2,1)S(1)} %get-tuple-element.25), channel_id=1, source_target_pairs={{0,4},{2,6},{4,0},{6,2},{8,12},{10,14},{12,8},{14,10},{1,5},{3,7},... | collective-permute-start | bytes 626696 | tf_op jit(solution)/shard_map/ppermute | solution.py:266
  15.8 0.1 copy.10
  16.0 2.8 %collective-permute-start.4 = (bf16[128,768]{1,0:T(8,128)(2,1)S(1)}, bf16[128,768]{1,0:T(8,128)(2,1)S(1)}, u32[]{:S(2)}, u32[]{:S(2)}) collective-permute-start(bf16[128,768]{1,0:T(8,128)(2,1)S(1)} %get-tuple-element.28), channel_id=1, source_target_pairs={{0,10},{2,8},{4,14},{6,12},{8,2},{10,0},{12,6},{14,4},{1,11},{3,9}... | collective-permute-start | bytes 589832 | tf_op jit(solution)/shard_map/ppermute | solution.py:266
  18.8 4.8 %collective-permute-done.1.refs_4_.refs_2_ = bf16[816,128]{1,0:T(8,128)(2,1)S(1)} collective-permute-done((bf16[816,128]{1,0:T(8,128)(2,1)S(1)}, bf16[816,128]{1,0:T(8,128)(2,1)S(1)}, u32[]{:S(2)}, u32[]{:S(2)}) %collective-permute-start.1) | collective-permute-done | bytes 208928 | tf_op jit(solution)/shard_map/ppermute | solution.py:266
  23.6 0.4 shard_map.51
  24.1 1.0 %collective-permute-start.2 = (bf16[128,768]{1,0:T(8,128)(2,1)S(1)}, bf16[128,768]{1,0:T(8,128)(2,1)S(1)}, u32[]{:S(2)}, u32[]{:S(2)}) collective-permute-start(bf16[128,768]{1,0:T(8,128)(2,1)S(1)} %get-tuple-element.26), channel_id=1, source_target_pairs={{0,6},{2,4},{4,2},{6,0},{8,14},{10,12},{12,10},{14,8},{1,7},{3,5},... | collective-permute-start | bytes 589832 | tf_op jit(solution)/shard_map/ppermute | solution.py:266
  25.1 3.6 %collective-permute-start.6 = (bf16[776,128]{1,0:T(8,128)(2,1)S(1)}, bf16[776,128]{1,0:T(8,128)(2,1)S(1)}, u32[]{:S(2)}, u32[]{:S(2)}) collective-permute-start(bf16[776,128]{1,0:T(8,128)(2,1)S(1)} %get-tuple-element.30), channel_id=1, source_target_pairs={{0,14},{2,12},{4,10},{6,8},{8,6},{10,4},{12,2},{14,0},{1,15},{3,13... | collective-permute-start | bytes 595976 | tf_op jit(solution)/shard_map/ppermute | solution.py:266
  28.7 0.0 collective-permute-done.3.refs_4_
  28.7 0.0 collective-permute-done.5.refs_6_
  28.7 9.5 %collective-permute-done.4.refs_5_ = bf16[128,768]{1,0:T(8,128)(2,1)S(1)} collective-permute-done((bf16[128,768]{1,0:T(8,128)(2,1)S(1)}, bf16[128,768]{1,0:T(8,128)(2,1)S(1)}, u32[]{:S(2)}, u32[]{:S(2)}) %collective-permute-start.4) | collective-permute-done | bytes 196640 | tf_op jit(solution)/shard_map/ppermute | solution.py:266
  38.2 2.0 %collective-permute-done.2.refs_3_ = bf16[128,768]{1,0:T(8,128)(2,1)S(1)} collective-permute-done((bf16[128,768]{1,0:T(8,128)(2,1)S(1)}, bf16[128,768]{1,0:T(8,128)(2,1)S(1)}, u32[]{:S(2)}, u32[]{:S(2)}) %collective-permute-start.2) | collective-permute-done | bytes 196640 | tf_op jit(solution)/shard_map/ppermute | solution.py:266
  40.2 0.0 collective-permute-done.6.refs_7_
  40.2 0.4 shard_map.52.refs_9_
  40.7 0.1 collective-permute-start.12
  40.7 0.5 shard_map.53
  41.3 0.6 collective-permute-start.7
  41.8 0.3 collective-permute-done.12
  42.2 0.1 add.10
  42.2 3.5 %collective-permute-start.13 = (bf16[128,768]{1,0:T(8,128)(2,1)S(1)}, bf16[128,768]{1,0:T(8,128)(2,1)S(1)}, u32[]{:S(2)}, u32[]{:S(2)}) collective-permute-start(bf16[128,768]{1,0:T(8,128)(2,1)S(1)} %add.10), channel_id=1, source_target_pairs={{0,9},{1,8},{4,13},{5,12},{8,1},{9,0},{12,5},{13,4},{2,11},{3,10},... | collective-permute-start | bytes 589832 | tf_op jit(solution)/shard_map/ppermute | solution.py:373
  45.8 0.9 %shard_map.54 = (bf16[112,768]{1,0:T(8,128)(2,1)S(1)}, bf16[112,768]{1,0:T(8,128)(2,1)S(1)}, bf16[112,768]{1,0:T(8,128)(2,1)S(1)}, bf16[112,768]{1,0:T(8,128)(2,1)S(1)}) custom-call(bf16[776,128]{1,0:T(8,128)(2,1)S(1)} %get-tuple-element.23.refs_0_, bf16[816,128]{1,0:T(8,128)(2,1)S(1)} %collective-permute-done.refs_3_.refs_1_, ...), custom_call_target="tpu_custom_call" | custom-call | flops 805306368 | bytes 2289664 | tf_op jit(solution)/shard_map/pallas_call | solution.py:41
  46.7 0.4 collective-permute-start.8
  47.1 0.1 collective-permute-start.9
  47.2 0.4 collective-permute-start.10
  47.6 0.0 collective-permute-done.7.refs_5_
  47.6 0.1 collective-permute-start.11
  47.8 0.4 collective-permute-done.8.refs_6_
  48.1 0.4 collective-permute-done.9.refs_7_
  48.5 0.2 collective-permute-done.10.refs_8_
  48.8 0.3 collective-permute-done.11.refs_9_
  49.0 1.0 %shard_map.55.refs_11_ = f32[1,512]{1,0:T(1,128)S(1)} custom-call(bf16[64,768]{1,0:T(8,128)(2,1)S(1)} %get-tuple-element.31.refs_0_, bf16[112,768]{1,0:T(8,128)(2,1)S(1)} %get-tuple-element.33.refs_1_, bf16[112,768]{1,0:T(8,128)(2,1)S(1)} %get-tuple-element.34.refs_2_, bf16[112,768]{1,0:T(8,128)(2,1)S(1)} %get-tuple-element.35.refs_3_, ...), custom_call_target="tpu_custom_call" | custom-call | tf_op jit(solution)/shard_map/pallas_call | solution.py:41
  50.1 5.0 %collective-permute-done.13.refs_10_ = bf16[128,768]{1,0:T(8,128)(2,1)S(1)} collective-permute-done((bf16[128,768]{1,0:T(8,128)(2,1)S(1)}, bf16[128,768]{1,0:T(8,128)(2,1)S(1)}, u32[]{:S(2)}, u32[]{:S(2)}) %collective-permute-start.13) | collective-permute-done | bytes 196640 | tf_op jit(solution)/shard_map/ppermute | solution.py:373
  55.1 0.6 shard_map.56
  55.8 0.2 collective-permute-start.14
  56.0 1.0 %collective-permute-done.14 = f32[8,128]{1,0:T(8,128)S(1)} collective-permute-done((f32[8,128]{1,0:T(8,128)S(1)}, f32[8,128]{1,0:T(8,128)S(1)}, u32[]{:S(2)}, u32[]{:S(2)}) %collective-permute-start.14) | collective-permute-done | bytes 4128 | tf_op jit(solution)/shard_map/ppermute | solution.py:401
  57.0 0.4 collective-permute-start.15
  57.4 2.7 %collective-permute-done.15 = f32[8,128]{1,0:T(8,128)S(1)} collective-permute-done((f32[8,128]{1,0:T(8,128)S(1)}, f32[8,128]{1,0:T(8,128)S(1)}, u32[]{:S(2)}, u32[]{:S(2)}) %collective-permute-start.15) | collective-permute-done | bytes 4128 | tf_op jit(solution)/shard_map/ppermute | solution.py:270
  60.2 0.1 collective-permute-start.16
  60.3 3.0 %collective-permute-done.16 = f32[16,128]{1,0:T(8,128)S(1)} collective-permute-done((f32[16,128]{1,0:T(8,128)S(1)}, f32[16,128]{1,0:T(8,128)S(1)}, u32[]{:S(2)}, u32[]{:S(2)}) %collective-permute-start.16) | collective-permute-done | bytes 8224 | tf_op jit(solution)/shard_map/ppermute | solution.py:270
  63.3 1.4 %collective-permute-start.17 = (f32[16,128]{1,0:T(8,128)S(1)}, f32[16,128]{1,0:T(8,128)S(1)}, u32[]{:S(2)}, u32[]{:S(2)}) collective-permute-start(f32[16,128]{1,0:T(8,128)S(1)} %fusion), channel_id=1, source_target_pairs={{0,9},{1,8},{2,11},{3,10},{4,13},{5,12},{6,15},{7,14},{8,1},{9,0},... | collective-permute-start | bytes 24584 | tf_op jit(solution)/shard_map/ppermute | solution.py:270
  64.7 2.7 %collective-permute-done.17 = f32[16,128]{1,0:T(8,128)S(1)} collective-permute-done((f32[16,128]{1,0:T(8,128)S(1)}, f32[16,128]{1,0:T(8,128)S(1)}, u32[]{:S(2)}, u32[]{:S(2)}) %collective-permute-start.17) | collective-permute-done | bytes 8224 | tf_op jit(solution)/shard_map/ppermute | solution.py:270
  67.4 0.7 %shard_map.57 = f32[4,128]{1,0:T(4,128)} custom-call(f32[32,128]{1,0:T(8,128)S(1)} %pad_maximum_fusion.refs_0_, s32[4,128]{1,0:T(4,128)S(1)} %bitcast.17, s32[4,128]{1,0:T(4,128)S(1)} %bitcast.15, s32[1,1]{1,0:T(1,128)} %bitcast.1.refs_2_.refs_3_), custom_call_target="tpu_custom_call" | custom-call | flops 4096 | bytes 22532 | tf_op jit(solution)/shard_map/pallas_call | solution.py:41
  (15 shorter events, 0.1 us)
Async XLA Ops:
  0.0 1.1 %copy-start.2 = (bf16[512,768]{1,0:T(8,128)(2,1)S(1)}, bf16[512,768]{1,0:T(8,128)(2,1)}, u32[]{:S(2)}) copy-start(bf16[512,768]{1,0:T(8,128)(2,1)} %refs_0_.1) | copy-start | bytes 2359300
  0.0 0.8 %copy-start.1 = (s32[512]{0:T(512)S(1)}, s32[512]{0:T(512)}, u32[]{:S(2)}) copy-start(s32[512]{0:T(512)} %param.6) | copy-start | bytes 6148
  1.7 27.0 %collective-permute-start.3 = (bf16[128,768]{1,0:T(8,128)(2,1)S(1)}, bf16[128,768]{1,0:T(8,128)(2,1)S(1)}, u32[]{:S(2)}, u32[]{:S(2)}) collective-permute-start(bf16[128,768]{1,0:T(8,128)(2,1)S(1)} %get-tuple-element.27), channel_id=1, source_target_pairs={{0,8},{2,10},{4,12},{6,14},{8,0},{10,2},{12,4},{14,6},{1,9},{3,11}... | collective-permute-start | bytes 589832 | tf_op jit(solution)/shard_map/ppermute | solution.py:266
  5.8 1.4 %copy-start = (s32[512]{0:T(512)S(1)}, s32[512]{0:T(512)}, u32[]{:S(2)}) copy-start(s32[512]{0:T(512)} %param.7) | copy-start | bytes 6148
  5.8 22.9 %collective-permute-start.5 = (bf16[128,768]{1,0:T(8,128)(2,1)S(1)}, bf16[128,768]{1,0:T(8,128)(2,1)S(1)}, u32[]{:S(2)}, u32[]{:S(2)}) collective-permute-start(bf16[128,768]{1,0:T(8,128)(2,1)S(1)} %get-tuple-element.29), channel_id=1, source_target_pairs={{0,12},{2,14},{4,8},{6,10},{8,4},{10,6},{12,0},{14,2},{1,13},{3,15... | collective-permute-start | bytes 589832 | tf_op jit(solution)/shard_map/ppermute | solution.py:266
  7.7 6.4 %collective-permute-start = (bf16[816,128]{1,0:T(8,128)(2,1)S(1)}, bf16[816,128]{1,0:T(8,128)(2,1)S(1)}, u32[]{:S(2)}, u32[]{:S(2)}) collective-permute-start(bf16[816,128]{1,0:T(8,128)(2,1)S(1)} %get-tuple-element.24), channel_id=1, source_target_pairs={{0,2},{2,0},{4,6},{6,4},{8,10},{10,8},{12,14},{14,12},{1,3},{3,1},... | collective-permute-start | bytes 626696 | tf_op jit(solution)/shard_map/ppermute | solution.py:266
  9.3 0.7 copy-start.3
  14.6 9.0 %collective-permute-start.1 = (bf16[816,128]{1,0:T(8,128)(2,1)S(1)}, bf16[816,128]{1,0:T(8,128)(2,1)S(1)}, u32[]{:S(2)}, u32[]{:S(2)}) collective-permute-start(bf16[816,128]{1,0:T(8,128)(2,1)S(1)} %get-tuple-element.25), channel_id=1, source_target_pairs={{0,4},{2,6},{4,0},{6,2},{8,12},{10,14},{12,8},{14,10},{1,5},{3,7},... | collective-permute-start | bytes 626696 | tf_op jit(solution)/shard_map/ppermute | solution.py:266
  16.0 22.3 %collective-permute-start.4 = (bf16[128,768]{1,0:T(8,128)(2,1)S(1)}, bf16[128,768]{1,0:T(8,128)(2,1)S(1)}, u32[]{:S(2)}, u32[]{:S(2)}) collective-permute-start(bf16[128,768]{1,0:T(8,128)(2,1)S(1)} %get-tuple-element.28), channel_id=1, source_target_pairs={{0,10},{2,8},{4,14},{6,12},{8,2},{10,0},{12,6},{14,4},{1,11},{3,9}... | collective-permute-start | bytes 589832 | tf_op jit(solution)/shard_map/ppermute | solution.py:266
  24.1 16.2 %collective-permute-start.2 = (bf16[128,768]{1,0:T(8,128)(2,1)S(1)}, bf16[128,768]{1,0:T(8,128)(2,1)S(1)}, u32[]{:S(2)}, u32[]{:S(2)}) collective-permute-start(bf16[128,768]{1,0:T(8,128)(2,1)S(1)} %get-tuple-element.26), channel_id=1, source_target_pairs={{0,6},{2,4},{4,2},{6,0},{8,14},{10,12},{12,10},{14,8},{1,7},{3,5},... | collective-permute-start | bytes 589832 | tf_op jit(solution)/shard_map/ppermute | solution.py:266
  25.1 15.2 %collective-permute-start.6 = (bf16[776,128]{1,0:T(8,128)(2,1)S(1)}, bf16[776,128]{1,0:T(8,128)(2,1)S(1)}, u32[]{:S(2)}, u32[]{:S(2)}) collective-permute-start(bf16[776,128]{1,0:T(8,128)(2,1)S(1)} %get-tuple-element.30), channel_id=1, source_target_pairs={{0,14},{2,12},{4,10},{6,8},{8,6},{10,4},{12,2},{14,0},{1,15},{3,13... | collective-permute-start | bytes 595976 | tf_op jit(solution)/shard_map/ppermute | solution.py:266
  40.7 1.5 %collective-permute-start.12 = (bf16[128,768]{1,0:T(8,128)(2,1)S(1)}, bf16[128,768]{1,0:T(8,128)(2,1)S(1)}, u32[]{:S(2)}, u32[]{:S(2)}) collective-permute-start(bf16[128,768]{1,0:T(8,128)(2,1)S(1)} %shard_map.52.refs_9_), channel_id=1, source_target_pairs={{0,1},{1,0},{2,3},{3,2},{4,5},{5,4},{6,7},{7,6},{8,9},{9,8},{10,11... | collective-permute-start | bytes 589832 | tf_op jit(solution)/shard_map/ppermute | solution.py:372
  41.3 6.3 %collective-permute-start.7 = (bf16[64,768]{1,0:T(8,128)(2,1)S(1)}, bf16[64,768]{1,0:T(8,128)(2,1)S(1)}, u32[]{:S(2)}, u32[]{:S(2)}) collective-permute-start(bf16[64,768]{1,0:T(8,128)(2,1)S(1)} %get-tuple-element.31.refs_0_), channel_id=1, source_target_pairs={{0,1},{1,0},{2,3},{3,2},{4,5},{5,4},{6,7},{7,6},{8,9},{9,8},{10,11... | collective-permute-start | bytes 294920 | tf_op jit(solution)/shard_map/ppermute | solution.py:383
  42.2 12.9 %collective-permute-start.13 = (bf16[128,768]{1,0:T(8,128)(2,1)S(1)}, bf16[128,768]{1,0:T(8,128)(2,1)S(1)}, u32[]{:S(2)}, u32[]{:S(2)}) collective-permute-start(bf16[128,768]{1,0:T(8,128)(2,1)S(1)} %add.10), channel_id=1, source_target_pairs={{0,9},{1,8},{4,13},{5,12},{8,1},{9,0},{12,5},{13,4},{2,11},{3,10},... | collective-permute-start | bytes 589832 | tf_op jit(solution)/shard_map/ppermute | solution.py:373
  46.7 1.5 %collective-permute-start.8 = (bf16[112,768]{1,0:T(8,128)(2,1)S(1)}, bf16[112,768]{1,0:T(8,128)(2,1)S(1)}, u32[]{:S(2)}, u32[]{:S(2)}) collective-permute-start(bf16[112,768]{1,0:T(8,128)(2,1)S(1)} %get-tuple-element.33.refs_1_), channel_id=1, source_target_pairs={{0,1},{1,0},{2,3},{3,2},{4,5},{5,4},{6,7},{7,6},{8,9},{9,8},{10,11... | collective-permute-start | bytes 516104 | tf_op jit(solution)/shard_map/ppermute | solution.py:383
  47.1 1.4 %collective-permute-start.9 = (bf16[112,768]{1,0:T(8,128)(2,1)S(1)}, bf16[112,768]{1,0:T(8,128)(2,1)S(1)}, u32[]{:S(2)}, u32[]{:S(2)}) collective-permute-start(bf16[112,768]{1,0:T(8,128)(2,1)S(1)} %get-tuple-element.34.refs_2_), channel_id=1, source_target_pairs={{0,1},{1,0},{2,3},{3,2},{4,5},{5,4},{6,7},{7,6},{8,9},{9,8},{10,11... | collective-permute-start | bytes 516104 | tf_op jit(solution)/shard_map/ppermute | solution.py:383
  47.2 1.5 %collective-permute-start.10 = (bf16[112,768]{1,0:T(8,128)(2,1)S(1)}, bf16[112,768]{1,0:T(8,128)(2,1)S(1)}, u32[]{:S(2)}, u32[]{:S(2)}) collective-permute-start(bf16[112,768]{1,0:T(8,128)(2,1)S(1)} %get-tuple-element.35.refs_3_), channel_id=1, source_target_pairs={{0,1},{1,0},{2,3},{3,2},{4,5},{5,4},{6,7},{7,6},{8,9},{9,8},{10,11... | collective-permute-start | bytes 516104 | tf_op jit(solution)/shard_map/ppermute | solution.py:383
  47.6 1.4 %collective-permute-start.11 = (bf16[112,768]{1,0:T(8,128)(2,1)S(1)}, bf16[112,768]{1,0:T(8,128)(2,1)S(1)}, u32[]{:S(2)}, u32[]{:S(2)}) collective-permute-start(bf16[112,768]{1,0:T(8,128)(2,1)S(1)} %get-tuple-element.36.refs_4_), channel_id=1, source_target_pairs={{0,1},{1,0},{2,3},{3,2},{4,5},{5,4},{6,7},{7,6},{8,9},{9,8},{10,11... | collective-permute-start | bytes 516104 | tf_op jit(solution)/shard_map/ppermute | solution.py:383
  55.8 1.2 %collective-permute-start.14 = (f32[8,128]{1,0:T(8,128)S(1)}, f32[8,128]{1,0:T(8,128)S(1)}, u32[]{:S(2)}, u32[]{:S(2)}) collective-permute-start(f32[8,128]{1,0:T(8,128)S(1)} %pad_maximum_fusion.3), channel_id=1, source_target_pairs={{0,1},{1,0},{2,3},{3,2},{4,5},{5,4},{6,7},{7,6},{8,9},{9,8},{10,11... | collective-permute-start | bytes 12296 | tf_op jit(solution)/shard_map/ppermute | solution.py:401
  57.0 3.1 %collective-permute-start.15 = (f32[8,128]{1,0:T(8,128)S(1)}, f32[8,128]{1,0:T(8,128)S(1)}, u32[]{:S(2)}, u32[]{:S(2)}) collective-permute-start(f32[8,128]{1,0:T(8,128)S(1)} %pad_maximum_fusion.4), channel_id=1, source_target_pairs={{0,3},{1,2},{2,1},{3,0},{4,7},{5,6},{6,5},{7,4},{8,11},{9,10},{10,... | collective-permute-start | bytes 12296 | tf_op jit(solution)/shard_map/ppermute | solution.py:270
  60.2 3.1 %collective-permute-start.16 = (f32[16,128]{1,0:T(8,128)S(1)}, f32[16,128]{1,0:T(8,128)S(1)}, u32[]{:S(2)}, u32[]{:S(2)}) collective-permute-start(f32[16,128]{1,0:T(8,128)S(1)} %pad_maximum_fusion.1), channel_id=1, source_target_pairs={{0,5},{1,4},{2,7},{3,6},{4,1},{5,0},{6,3},{7,2},{8,13},{9,12},{10,... | collective-permute-start | bytes 24584 | tf_op jit(solution)/shard_map/ppermute | solution.py:270
  63.3 4.1 %collective-permute-start.17 = (f32[16,128]{1,0:T(8,128)S(1)}, f32[16,128]{1,0:T(8,128)S(1)}, u32[]{:S(2)}, u32[]{:S(2)}) collective-permute-start(f32[16,128]{1,0:T(8,128)S(1)} %fusion), channel_id=1, source_target_pairs={{0,9},{1,8},{2,11},{3,10},{4,13},{5,12},{6,15},{7,14},{8,1},{9,0},... | collective-permute-start | bytes 24584 | tf_op jit(solution)/shard_map/ppermute | solution.py:270

commit v6 on v5

--- a/solution.py
+++ b/solution.py
@@ -60,15 +60,15 @@
 
 TAGS = {
     0: ((0,), ()),
-    1: ((1, 3, 6, 4), ()),
-    2: ((2, 5), ((1, 1), (1, 3))),
-    7: ((7,), ((1, 2), (2, 1), (2, 3))),
+    1: ((1, 3, 7, 5), ()),
+    2: ((2, 4), ((1, 1), (1, 3))),
+    6: ((6,), ((1, 2), (2, 1), (2, 3))),
 }
-TAG_LINE = ((0, 0), (1, 0), (2, 0), (2, 2), (7, 3), (7, 2), (7, 1), (7, 0))
-STEPS = (((6, 4), ()), ((1, 0), ()), ((2, 5), (1,)), ((7, 3), (1, 2)))
-
-
-BELOW = {0: TAG_ROWS, 1: 6 * TAG_ROWS, 2: 6 * TAG_ROWS, 7: TAG_ROWS}
+TAG_LINE = ((0, 0), (1, 0), (2, 0), (2, 2), (6, 2), (6, 3), (6, 0), (6, 1))
+STEPS = (((7, 4), ()), ((1, 0), ()), ((2, 5), (1,)), ((6, 3), (1, 2)))
+
+
+BELOW = {0: TAG_ROWS, 1: 6 * TAG_ROWS, 2: 6 * TAG_ROWS, 6: TAG_ROWS}
 
 
 def chunk_shape(block, send, width):

time: 68.3 us -> 67.2 us (0.984)
  starting transfers between devices: 23.1 us -> 18.1 us
  waiting for transfers between devices: 36.4 us -> 40.3 us
    ppermute x7, starting transfers between devices: 15.7 us -> 10.6 us  [toward(): return lax.ppermute(x, OWNERS, [(i, i ^ flip) for i in range(owners)])]
    ppermute x7, waiting for transfers between devices: 20.4 us -> 25.1 us  [toward(): return lax.ppermute(x, OWNERS, [(i, i ^ flip) for i in range(owners)])]
where the time goes in v6:
time: 67.2 us; the launch traced here: 67 us
  waiting for transfers between devices  40.3 us (60%)
  starting transfers between devices  18.1 us (27%)
  Pallas kernels  6.45 us (10%)
  local copies, waits for them, and re-layouts  1.86 us (3%)
    ppermute x7, waiting for transfers between devices, toward(): return lax.ppermute(x, OWNERS, [(i, i ^ flip) for i in range(owners)])  25.1 us
    ppermute x7, starting transfers between devices, toward(): return lax.ppermute(x, OWNERS, [(i, i ^ flip) for i in range(owners)])  10.6 us
    ppermute x3, waiting for transfers between devices, across(): return lax.ppermute(x, (*OWNERS, 'rep'), pairs)  7.8 us
    pallas_call x12, Pallas kernels, call(): pl.pallas_call(kernel, out_shape=out_shape, in_specs=[spec] * count + [pl...  6.45 us
    ppermute x1, waiting for transfers between devices, per_device(): tile = lax.ppermute(chosen, ('clus', 'rep'), opposite)  4.92 us
    ppermute x1, starting transfers between devices, per_device(): tile = lax.ppermute(chosen, ('clus', 'rep'), opposite)  2.9 us
    ppermute x3, starting transfers between devices, across(): return lax.ppermute(x, (*OWNERS, 'rep'), pairs)  2.49 us
    ppermute x5, starting transfers between devices, per_device(): other = [lax.ppermute(part, 'rep', swap) for part in mine]  1.64 us
  transfers between devices with their start and end apart: 18, of which 14 were waited for; matrix products, arithmetic and copies ran while one was open for 1% of the time, Pallas kernels for 6%

profile of v6, /device:TPU:0, one launch (start us, length us, event | category | flops | bytes accessed | tf_op | source)
XLA Modules:
  0.0 67.0 jit_solution(12477649814036398862)
XLA Ops:
  0.0 0.0 copy-start.2
  0.0 0.0 copy-start.1
  0.0 0.7 %copy-done.1 = s32[512]{0:T(512)S(1)} copy-done((s32[512]{0:T(512)S(1)}, s32[512]{0:T(512)}, u32[]{:S(2)}) %copy-start.1) | copy-done | bytes 2072
  0.8 0.2 shard_map.47.refs_1_
  1.0 0.1 copy-done.2
  1.1 0.6 shard_map.48
  1.7 4.1 %collective-permute-start.3 = (bf16[128,768]{1,0:T(8,128)(2,1)S(1)}, bf16[128,768]{1,0:T(8,128)(2,1)S(1)}, u32[]{:S(2)}, u32[]{:S(2)}) collective-permute-start(bf16[128,768]{1,0:T(8,128)(2,1)S(1)} %get-tuple-element.27), channel_id=1, source_target_pairs={{0,8},{2,10},{4,12},{6,14},{8,0},{10,2},{12,4},{14,6},{1,9},{3,11}... | collective-permute-start | bytes 589832 | tf_op jit(solution)/shard_map/ppermute | solution.py:266
  5.8 0.0 copy-start
  5.8 2.3 %collective-permute-start.6 = (bf16[128,768]{1,0:T(8,128)(2,1)S(1)}, bf16[128,768]{1,0:T(8,128)(2,1)S(1)}, u32[]{:S(2)}, u32[]{:S(2)}) collective-permute-start(bf16[128,768]{1,0:T(8,128)(2,1)S(1)} %get-tuple-element.30), channel_id=1, source_target_pairs={{0,14},{2,12},{4,10},{6,8},{8,6},{10,4},{12,2},{14,0},{1,15},{3,13... | collective-permute-start | bytes 589832 | tf_op jit(solution)/shard_map/ppermute | solution.py:266
  8.1 0.0 copy-done
  8.1 0.5 shard_map.49
  8.6 0.6 collective-permute-start
  9.2 0.0 copy-start.3
  9.2 0.7 %copy-done.3 = s32[1,256]{1,0:T(1,128)S(1)} copy-done((s32[1,256]{1,0:T(1,128)S(1)}, s32[1,256]{1,0:T(1,128)}, u32[]{:S(2)}) %copy-start.3) | copy-done | bytes 1048
  9.9 0.1 copy.11
  10.1 9.2 %collective-permute-done.refs_3_.refs_1_ = bf16[816,128]{1,0:T(8,128)(2,1)S(1)} collective-permute-done((bf16[816,128]{1,0:T(8,128)(2,1)S(1)}, bf16[816,128]{1,0:T(8,128)(2,1)S(1)}, u32[]{:S(2)}, u32[]{:S(2)}) %collective-permute-start) | collective-permute-done | bytes 208928 | tf_op jit(solution)/shard_map/ppermute | solution.py:266
  19.3 0.4 shard_map.50
  19.8 0.1 collective-permute-start.1
  19.8 0.1 copy.10
  20.0 3.0 %collective-permute-start.4 = (bf16[128,768]{1,0:T(8,128)(2,1)S(1)}, bf16[128,768]{1,0:T(8,128)(2,1)S(1)}, u32[]{:S(2)}, u32[]{:S(2)}) collective-permute-start(bf16[128,768]{1,0:T(8,128)(2,1)S(1)} %get-tuple-element.28), channel_id=1, source_target_pairs={{0,10},{2,8},{4,14},{6,12},{8,2},{10,0},{12,6},{14,4},{1,11},{3,9}... | collective-permute-start | bytes 589832 | tf_op jit(solution)/shard_map/ppermute | solution.py:266
  23.0 6.7 %collective-permute-done.1.refs_4_.refs_2_ = bf16[816,128]{1,0:T(8,128)(2,1)S(1)} collective-permute-done((bf16[816,128]{1,0:T(8,128)(2,1)S(1)}, bf16[816,128]{1,0:T(8,128)(2,1)S(1)}, u32[]{:S(2)}, u32[]{:S(2)}) %collective-permute-start.1) | collective-permute-done | bytes 208928 | tf_op jit(solution)/shard_map/ppermute | solution.py:266
  29.7 0.4 shard_map.51
  30.1 0.1 collective-permute-start.2
  30.2 0.5 collective-permute-start.5
  30.7 0.0 collective-permute-done.3.refs_4_
  30.7 0.0 collective-permute-done.6.refs_7_
  30.7 5.3 %collective-permute-done.4.refs_5_ = bf16[128,768]{1,0:T(8,128)(2,1)S(1)} collective-permute-done((bf16[128,768]{1,0:T(8,128)(2,1)S(1)}, bf16[128,768]{1,0:T(8,128)(2,1)S(1)}, u32[]{:S(2)}, u32[]{:S(2)}) %collective-permute-start.4) | collective-permute-done | bytes 196640 | tf_op jit(solution)/shard_map/ppermute | solution.py:266
  36.0 3.9 %collective-permute-done.2.refs_3_ = bf16[128,768]{1,0:T(8,128)(2,1)S(1)} collective-permute-done((bf16[128,768]{1,0:T(8,128)(2,1)S(1)}, bf16[128,768]{1,0:T(8,128)(2,1)S(1)}, u32[]{:S(2)}, u32[]{:S(2)}) %collective-permute-start.2) | collective-permute-done | bytes 196640 | tf_op jit(solution)/shard_map/ppermute | solution.py:266
  39.9 0.0 collective-permute-done.5.refs_6_
  39.9 0.4 shard_map.52.refs_9_
  40.3 0.1 collective-permute-start.12
  40.4 0.5 shard_map.53
  41.0 0.6 collective-permute-start.7
  41.5 0.3 collective-permute-done.12
  41.8 0.1 add.10
  41.9 2.9 %collective-permute-start.13 = (bf16[128,768]{1,0:T(8,128)(2,1)S(1)}, bf16[128,768]{1,0:T(8,128)(2,1)S(1)}, u32[]{:S(2)}, u32[]{:S(2)}) collective-permute-start(bf16[128,768]{1,0:T(8,128)(2,1)S(1)} %add.10), channel_id=1, source_target_pairs={{0,9},{1,8},{4,13},{5,12},{8,1},{9,0},{12,5},{13,4},{2,11},{3,10},... | collective-permute-start | bytes 589832 | tf_op jit(solution)/shard_map/ppermute | solution.py:373
  44.8 0.9 %shard_map.54 = (bf16[112,768]{1,0:T(8,128)(2,1)S(1)}, bf16[112,768]{1,0:T(8,128)(2,1)S(1)}, bf16[112,768]{1,0:T(8,128)(2,1)S(1)}, bf16[112,768]{1,0:T(8,128)(2,1)S(1)}) custom-call(bf16[776,128]{1,0:T(8,128)(2,1)S(1)} %get-tuple-element.23.refs_0_, bf16[816,128]{1,0:T(8,128)(2,1)S(1)} %collective-permute-done.refs_3_.refs_1_, ...), custom_call_target="tpu_custom_call" | custom-call | flops 805306368 | bytes 2289664 | tf_op jit(solution)/shard_map/pallas_call | solution.py:41
  45.7 0.4 collective-permute-start.8
  46.1 0.1 collective-permute-start.9
  46.3 0.4 collective-permute-start.10
  46.6 0.0 collective-permute-done.7.refs_5_
  46.6 0.1 collective-permute-start.11
  46.8 0.4 collective-permute-done.8.refs_6_
  47.2 0.4 collective-permute-done.9.refs_7_
  47.5 0.2 collective-permute-done.10.refs_8_
  47.8 0.3 collective-permute-done.11.refs_9_
  48.1 1.0 %shard_map.55.refs_11_ = f32[1,512]{1,0:T(1,128)S(1)} custom-call(bf16[64,768]{1,0:T(8,128)(2,1)S(1)} %get-tuple-element.31.refs_0_, bf16[112,768]{1,0:T(8,128)(2,1)S(1)} %get-tuple-element.33.refs_1_, bf16[112,768]{1,0:T(8,128)(2,1)S(1)} %get-tuple-element.34.refs_2_, bf16[112,768]{1,0:T(8,128)(2,1)S(1)} %get-tuple-element.35.refs_3_, ...), custom_call_target="tpu_custom_call" | custom-call | tf_op jit(solution)/shard_map/pallas_call | solution.py:41
  49.1 4.9 %collective-permute-done.13.refs_10_ = bf16[128,768]{1,0:T(8,128)(2,1)S(1)} collective-permute-done((bf16[128,768]{1,0:T(8,128)(2,1)S(1)}, bf16[128,768]{1,0:T(8,128)(2,1)S(1)}, u32[]{:S(2)}, u32[]{:S(2)}) %collective-permute-start.13) | collective-permute-done | bytes 196640 | tf_op jit(solution)/shard_map/ppermute | solution.py:373
  54.0 0.7 shard_map.56
  54.7 0.3 collective-permute-start.14
  55.0 0.9 %collective-permute-done.14 = f32[8,128]{1,0:T(8,128)S(1)} collective-permute-done((f32[8,128]{1,0:T(8,128)S(1)}, f32[8,128]{1,0:T(8,128)S(1)}, u32[]{:S(2)}, u32[]{:S(2)}) %collective-permute-start.14) | collective-permute-done | bytes 4128 | tf_op jit(solution)/shard_map/ppermute | solution.py:401
  56.0 1.4 %collective-permute-start.15 = (f32[8,128]{1,0:T(8,128)S(1)}, f32[8,128]{1,0:T(8,128)S(1)}, u32[]{:S(2)}, u32[]{:S(2)}) collective-permute-start(f32[8,128]{1,0:T(8,128)S(1)} %pad_maximum_fusion.4), channel_id=1, source_target_pairs={{0,3},{1,2},{2,1},{3,0},{4,7},{5,6},{6,5},{7,4},{8,11},{9,10},{10,... | collective-permute-start | bytes 12296 | tf_op jit(solution)/shard_map/ppermute | solution.py:270
  57.4 1.7 %collective-permute-done.15 = f32[8,128]{1,0:T(8,128)S(1)} collective-permute-done((f32[8,128]{1,0:T(8,128)S(1)}, f32[8,128]{1,0:T(8,128)S(1)}, u32[]{:S(2)}, u32[]{:S(2)}) %collective-permute-start.15) | collective-permute-done | bytes 4128 | tf_op jit(solution)/shard_map/ppermute | solution.py:270
  59.1 0.1 collective-permute-start.16
  59.2 3.1 %collective-permute-done.16 = f32[16,128]{1,0:T(8,128)S(1)} collective-permute-done((f32[16,128]{1,0:T(8,128)S(1)}, f32[16,128]{1,0:T(8,128)S(1)}, u32[]{:S(2)}, u32[]{:S(2)}) %collective-permute-start.16) | collective-permute-done | bytes 8224 | tf_op jit(solution)/shard_map/ppermute | solution.py:270
  62.2 1.0 %collective-permute-start.17 = (f32[16,128]{1,0:T(8,128)S(1)}, f32[16,128]{1,0:T(8,128)S(1)}, u32[]{:S(2)}, u32[]{:S(2)}) collective-permute-start(f32[16,128]{1,0:T(8,128)S(1)} %fusion), channel_id=1, source_target_pairs={{0,9},{1,8},{2,11},{3,10},{4,13},{5,12},{6,15},{7,14},{8,1},{9,0},... | collective-permute-start | bytes 24584 | tf_op jit(solution)/shard_map/ppermute | solution.py:270
  63.2 3.1 %collective-permute-done.17 = f32[16,128]{1,0:T(8,128)S(1)} collective-permute-done((f32[16,128]{1,0:T(8,128)S(1)}, f32[16,128]{1,0:T(8,128)S(1)}, u32[]{:S(2)}, u32[]{:S(2)}) %collective-permute-start.17) | collective-permute-done | bytes 8224 | tf_op jit(solution)/shard_map/ppermute | solution.py:270
  66.3 0.7 %shard_map.57 = f32[4,128]{1,0:T(4,128)} custom-call(f32[32,128]{1,0:T(8,128)S(1)} %pad_maximum_fusion.refs_0_, s32[4,128]{1,0:T(4,128)S(1)} %bitcast.17, s32[4,128]{1,0:T(4,128)S(1)} %bitcast.15, s32[1,1]{1,0:T(1,128)} %bitcast.1.refs_2_.refs_3_), custom_call_target="tpu_custom_call" | custom-call | flops 4096 | bytes 22532 | tf_op jit(solution)/shard_map/pallas_call | solution.py:41
  (15 shorter events, 0.1 us)
Async XLA Ops:
  0.0 1.1 %copy-start.2 = (bf16[512,768]{1,0:T(8,128)(2,1)S(1)}, bf16[512,768]{1,0:T(8,128)(2,1)}, u32[]{:S(2)}) copy-start(bf16[512,768]{1,0:T(8,128)(2,1)} %refs_0_.1) | copy-start | bytes 2359300
  0.0 0.8 %copy-start.1 = (s32[512]{0:T(512)S(1)}, s32[512]{0:T(512)}, u32[]{:S(2)}) copy-start(s32[512]{0:T(512)} %param.6) | copy-start | bytes 6148
  1.7 29.0 %collective-permute-start.3 = (bf16[128,768]{1,0:T(8,128)(2,1)S(1)}, bf16[128,768]{1,0:T(8,128)(2,1)S(1)}, u32[]{:S(2)}, u32[]{:S(2)}) collective-permute-start(bf16[128,768]{1,0:T(8,128)(2,1)S(1)} %get-tuple-element.27), channel_id=1, source_target_pairs={{0,8},{2,10},{4,12},{6,14},{8,0},{10,2},{12,4},{14,6},{1,9},{3,11}... | collective-permute-start | bytes 589832 | tf_op jit(solution)/shard_map/ppermute | solution.py:266
  5.8 2.3 %copy-start = (s32[512]{0:T(512)S(1)}, s32[512]{0:T(512)}, u32[]{:S(2)}) copy-start(s32[512]{0:T(512)} %param.7) | copy-start | bytes 6148
  5.8 24.9 %collective-permute-start.6 = (bf16[128,768]{1,0:T(8,128)(2,1)S(1)}, bf16[128,768]{1,0:T(8,128)(2,1)S(1)}, u32[]{:S(2)}, u32[]{:S(2)}) collective-permute-start(bf16[128,768]{1,0:T(8,128)(2,1)S(1)} %get-tuple-element.30), channel_id=1, source_target_pairs={{0,14},{2,12},{4,10},{6,8},{8,6},{10,4},{12,2},{14,0},{1,15},{3,13... | collective-permute-start | bytes 589832 | tf_op jit(solution)/shard_map/ppermute | solution.py:266
  8.6 10.7 %collective-permute-start = (bf16[816,128]{1,0:T(8,128)(2,1)S(1)}, bf16[816,128]{1,0:T(8,128)(2,1)S(1)}, u32[]{:S(2)}, u32[]{:S(2)}) collective-permute-start(bf16[816,128]{1,0:T(8,128)(2,1)S(1)} %get-tuple-element.24), channel_id=1, source_target_pairs={{0,2},{2,0},{4,6},{6,4},{8,10},{10,8},{12,14},{14,12},{1,3},{3,1},... | collective-permute-start | bytes 626696 | tf_op jit(solution)/shard_map/ppermute | solution.py:266
  9.2 0.7 %copy-start.3 = (s32[1,256]{1,0:T(1,128)S(1)}, s32[1,256]{1,0:T(1,128)}, u32[]{:S(2)}) copy-start(s32[1,256]{1,0:T(1,128)} %param.8) | copy-start | bytes 3076
  19.8 9.9 %collective-permute-start.1 = (bf16[816,128]{1,0:T(8,128)(2,1)S(1)}, bf16[816,128]{1,0:T(8,128)(2,1)S(1)}, u32[]{:S(2)}, u32[]{:S(2)}) collective-permute-start(bf16[816,128]{1,0:T(8,128)(2,1)S(1)} %get-tuple-element.25), channel_id=1, source_target_pairs={{0,4},{2,6},{4,0},{6,2},{8,12},{10,14},{12,8},{14,10},{1,5},{3,7},... | collective-permute-start | bytes 626696 | tf_op jit(solution)/shard_map/ppermute | solution.py:266
  20.0 16.0 %collective-permute-start.4 = (bf16[128,768]{1,0:T(8,128)(2,1)S(1)}, bf16[128,768]{1,0:T(8,128)(2,1)S(1)}, u32[]{:S(2)}, u32[]{:S(2)}) collective-permute-start(bf16[128,768]{1,0:T(8,128)(2,1)S(1)} %get-tuple-element.28), channel_id=1, source_target_pairs={{0,10},{2,8},{4,14},{6,12},{8,2},{10,0},{12,6},{14,4},{1,11},{3,9}... | collective-permute-start | bytes 589832 | tf_op jit(solution)/shard_map/ppermute | solution.py:266
  30.1 9.8 %collective-permute-start.2 = (bf16[128,768]{1,0:T(8,128)(2,1)S(1)}, bf16[128,768]{1,0:T(8,128)(2,1)S(1)}, u32[]{:S(2)}, u32[]{:S(2)}) collective-permute-start(bf16[128,768]{1,0:T(8,128)(2,1)S(1)} %get-tuple-element.26), channel_id=1, source_target_pairs={{0,6},{2,4},{4,2},{6,0},{8,14},{10,12},{12,10},{14,8},{1,7},{3,5},... | collective-permute-start | bytes 589832 | tf_op jit(solution)/shard_map/ppermute | solution.py:266
  30.2 9.7 %collective-permute-start.5 = (bf16[776,128]{1,0:T(8,128)(2,1)S(1)}, bf16[776,128]{1,0:T(8,128)(2,1)S(1)}, u32[]{:S(2)}, u32[]{:S(2)}) collective-permute-start(bf16[776,128]{1,0:T(8,128)(2,1)S(1)} %get-tuple-element.29), channel_id=1, source_target_pairs={{0,12},{2,14},{4,8},{6,10},{8,4},{10,6},{12,0},{14,2},{1,13},{3,15... | collective-permute-start | bytes 595976 | tf_op jit(solution)/shard_map/ppermute | solution.py:266
  40.3 1.5 %collective-permute-start.12 = (bf16[128,768]{1,0:T(8,128)(2,1)S(1)}, bf16[128,768]{1,0:T(8,128)(2,1)S(1)}, u32[]{:S(2)}, u32[]{:S(2)}) collective-permute-start(bf16[128,768]{1,0:T(8,128)(2,1)S(1)} %shard_map.52.refs_9_), channel_id=1, source_target_pairs={{0,1},{1,0},{2,3},{3,2},{4,5},{5,4},{6,7},{7,6},{8,9},{9,8},{10,11... | collective-permute-start | bytes 589832 | tf_op jit(solution)/shard_map/ppermute | solution.py:372
  41.0 5.7 %collective-permute-start.7 = (bf16[64,768]{1,0:T(8,128)(2,1)S(1)}, bf16[64,768]{1,0:T(8,128)(2,1)S(1)}, u32[]{:S(2)}, u32[]{:S(2)}) collective-permute-start(bf16[64,768]{1,0:T(8,128)(2,1)S(1)} %get-tuple-element.31.refs_0_), channel_id=1, source_target_pairs={{0,1},{1,0},{2,3},{3,2},{4,5},{5,4},{6,7},{7,6},{8,9},{9,8},{10,11... | collective-permute-start | bytes 294920 | tf_op jit(solution)/shard_map/ppermute | solution.py:383
  41.9 12.1 %collective-permute-start.13 = (bf16[128,768]{1,0:T(8,128)(2,1)S(1)}, bf16[128,768]{1,0:T(8,128)(2,1)S(1)}, u32[]{:S(2)}, u32[]{:S(2)}) collective-permute-start(bf16[128,768]{1,0:T(8,128)(2,1)S(1)} %add.10), channel_id=1, source_target_pairs={{0,9},{1,8},{4,13},{5,12},{8,1},{9,0},{12,5},{13,4},{2,11},{3,10},... | collective-permute-start | bytes 589832 | tf_op jit(solution)/shard_map/ppermute | solution.py:373
  45.7 1.5 %collective-permute-start.8 = (bf16[112,768]{1,0:T(8,128)(2,1)S(1)}, bf16[112,768]{1,0:T(8,128)(2,1)S(1)}, u32[]{:S(2)}, u32[]{:S(2)}) collective-permute-start(bf16[112,768]{1,0:T(8,128)(2,1)S(1)} %get-tuple-element.33.refs_1_), channel_id=1, source_target_pairs={{0,1},{1,0},{2,3},{3,2},{4,5},{5,4},{6,7},{7,6},{8,9},{9,8},{10,11... | collective-permute-start | bytes 516104 | tf_op jit(solution)/shard_map/ppermute | solution.py:383
  46.1 1.4 %collective-permute-start.9 = (bf16[112,768]{1,0:T(8,128)(2,1)S(1)}, bf16[112,768]{1,0:T(8,128)(2,1)S(1)}, u32[]{:S(2)}, u32[]{:S(2)}) collective-permute-start(bf16[112,768]{1,0:T(8,128)(2,1)S(1)} %get-tuple-element.34.refs_2_), channel_id=1, source_target_pairs={{0,1},{1,0},{2,3},{3,2},{4,5},{5,4},{6,7},{7,6},{8,9},{9,8},{10,11... | collective-permute-start | bytes 516104 | tf_op jit(solution)/shard_map/ppermute | solution.py:383
  46.3 1.5 %collective-permute-start.10 = (bf16[112,768]{1,0:T(8,128)(2,1)S(1)}, bf16[112,768]{1,0:T(8,128)(2,1)S(1)}, u32[]{:S(2)}, u32[]{:S(2)}) collective-permute-start(bf16[112,768]{1,0:T(8,128)(2,1)S(1)} %get-tuple-element.35.refs_3_), channel_id=1, source_target_pairs={{0,1},{1,0},{2,3},{3,2},{4,5},{5,4},{6,7},{7,6},{8,9},{9,8},{10,11... | collective-permute-start | bytes 516104 | tf_op jit(solution)/shard_map/ppermute | solution.py:383
  46.6 1.4 %collective-permute-start.11 = (bf16[112,768]{1,0:T(8,128)(2,1)S(1)}, bf16[112,768]{1,0:T(8,128)(2,1)S(1)}, u32[]{:S(2)}, u32[]{:S(2)}) collective-permute-start(bf16[112,768]{1,0:T(8,128)(2,1)S(1)} %get-tuple-element.36.refs_4_), channel_id=1, source_target_pairs={{0,1},{1,0},{2,3},{3,2},{4,5},{5,4},{6,7},{7,6},{8,9},{9,8},{10,11... | collective-permute-start | bytes 516104 | tf_op jit(solution)/shard_map/ppermute | solution.py:383
  54.7 1.2 %collective-permute-start.14 = (f32[8,128]{1,0:T(8,128)S(1)}, f32[8,128]{1,0:T(8,128)S(1)}, u32[]{:S(2)}, u32[]{:S(2)}) collective-permute-start(f32[8,128]{1,0:T(8,128)S(1)} %pad_maximum_fusion.3), channel_id=1, source_target_pairs={{0,1},{1,0},{2,3},{3,2},{4,5},{5,4},{6,7},{7,6},{8,9},{9,8},{10,11... | collective-permute-start | bytes 12296 | tf_op jit(solution)/shard_map/ppermute | solution.py:401
  56.0 3.1 %collective-permute-start.15 = (f32[8,128]{1,0:T(8,128)S(1)}, f32[8,128]{1,0:T(8,128)S(1)}, u32[]{:S(2)}, u32[]{:S(2)}) collective-permute-start(f32[8,128]{1,0:T(8,128)S(1)} %pad_maximum_fusion.4), channel_id=1, source_target_pairs={{0,3},{1,2},{2,1},{3,0},{4,7},{5,6},{6,5},{7,4},{8,11},{9,10},{10,... | collective-permute-start | bytes 12296 | tf_op jit(solution)/shard_map/ppermute | solution.py:270
  59.1 3.1 %collective-permute-start.16 = (f32[16,128]{1,0:T(8,128)S(1)}, f32[16,128]{1,0:T(8,128)S(1)}, u32[]{:S(2)}, u32[]{:S(2)}) collective-permute-start(f32[16,128]{1,0:T(8,128)S(1)} %pad_maximum_fusion.1), channel_id=1, source_target_pairs={{0,5},{1,4},{2,7},{3,6},{4,1},{5,0},{6,3},{7,2},{8,13},{9,12},{10,... | collective-permute-start | bytes 24584 | tf_op jit(solution)/shard_map/ppermute | solution.py:270
  62.2 4.1 %collective-permute-start.17 = (f32[16,128]{1,0:T(8,128)S(1)}, f32[16,128]{1,0:T(8,128)S(1)}, u32[]{:S(2)}, u32[]{:S(2)}) collective-permute-start(f32[16,128]{1,0:T(8,128)S(1)} %fusion), channel_id=1, source_target_pairs={{0,9},{1,8},{2,11},{3,10},{4,13},{5,12},{6,15},{7,14},{8,1},{9,0},... | collective-permute-start | bytes 24584 | tf_op jit(solution)/shard_map/ppermute | solution.py:270

commit v7 on v6

--- a/solution.py
+++ b/solution.py
@@ -236,10 +236,13 @@
             out_ref[r : r + 1, :] = total[:, r * LANES : (r + 1) * LANES]
 
 
-def answer_body(scores_ref, cluster_ref, order_ref, base_ref, out_ref):
+def answer_body(backwards, scores_ref, cluster_ref, order_ref, base_ref, out_ref):
     lines_each = HALF // LANES
     place = order_ref[...] % HALF
-    line = (cluster_ref[...] ^ base_ref[...]) * lines_each + place // LANES
+    owner = cluster_ref[...] ^ base_ref[...]
+    if backwards:
+        owner = owner % 2 * 4 + owner // 2 % 2 * 2 + owner // 4
+    line = owner * lines_each + place // LANES
     lane = place % LANES
 
     def add(n, found):
@@ -275,12 +278,11 @@
     def gather_halves(mine, other):
         if not paired:
             return gather(mine)
-        for flip in (1, 2, 4):
-            arrived = across(jnp.concatenate([other, mine]) if flip < 4 else other, flip)
-            mine = jnp.concatenate([mine, arrived[: mine.shape[0]]])
-            if flip < 4:
-                other = jnp.concatenate([other, arrived[other.shape[0] :]])
-        return mine
+        count = mine.shape[0]
+        arrived = across(jnp.concatenate([other, mine]), 4)
+        mine = jnp.concatenate([mine, arrived[:count]])
+        other = jnp.concatenate([other, arrived[count:]])
+        return jnp.concatenate([mine] + [across(other, flip) for flip in (2, 1, 3)])
 
     base = me if paired else jnp.zeros_like(me)
     base = base.reshape(1, 1)
@@ -403,7 +405,7 @@
     scores = -jnp.log(totals / (CAP - 1 + BORDER))
     lines = HALF // LANES
     answers = call(
-        answer_body,
+        functools.partial(answer_body, paired),
         jax.ShapeDtypeStruct((rows // LANES, LANES), jnp.float32),
         owners * HALF,
         gather_halves(scores[:lines], scores[lines:]),

time: 67.2 us -> 65.4 us (0.973)
  waiting for transfers between devices: 40.3 us -> 37.8 us
  starting transfers between devices: 18.1 us -> 18.8 us
    ppermute x3 -> x4, waiting for transfers between devices: 7.8 us -> 5.32 us  [across(): return lax.ppermute(x, (*OWNERS, 'rep'), pairs)]
    ppermute x3 -> x4, starting transfers between devices: 2.49 us -> 3.2 us  [across(): return lax.ppermute(x, (*OWNERS, 'rep'), pairs)]
  transfers between devices with their start and end apart: 18 -> 19, of which waited for: 14 -> 14; matrix products, arithmetic and copies ran while one was open for 1% -> 1% of each run, Pallas kernels for 6% -> 6%
where the time goes in v7:
time: 65.4 us; the launch traced here: 65.2 us
  waiting for transfers between devices  37.8 us (58%)
  starting transfers between devices  18.8 us (29%)
  Pallas kernels  6.45 us (10%)
  local copies, waits for them, and re-layouts  1.88 us (3%)
    ppermute x7, waiting for transfers between devices, toward(): return lax.ppermute(x, OWNERS, [(i, i ^ flip) for i in range(owners)])  25.1 us
    ppermute x7, starting transfers between devices, toward(): return lax.ppermute(x, OWNERS, [(i, i ^ flip) for i in range(owners)])  10.6 us
    pallas_call x12, Pallas kernels, call(): pl.pallas_call(kernel, out_shape=out_shape, in_specs=[spec] * count + [pl...  6.45 us
    ppermute x4, waiting for transfers between devices, across(): return lax.ppermute(x, (*OWNERS, 'rep'), pairs)  5.32 us
    ppermute x1, waiting for transfers between devices, per_device(): tile = lax.ppermute(chosen, ('clus', 'rep'), opposite)  4.92 us
    ppermute x4, starting transfers between devices, across(): return lax.ppermute(x, (*OWNERS, 'rep'), pairs)  3.2 us
    ppermute x1, starting transfers between devices, per_device(): tile = lax.ppermute(chosen, ('clus', 'rep'), opposite)  2.9 us
    ppermute x5, starting transfers between devices, per_device(): other = [lax.ppermute(part, 'rep', swap) for part in mine]  1.64 us
  transfers between devices with their start and end apart: 19, of which 14 were waited for; matrix products, arithmetic and copies ran while one was open for 1% of the time, Pallas kernels for 6%

profile of v7, /device:TPU:0, one launch (start us, length us, event | category | flops | bytes accessed | tf_op | source)
XLA Modules:
  0.0 65.2 jit_solution(17515626024373953206)
XLA Ops:
  0.0 0.0 copy-start.2
  0.0 0.0 copy-start.1
  0.0 0.7 %copy-done.1 = s32[512]{0:T(512)S(1)} copy-done((s32[512]{0:T(512)S(1)}, s32[512]{0:T(512)}, u32[]{:S(2)}) %copy-start.1) | copy-done | bytes 2072
  0.8 0.2 shard_map.47.refs_1_
  1.0 0.1 copy-done.2
  1.1 0.6 shard_map.48
  1.7 4.1 %collective-permute-start.3 = (bf16[128,768]{1,0:T(8,128)(2,1)S(1)}, bf16[128,768]{1,0:T(8,128)(2,1)S(1)}, u32[]{:S(2)}, u32[]{:S(2)}) collective-permute-start(bf16[128,768]{1,0:T(8,128)(2,1)S(1)} %get-tuple-element.27), channel_id=1, source_target_pairs={{0,8},{2,10},{4,12},{6,14},{8,0},{10,2},{12,4},{14,6},{1,9},{3,11}... | collective-permute-start | bytes 589832 | tf_op jit(solution)/shard_map/ppermute | solution.py:269
  5.8 0.0 copy-start
  5.8 2.3 %collective-permute-start.6 = (bf16[128,768]{1,0:T(8,128)(2,1)S(1)}, bf16[128,768]{1,0:T(8,128)(2,1)S(1)}, u32[]{:S(2)}, u32[]{:S(2)}) collective-permute-start(bf16[128,768]{1,0:T(8,128)(2,1)S(1)} %get-tuple-element.30), channel_id=1, source_target_pairs={{0,14},{2,12},{4,10},{6,8},{8,6},{10,4},{12,2},{14,0},{1,15},{3,13... | collective-permute-start | bytes 589832 | tf_op jit(solution)/shard_map/ppermute | solution.py:269
  8.1 0.0 copy-done
  8.1 0.5 shard_map.49
  8.6 0.6 collective-permute-start
  9.2 0.0 copy-start.3
  9.2 0.7 %copy-done.3 = s32[1,256]{1,0:T(1,128)S(1)} copy-done((s32[1,256]{1,0:T(1,128)S(1)}, s32[1,256]{1,0:T(1,128)}, u32[]{:S(2)}) %copy-start.3) | copy-done | bytes 1048
  9.9 0.1 copy.11
  10.1 9.2 %collective-permute-done.refs_3_.refs_1_ = bf16[816,128]{1,0:T(8,128)(2,1)S(1)} collective-permute-done((bf16[816,128]{1,0:T(8,128)(2,1)S(1)}, bf16[816,128]{1,0:T(8,128)(2,1)S(1)}, u32[]{:S(2)}, u32[]{:S(2)}) %collective-permute-start) | collective-permute-done | bytes 208928 | tf_op jit(solution)/shard_map/ppermute | solution.py:269
  19.3 0.4 shard_map.50
  19.8 0.1 collective-permute-start.1
  19.8 0.1 copy.10
  20.0 3.0 %collective-permute-start.4 = (bf16[128,768]{1,0:T(8,128)(2,1)S(1)}, bf16[128,768]{1,0:T(8,128)(2,1)S(1)}, u32[]{:S(2)}, u32[]{:S(2)}) collective-permute-start(bf16[128,768]{1,0:T(8,128)(2,1)S(1)} %get-tuple-element.28), channel_id=1, source_target_pairs={{0,10},{2,8},{4,14},{6,12},{8,2},{10,0},{12,6},{14,4},{1,11},{3,9}... | collective-permute-start | bytes 589832 | tf_op jit(solution)/shard_map/ppermute | solution.py:269
  23.0 6.7 %collective-permute-done.1.refs_4_.refs_2_ = bf16[816,128]{1,0:T(8,128)(2,1)S(1)} collective-permute-done((bf16[816,128]{1,0:T(8,128)(2,1)S(1)}, bf16[816,128]{1,0:T(8,128)(2,1)S(1)}, u32[]{:S(2)}, u32[]{:S(2)}) %collective-permute-start.1) | collective-permute-done | bytes 208928 | tf_op jit(solution)/shard_map/ppermute | solution.py:269
  29.7 0.4 shard_map.51
  30.1 0.1 collective-permute-start.2
  30.2 0.5 collective-permute-start.5
  30.7 0.0 collective-permute-done.3.refs_4_
  30.7 0.0 collective-permute-done.6.refs_7_
  30.7 5.3 %collective-permute-done.4.refs_5_ = bf16[128,768]{1,0:T(8,128)(2,1)S(1)} collective-permute-done((bf16[128,768]{1,0:T(8,128)(2,1)S(1)}, bf16[128,768]{1,0:T(8,128)(2,1)S(1)}, u32[]{:S(2)}, u32[]{:S(2)}) %collective-permute-start.4) | collective-permute-done | bytes 196640 | tf_op jit(solution)/shard_map/ppermute | solution.py:269
  36.0 3.9 %collective-permute-done.2.refs_3_ = bf16[128,768]{1,0:T(8,128)(2,1)S(1)} collective-permute-done((bf16[128,768]{1,0:T(8,128)(2,1)S(1)}, bf16[128,768]{1,0:T(8,128)(2,1)S(1)}, u32[]{:S(2)}, u32[]{:S(2)}) %collective-permute-start.2) | collective-permute-done | bytes 196640 | tf_op jit(solution)/shard_map/ppermute | solution.py:269
  39.9 0.0 collective-permute-done.5.refs_6_
  39.9 0.4 shard_map.52.refs_9_
  40.3 0.1 collective-permute-start.12
  40.4 0.5 shard_map.53
  41.0 0.6 collective-permute-start.7
  41.5 0.3 collective-permute-done.12
  41.8 0.1 add.10
  41.9 2.9 %collective-permute-start.13 = (bf16[128,768]{1,0:T(8,128)(2,1)S(1)}, bf16[128,768]{1,0:T(8,128)(2,1)S(1)}, u32[]{:S(2)}, u32[]{:S(2)}) collective-permute-start(bf16[128,768]{1,0:T(8,128)(2,1)S(1)} %add.10), channel_id=1, source_target_pairs={{0,9},{1,8},{4,13},{5,12},{8,1},{9,0},{12,5},{13,4},{2,11},{3,10},... | collective-permute-start | bytes 589832 | tf_op jit(solution)/shard_map/ppermute | solution.py:375
  44.8 0.9 %shard_map.54 = (bf16[112,768]{1,0:T(8,128)(2,1)S(1)}, bf16[112,768]{1,0:T(8,128)(2,1)S(1)}, bf16[112,768]{1,0:T(8,128)(2,1)S(1)}, bf16[112,768]{1,0:T(8,128)(2,1)S(1)}) custom-call(bf16[776,128]{1,0:T(8,128)(2,1)S(1)} %get-tuple-element.23.refs_0_, bf16[816,128]{1,0:T(8,128)(2,1)S(1)} %collective-permute-done.refs_3_.refs_1_, ...), custom_call_target="tpu_custom_call" | custom-call | flops 805306368 | bytes 2289664 | tf_op jit(solution)/shard_map/pallas_call | solution.py:41
  45.7 0.4 collective-permute-start.8
  46.1 0.1 collective-permute-start.9
  46.3 0.4 collective-permute-start.10
  46.6 0.0 collective-permute-done.7.refs_5_
  46.6 0.1 collective-permute-start.11
  46.8 0.4 collective-permute-done.8.refs_6_
  47.2 0.4 collective-permute-done.9.refs_7_
  47.5 0.2 collective-permute-done.10.refs_8_
  47.8 0.3 collective-permute-done.11.refs_9_
  48.1 1.0 %shard_map.55.refs_11_ = f32[1,512]{1,0:T(1,128)S(1)} custom-call(bf16[64,768]{1,0:T(8,128)(2,1)S(1)} %get-tuple-element.31.refs_0_, bf16[112,768]{1,0:T(8,128)(2,1)S(1)} %get-tuple-element.33.refs_1_, bf16[112,768]{1,0:T(8,128)(2,1)S(1)} %get-tuple-element.34.refs_2_, bf16[112,768]{1,0:T(8,128)(2,1)S(1)} %get-tuple-element.35.refs_3_, ...), custom_call_target="tpu_custom_call" | custom-call | tf_op jit(solution)/shard_map/pallas_call | solution.py:41
  49.1 4.9 %collective-permute-done.13.refs_10_ = bf16[128,768]{1,0:T(8,128)(2,1)S(1)} collective-permute-done((bf16[128,768]{1,0:T(8,128)(2,1)S(1)}, bf16[128,768]{1,0:T(8,128)(2,1)S(1)}, u32[]{:S(2)}, u32[]{:S(2)}) %collective-permute-start.13) | collective-permute-done | bytes 196640 | tf_op jit(solution)/shard_map/ppermute | solution.py:375
  54.0 0.7 shard_map.56
  54.7 0.3 collective-permute-start.14
  55.0 0.9 %collective-permute-done.14 = f32[8,128]{1,0:T(8,128)S(1)} collective-permute-done((f32[8,128]{1,0:T(8,128)S(1)}, f32[8,128]{1,0:T(8,128)S(1)}, u32[]{:S(2)}, u32[]{:S(2)}) %collective-permute-start.14) | collective-permute-done | bytes 4128 | tf_op jit(solution)/shard_map/ppermute | solution.py:403
  56.0 0.1 collective-permute-start.15
  56.1 3.9 %collective-permute-done.15 = f32[8,128]{1,0:T(8,128)S(1)} collective-permute-done((f32[8,128]{1,0:T(8,128)S(1)}, f32[8,128]{1,0:T(8,128)S(1)}, u32[]{:S(2)}, u32[]{:S(2)}) %collective-permute-start.15) | collective-permute-done | bytes 4128 | tf_op jit(solution)/shard_map/ppermute | solution.py:273
  60.0 0.1 collective-permute-start.18
  60.1 1.4 %collective-permute-start.17 = (f32[8,128]{1,0:T(8,128)S(1)}, f32[8,128]{1,0:T(8,128)S(1)}, u32[]{:S(2)}, u32[]{:S(2)}) collective-permute-start(f32[8,128]{1,0:T(8,128)S(1)} %pad_maximum_fusion), channel_id=1, source_target_pairs={{0,3},{1,2},{2,1},{3,0},{4,7},{5,6},{6,5},{7,4},{8,11},{9,10},{10,... | collective-permute-start | bytes 12296 | tf_op jit(solution)/shard_map/ppermute | solution.py:273
  61.5 1.6 %collective-permute-start.16 = (f32[8,128]{1,0:T(8,128)S(1)}, f32[8,128]{1,0:T(8,128)S(1)}, u32[]{:S(2)}, u32[]{:S(2)}) collective-permute-start(f32[8,128]{1,0:T(8,128)S(1)} %pad_maximum_fusion), channel_id=1, source_target_pairs={{0,5},{1,4},{2,7},{3,6},{4,1},{5,0},{6,3},{7,2},{8,13},{9,12},{10,... | collective-permute-start | bytes 12296 | tf_op jit(solution)/shard_map/ppermute | solution.py:273
  63.1 0.9 %collective-permute-done.18 = f32[8,128]{1,0:T(8,128)S(1)} collective-permute-done((f32[8,128]{1,0:T(8,128)S(1)}, f32[8,128]{1,0:T(8,128)S(1)}, u32[]{:S(2)}, u32[]{:S(2)}) %collective-permute-start.18) | collective-permute-done | bytes 4128 | tf_op jit(solution)/shard_map/ppermute | solution.py:273
  64.0 0.0 collective-permute-done.17
  64.0 0.5 collective-permute-done.16
  64.5 0.7 %shard_map.57 = f32[4,128]{1,0:T(4,128)} custom-call(f32[32,128]{1,0:T(8,128)S(1)} %concatenate.32.refs_0_, s32[4,128]{1,0:T(4,128)S(1)} %bitcast.17, s32[4,128]{1,0:T(4,128)S(1)} %bitcast.15, s32[1,1]{1,0:T(1,128)} %bitcast.1.refs_2_.refs_3_), custom_call_target="tpu_custom_call" | custom-call | flops 4096 | bytes 22532 | tf_op jit(solution)/shard_map/pallas_call | solution.py:41
  (13 shorter events, 0.1 us)
Async XLA Ops:
  0.0 1.1 %copy-start.2 = (bf16[512,768]{1,0:T(8,128)(2,1)S(1)}, bf16[512,768]{1,0:T(8,128)(2,1)}, u32[]{:S(2)}) copy-start(bf16[512,768]{1,0:T(8,128)(2,1)} %refs_0_.1) | copy-start | bytes 2359300
  0.0 0.8 %copy-start.1 = (s32[512]{0:T(512)S(1)}, s32[512]{0:T(512)}, u32[]{:S(2)}) copy-start(s32[512]{0:T(512)} %param.6) | copy-start | bytes 6148
  1.7 29.0 %collective-permute-start.3 = (bf16[128,768]{1,0:T(8,128)(2,1)S(1)}, bf16[128,768]{1,0:T(8,128)(2,1)S(1)}, u32[]{:S(2)}, u32[]{:S(2)}) collective-permute-start(bf16[128,768]{1,0:T(8,128)(2,1)S(1)} %get-tuple-element.27), channel_id=1, source_target_pairs={{0,8},{2,10},{4,12},{6,14},{8,0},{10,2},{12,4},{14,6},{1,9},{3,11}... | collective-permute-start | bytes 589832 | tf_op jit(solution)/shard_map/ppermute | solution.py:269
  5.8 2.3 %copy-start = (s32[512]{0:T(512)S(1)}, s32[512]{0:T(512)}, u32[]{:S(2)}) copy-start(s32[512]{0:T(512)} %param.7) | copy-start | bytes 6148
  5.8 24.9 %collective-permute-start.6 = (bf16[128,768]{1,0:T(8,128)(2,1)S(1)}, bf16[128,768]{1,0:T(8,128)(2,1)S(1)}, u32[]{:S(2)}, u32[]{:S(2)}) collective-permute-start(bf16[128,768]{1,0:T(8,128)(2,1)S(1)} %get-tuple-element.30), channel_id=1, source_target_pairs={{0,14},{2,12},{4,10},{6,8},{8,6},{10,4},{12,2},{14,0},{1,15},{3,13... | collective-permute-start | bytes 589832 | tf_op jit(solution)/shard_map/ppermute | solution.py:269
  8.6 10.7 %collective-permute-start = (bf16[816,128]{1,0:T(8,128)(2,1)S(1)}, bf16[816,128]{1,0:T(8,128)(2,1)S(1)}, u32[]{:S(2)}, u32[]{:S(2)}) collective-permute-start(bf16[816,128]{1,0:T(8,128)(2,1)S(1)} %get-tuple-element.24), channel_id=1, source_target_pairs={{0,2},{2,0},{4,6},{6,4},{8,10},{10,8},{12,14},{14,12},{1,3},{3,1},... | collective-permute-start | bytes 626696 | tf_op jit(solution)/shard_map/ppermute | solution.py:269
  9.2 0.7 %copy-start.3 = (s32[1,256]{1,0:T(1,128)S(1)}, s32[1,256]{1,0:T(1,128)}, u32[]{:S(2)}) copy-start(s32[1,256]{1,0:T(1,128)} %param.8) | copy-start | bytes 3076
  19.8 9.9 %collective-permute-start.1 = (bf16[816,128]{1,0:T(8,128)(2,1)S(1)}, bf16[816,128]{1,0:T(8,128)(2,1)S(1)}, u32[]{:S(2)}, u32[]{:S(2)}) collective-permute-start(bf16[816,128]{1,0:T(8,128)(2,1)S(1)} %get-tuple-element.25), channel_id=1, source_target_pairs={{0,4},{2,6},{4,0},{6,2},{8,12},{10,14},{12,8},{14,10},{1,5},{3,7},... | collective-permute-start | bytes 626696 | tf_op jit(solution)/shard_map/ppermute | solution.py:269
  20.0 16.0 %collective-permute-start.4 = (bf16[128,768]{1,0:T(8,128)(2,1)S(1)}, bf16[128,768]{1,0:T(8,128)(2,1)S(1)}, u32[]{:S(2)}, u32[]{:S(2)}) collective-permute-start(bf16[128,768]{1,0:T(8,128)(2,1)S(1)} %get-tuple-element.28), channel_id=1, source_target_pairs={{0,10},{2,8},{4,14},{6,12},{8,2},{10,0},{12,6},{14,4},{1,11},{3,9}... | collective-permute-start | bytes 589832 | tf_op jit(solution)/shard_map/ppermute | solution.py:269
  30.1 9.8 %collective-permute-start.2 = (bf16[128,768]{1,0:T(8,128)(2,1)S(1)}, bf16[128,768]{1,0:T(8,128)(2,1)S(1)}, u32[]{:S(2)}, u32[]{:S(2)}) collective-permute-start(bf16[128,768]{1,0:T(8,128)(2,1)S(1)} %get-tuple-element.26), channel_id=1, source_target_pairs={{0,6},{2,4},{4,2},{6,0},{8,14},{10,12},{12,10},{14,8},{1,7},{3,5},... | collective-permute-start | bytes 589832 | tf_op jit(solution)/shard_map/ppermute | solution.py:269
  30.2 9.7 %collective-permute-start.5 = (bf16[776,128]{1,0:T(8,128)(2,1)S(1)}, bf16[776,128]{1,0:T(8,128)(2,1)S(1)}, u32[]{:S(2)}, u32[]{:S(2)}) collective-permute-start(bf16[776,128]{1,0:T(8,128)(2,1)S(1)} %get-tuple-element.29), channel_id=1, source_target_pairs={{0,12},{2,14},{4,8},{6,10},{8,4},{10,6},{12,0},{14,2},{1,13},{3,15... | collective-permute-start | bytes 595976 | tf_op jit(solution)/shard_map/ppermute | solution.py:269
  40.3 1.5 %collective-permute-start.12 = (bf16[128,768]{1,0:T(8,128)(2,1)S(1)}, bf16[128,768]{1,0:T(8,128)(2,1)S(1)}, u32[]{:S(2)}, u32[]{:S(2)}) collective-permute-start(bf16[128,768]{1,0:T(8,128)(2,1)S(1)} %shard_map.52.refs_9_), channel_id=1, source_target_pairs={{0,1},{1,0},{2,3},{3,2},{4,5},{5,4},{6,7},{7,6},{8,9},{9,8},{10,11... | collective-permute-start | bytes 589832 | tf_op jit(solution)/shard_map/ppermute | solution.py:374
  41.0 5.7 %collective-permute-start.7 = (bf16[64,768]{1,0:T(8,128)(2,1)S(1)}, bf16[64,768]{1,0:T(8,128)(2,1)S(1)}, u32[]{:S(2)}, u32[]{:S(2)}) collective-permute-start(bf16[64,768]{1,0:T(8,128)(2,1)S(1)} %get-tuple-element.31.refs_0_), channel_id=1, source_target_pairs={{0,1},{1,0},{2,3},{3,2},{4,5},{5,4},{6,7},{7,6},{8,9},{9,8},{10,11... | collective-permute-start | bytes 294920 | tf_op jit(solution)/shard_map/ppermute | solution.py:385
  41.9 12.1 %collective-permute-start.13 = (bf16[128,768]{1,0:T(8,128)(2,1)S(1)}, bf16[128,768]{1,0:T(8,128)(2,1)S(1)}, u32[]{:S(2)}, u32[]{:S(2)}) collective-permute-start(bf16[128,768]{1,0:T(8,128)(2,1)S(1)} %add.10), channel_id=1, source_target_pairs={{0,9},{1,8},{4,13},{5,12},{8,1},{9,0},{12,5},{13,4},{2,11},{3,10},... | collective-permute-start | bytes 589832 | tf_op jit(solution)/shard_map/ppermute | solution.py:375
  45.7 1.5 %collective-permute-start.8 = (bf16[112,768]{1,0:T(8,128)(2,1)S(1)}, bf16[112,768]{1,0:T(8,128)(2,1)S(1)}, u32[]{:S(2)}, u32[]{:S(2)}) collective-permute-start(bf16[112,768]{1,0:T(8,128)(2,1)S(1)} %get-tuple-element.33.refs_1_), channel_id=1, source_target_pairs={{0,1},{1,0},{2,3},{3,2},{4,5},{5,4},{6,7},{7,6},{8,9},{9,8},{10,11... | collective-permute-start | bytes 516104 | tf_op jit(solution)/shard_map/ppermute | solution.py:385
  46.1 1.4 %collective-permute-start.9 = (bf16[112,768]{1,0:T(8,128)(2,1)S(1)}, bf16[112,768]{1,0:T(8,128)(2,1)S(1)}, u32[]{:S(2)}, u32[]{:S(2)}) collective-permute-start(bf16[112,768]{1,0:T(8,128)(2,1)S(1)} %get-tuple-element.34.refs_2_), channel_id=1, source_target_pairs={{0,1},{1,0},{2,3},{3,2},{4,5},{5,4},{6,7},{7,6},{8,9},{9,8},{10,11... | collective-permute-start | bytes 516104 | tf_op jit(solution)/shard_map/ppermute | solution.py:385
  46.3 1.5 %collective-permute-start.10 = (bf16[112,768]{1,0:T(8,128)(2,1)S(1)}, bf16[112,768]{1,0:T(8,128)(2,1)S(1)}, u32[]{:S(2)}, u32[]{:S(2)}) collective-permute-start(bf16[112,768]{1,0:T(8,128)(2,1)S(1)} %get-tuple-element.35.refs_3_), channel_id=1, source_target_pairs={{0,1},{1,0},{2,3},{3,2},{4,5},{5,4},{6,7},{7,6},{8,9},{9,8},{10,11... | collective-permute-start | bytes 516104 | tf_op jit(solution)/shard_map/ppermute | solution.py:385
  46.6 1.4 %collective-permute-start.11 = (bf16[112,768]{1,0:T(8,128)(2,1)S(1)}, bf16[112,768]{1,0:T(8,128)(2,1)S(1)}, u32[]{:S(2)}, u32[]{:S(2)}) collective-permute-start(bf16[112,768]{1,0:T(8,128)(2,1)S(1)} %get-tuple-element.36.refs_4_), channel_id=1, source_target_pairs={{0,1},{1,0},{2,3},{3,2},{4,5},{5,4},{6,7},{7,6},{8,9},{9,8},{10,11... | collective-permute-start | bytes 516104 | tf_op jit(solution)/shard_map/ppermute | solution.py:385
  54.7 1.2 %collective-permute-start.14 = (f32[8,128]{1,0:T(8,128)S(1)}, f32[8,128]{1,0:T(8,128)S(1)}, u32[]{:S(2)}, u32[]{:S(2)}) collective-permute-start(f32[8,128]{1,0:T(8,128)S(1)} %pad_maximum_fusion.2), channel_id=1, source_target_pairs={{0,1},{1,0},{2,3},{3,2},{4,5},{5,4},{6,7},{7,6},{8,9},{9,8},{10,11... | collective-permute-start | bytes 12296 | tf_op jit(solution)/shard_map/ppermute | solution.py:403
  56.0 4.0 %collective-permute-start.15 = (f32[8,128]{1,0:T(8,128)S(1)}, f32[8,128]{1,0:T(8,128)S(1)}, u32[]{:S(2)}, u32[]{:S(2)}) collective-permute-start(f32[8,128]{1,0:T(8,128)S(1)} %pad_maximum_fusion.1), channel_id=1, source_target_pairs={{0,9},{1,8},{2,11},{3,10},{4,13},{5,12},{6,15},{7,14},{8,1},{9,0},... | collective-permute-start | bytes 12296 | tf_op jit(solution)/shard_map/ppermute | solution.py:273
  60.0 4.0 %collective-permute-start.18 = (f32[8,128]{1,0:T(8,128)S(1)}, f32[8,128]{1,0:T(8,128)S(1)}, u32[]{:S(2)}, u32[]{:S(2)}) collective-permute-start(f32[8,128]{1,0:T(8,128)S(1)} %pad_maximum_fusion), channel_id=1, source_target_pairs={{0,7},{1,6},{2,5},{3,4},{4,3},{5,2},{6,1},{7,0},{8,15},{9,14},{10,... | collective-permute-start | bytes 12296 | tf_op jit(solution)/shard_map/ppermute | solution.py:273
  60.1 3.9 %collective-permute-start.17 = (f32[8,128]{1,0:T(8,128)S(1)}, f32[8,128]{1,0:T(8,128)S(1)}, u32[]{:S(2)}, u32[]{:S(2)}) collective-permute-start(f32[8,128]{1,0:T(8,128)S(1)} %pad_maximum_fusion), channel_id=1, source_target_pairs={{0,3},{1,2},{2,1},{3,0},{4,7},{5,6},{6,5},{7,4},{8,11},{9,10},{10,... | collective-permute-start | bytes 12296 | tf_op jit(solution)/shard_map/ppermute | solution.py:273
  61.5 3.0 %collective-permute-start.16 = (f32[8,128]{1,0:T(8,128)S(1)}, f32[8,128]{1,0:T(8,128)S(1)}, u32[]{:S(2)}, u32[]{:S(2)}) collective-permute-start(f32[8,128]{1,0:T(8,128)S(1)} %pad_maximum_fusion), channel_id=1, source_target_pairs={{0,5},{1,4},{2,7},{3,6},{4,1},{5,0},{6,3},{7,2},{8,13},{9,12},{10,... | collective-permute-start | bytes 12296 | tf_op jit(solution)/shard_map/ppermute | solution.py:273
